TPU v7x, 128 devices: a whole 4x4x4 slice. The times are simulated.
128 devices in a mesh: batch: 16 (over z_lo, x, core), space: 8 (over y, z_hi).
Axes of the slice: x: 4, y: 4, z: 4 (z_hi: 2, z_lo: 2; z = z_hi * 2 + z_lo), core: 2. Of those that a mesh axis runs over, the one named last changes fastest.
Arguments:
- images: bfloat16 [16, 64, 256, 1024], P('batch', 'space'), may hold values from -6 to 6
- heights: int32 [16], P('batch'), may hold values from 32 to 64, as said below
- widths: int32 [16], P('batch'), may hold values from 512 to 1024, as said below
- conv_reduce: bfloat16 [2, 256, 64], replicated, may hold values from -0.375 to 0.375
- conv_spatial: bfloat16 [2, 3, 3, 64, 64], replicated, may hold values from -0.25 to 0.25
- conv_expand: bfloat16 [2, 64, 256], replicated, may hold values from -0.75 to 0.75
- scale_mid: float32 [2, 2, 64], replicated, may hold values from 0.25 to 1.75
- shift_mid: float32 [2, 2, 64], replicated, may hold values from -3 to 3
- scale_out: float32 [2, 256], replicated, may hold values from 0.25 to 1.75
- shift_out: float32 [2, 256], replicated, may hold values from -3 to 3
- cotangent: bfloat16 [16, 64, 256, 1024], P('batch', 'space'), may hold values from -6 to 6
Outputs:
- grad_images: bfloat16 [16, 64, 256, 1024], P('batch', 'space')
- grad_reduce: float32 [2, 256, 64], replicated
- grad_spatial: float32 [2, 3, 3, 64, 64], replicated
- grad_expand: float32 [2, 64, 256], replicated
Inputs may be any that keep to these rules, and one draw needn't show every extreme that they name: `heights`: some image fills all 64 rows. `widths`: some image fills all 1024 columns.
All inputs are finite; a program needn't handle non-finite values.
Results may differ from a plain program's by a relative error of at most 0.015.
Values may be sent and summed in bfloat16 or wider, within the bound.
No kernel may reach another device: no remote copies, remote signals or barrier semaphores. Data moves between devices by JAX's collectives and lax.ppermute only.
A program may use at most 128 MiB of HBM per device.

v0:
```python
import functools
import math

import jax
import jax.numpy as jnp
from jax import lax
from jax.experimental import pallas as pl
from jax.experimental.pallas import tpu as pltpu
from jax.sharding import PartitionSpec as P

F32 = jnp.float32
BF16 = jnp.bfloat16
VMEM_LIMIT = 12 * 1024 * 1024
CHUNK = 256
VMEM = pl.BlockSpec(memory_space=pltpu.VMEM)
SMEM = pl.BlockSpec(memory_space=pltpu.SMEM)
HBM = pl.BlockSpec(memory_space=pltpu.HBM)


def mm(a, b):
    return lax.dot_general(a, b, (((1,), (0,)), ((), ())), preferred_element_type=F32)


def mm_nt(a, b):
    return lax.dot_general(a, b, (((1,), (1,)), ((), ())), preferred_element_type=F32)


def gate(h):
    t = jnp.tanh(h)
    p = 1 + t
    y = h * p
    return y, p + y * (1 - t)


def wide(bias, cols):
    return jnp.concatenate([bias[...]] * (cols // bias.shape[-1]), axis=1)


def row_mask(heights, widths, row, rows, cols):
    where = lax.axis_index("space") * rows + row
    limit = jnp.where(where < heights[0], widths[0], 0)
    ids = lax.broadcasted_iota(jnp.int32, (1, cols), 1)
    return jnp.where(ids < limit, 1.0, 0.0).astype(BF16)


def before(v):
    ids = lax.broadcasted_iota(jnp.int32, (1, v.shape[-1]), 1)
    return pltpu.roll(v, 1, 1) * jnp.where(ids > 0, 1.0, 0.0).astype(v.dtype)


def after(v):
    cols = v.shape[-1]
    ids = lax.broadcasted_iota(jnp.int32, (1, cols), 1)
    return pltpu.roll(v, cols - 1, 1) * jnp.where(ids < cols - 1, 1.0, 0.0).astype(v.dtype)


def edge_taps(strip, halo_above, halo_below, last):
    me = lax.axis_index("space")
    rows = strip.shape[0]
    if last:
        have = jnp.where(me < lax.axis_size("space") - 1, 1.0, 0.0).astype(BF16)
        parts = [strip[rows - 2], strip[rows - 1], halo_below[...] * have]
    else:
        have = jnp.where(me > 0, 1.0, 0.0).astype(BF16)
        parts = [halo_above[...] * have, strip[0], strip[1]]
    return jnp.concatenate(parts, axis=0)


def inner_taps(strip, row, count):
    part = strip[pl.ds(row - 1, count)]
    return part.reshape(part.shape[0] * part.shape[1], part.shape[2])


def join(out, flip):
    mid = out.shape[0] // 3
    first, centre, last = out[:mid], out[mid : 2 * mid], out[2 * mid :]
    if flip:
        first, last = last, first
    return before(first) + centre + after(last)


def spread(v):
    return jnp.concatenate([after(v), v, before(v)], axis=0)


def chunks(cols):
    return [slice(c, c + CHUNK) for c in range(0, cols, CHUNK)]


def reduce_part(x, w_reduce, b_first, mask):
    h = (mm(w_reduce[...], x) + wide(b_first, CHUNK)).astype(BF16)
    y, d = gate(h)
    return y * mask, d * mask


def conv_rows(edges, rows, strip, halos, single, double, flip, work):
    if edges:
        for last in (False, True):
            taps = edge_taps(strip, *halos, last)
            work(rows - 1 if last else 0, int(last), join(mm(single[...], taps), flip))
        return

    def pair(i, carry):
        row = 1 + 2 * i
        out = mm(double[...], inner_taps(strip, row, 4))
        half = out.shape[0] // 2
        work(row, row - 1, join(out[:half], flip))
        work(row + 1, row, join(out[half:], flip))
        return carry

    lax.fori_loop(0, (rows - 2) // 2, pair, 0)


def taps_of(edges, strip, halos, row):
    return edge_taps(strip, *halos, row > 0) if edges else inner_taps(strip, row, 3)


def start_sums(have, sums):
    for value, out in zip(have or [None] * len(sums), sums):
        out[...] = jnp.zeros_like(out) if value is None else value[...]


def gather_rows(full, inner, top, bottom):
    rows = full.shape[0]
    full[0] = top[...]
    full[rows - 1] = bottom[...]
    for r in range(1, rows - 1):
        full[r] = inner[r - 1]


def forward_rows(edges, hw, strip, halos, x, kf, kf2, b_second, we, b_out, w_reduce, b_first,
                 second, slope2, slope3, x1, slope1, put_first):
    rows, cols = x.shape[0], x.shape[-1]

    def work(row, slot, pre):
        mask = row_mask(*hw, row, rows, cols)
        for cut in chunks(cols):
            h = (pre[:, cut] + wide(b_second, CHUNK)).astype(BF16)
            y, d = gate(h)
            second[slot, :, cut] = y
            slope2[slot, :, cut] = d
            h = (mm(we[...], y) + wide(b_out, CHUNK)).astype(BF16) + x[row, :, cut] * 0.5
            y, d = gate(h)
            slope3[slot, :, cut] = d
            x1[slot, :, cut] = y
            first, slope1[slot, :, cut] = reduce_part(y, w_reduce, b_first, mask[:, cut])
            put_first(row, slot, cut, first)

    conv_rows(edges, rows, strip, halos, kf, kf2, False, work)


def forward_inner(heights, widths, x, top, bottom, kf, kf2, b2, we, b3, wr, b1,
                  first0, slope1_0, second, slope2, slope3, x1, slope1_1, first1):
    rows, cols = x.shape[0], x.shape[-1]
    first0[0] = top[...]
    first0[rows - 1] = bottom[...]

    @pl.loop(1, rows - 1)
    def _(row):
        mask = row_mask(heights, widths, row, rows, cols)
        for cut in chunks(cols):
            first0[row, :, cut], slope1_0[row - 1, :, cut] = reduce_part(
                x[row, :, cut], wr.at[0], b1.at[0], mask[:, cut])

    def put_first(row, slot, cut, value):
        first1[slot, :, cut] = value

    forward_rows(False, (heights, widths), first0, None, x, kf.at[0], kf2.at[0], b2.at[0], we.at[0], b3.at[0],
                 wr.at[1], b1.at[1], second, slope2, slope3, x1, slope1_1, put_first)


def forward_edge(heights, widths, x, first0, above, below, first1_inner, kf, kf2, b2, we, b3, wr, b1,
                 second, slope2, slope3, x1, slope1_1, first1, top, bottom):
    def put_first(row, slot, cut, value):
        (bottom if slot else top)[:, cut] = value

    forward_rows(True, (heights, widths), first0, (above, below), x, kf.at[0], kf2.at[0], b2.at[0], we.at[0],
                 b3.at[0], wr.at[1], b1.at[1], second, slope2, slope3, x1, slope1_1, put_first)
    gather_rows(first1, first1_inner, top, bottom)


def turn_rows(edges, hw, first1, halos, x1, cot, kf, kf2, b2, we, b3, we_back, gsum, dexp, put_mid2):
    rows, cols = cot.shape[0], cot.shape[-1]

    def work(row, slot, pre):
        mask = row_mask(*hw, row, rows, cols)
        for cut in chunks(cols):
            h = (pre[:, cut] + wide(b2.at[1], CHUNK)).astype(BF16)
            y2, d2 = gate(h)
            h = (mm(we[1], y2) + wide(b3.at[1], CHUNK)).astype(BF16) + x1[slot, :, cut] * 0.5
            _, d3 = gate(h)
            g = cot[row, :, cut] * mask[:, cut] * d3
            gsum[slot, :, cut] = g
            put_mid2(row, slot, cut, mm(we_back[1], g).astype(BF16) * d2)
            dexp[...] += mm_nt(y2, g)

    conv_rows(edges, rows, first1, halos, kf.at[1], kf2.at[1], False, work)


def turn_inner(heights, widths, first1, x1, cot, kf, kf2, b2, we, b3, we_back, gsum, gmid2, dexp):
    start_sums(None, [dexp])

    def put_mid2(row, slot, cut, value):
        gmid2[slot, :, cut] = value

    turn_rows(False, (heights, widths), first1, None, x1, cot, kf, kf2, b2, we, b3, we_back, gsum, dexp, put_mid2)


def turn_edge(heights, widths, first1, above, below, x1, cot, kf, kf2, b2, we, b3, we_back, gmid2_inner, dexp_inner,
              gsum, gmid2, dexp, top, bottom):
    start_sums([dexp_inner], [dexp])

    def put_mid2(row, slot, cut, value):
        (bottom if slot else top)[:, cut] = value

    turn_rows(True, (heights, widths), first1, (above, below), x1, cot, kf, kf2, b2, we, b3, we_back, gsum, dexp, put_mid2)
    gather_rows(gmid2, gmid2_inner, top, bottom)


def backward_rows(edges, hw, gmid2, g_halos, first1, f_halos, slope1, x1, gsum1, slope3, slope2, second,
                  kb, kb2, wr_back, we_back, gsum0, dred, dspat, dexp, put_mid2):
    rows, cols = gmid2.shape[0], gmid2.shape[-1]

    def work(row, slot, back):
        mask = row_mask(*hw, row, rows, cols)
        for cut in chunks(cols):
            g1 = back[:, cut].astype(BF16) * slope1[slot, :, cut]
            dred[...] += mm_nt(g1, x1[slot, :, cut])
            up = (mm(wr_back[1], g1) + gsum1[slot, :, cut].astype(F32)).astype(BF16)
            g = up * slope3[slot, :, cut] * mask[:, cut]
            gsum0[slot, :, cut] = g
            put_mid2(row, slot, cut, mm(we_back[0], g).astype(BF16) * slope2[slot, :, cut])
            dexp[...] += mm_nt(second[slot, :, cut], g)
        dspat[...] += mm_nt(taps_of(edges, first1, f_halos, row), spread(gmid2[row]))

    conv_rows(edges, rows, gmid2, g_halos, kb.at[1], kb2.at[1], True, work)


def backward_inner(heights, widths, gmid2, first1, slope1, x1, gsum1, slope3, slope2, second, kb, kb2, wr_back, we_back,
                   gsum0, gmid2_0, dred, dspat, dexp):
    start_sums(None, [dred, dspat, dexp])

    def put_mid2(row, slot, cut, value):
        gmid2_0[slot, :, cut] = value

    backward_rows(False, (heights, widths), gmid2, None, first1, None, slope1, x1, gsum1, slope3, slope2, second,
                  kb, kb2, wr_back, we_back, gsum0, dred, dspat, dexp, put_mid2)


def backward_edge(heights, widths, gmid2, above, below, first1, f_above, f_below, slope1, x1, gsum1, slope3, slope2, second,
                  kb, kb2, wr_back, we_back, gmid2_inner, dred_inner, dspat_inner, dexp_inner,
                  gsum0, gmid2_0, dred, dspat, dexp, top, bottom):
    start_sums([dred_inner, dspat_inner, dexp_inner], [dred, dspat, dexp])

    def put_mid2(row, slot, cut, value):
        (bottom if slot else top)[:, cut] = value

    backward_rows(True, (heights, widths), gmid2, (above, below), first1, (f_above, f_below), slope1, x1, gsum1, slope3,
                  slope2, second, kb, kb2, wr_back, we_back, gsum0, dred, dspat, dexp, put_mid2)
    gather_rows(gmid2_0, gmid2_inner, top, bottom)


def last_rows(edges, gmid2, g_halos, first0, f_halos, slope1, x, kb, kb2, gmid1, dred, dspat):
    def work(row, slot, back):
        g1 = back.astype(BF16) * slope1[slot]
        gmid1[slot] = g1
        dred[...] += mm_nt(g1, x[row])
        dspat[...] += mm_nt(taps_of(edges, first0, f_halos, row), spread(gmid2[row]))

    conv_rows(edges, x.shape[0], gmid2, g_halos, kb.at[0], kb2.at[0], True, work)


def last_inner(gmid2, first0, slope1, x, kb, kb2, gmid1, dred, dspat):
    start_sums(None, [dred, dspat])
    last_rows(False, gmid2, None, first0, None, slope1, x, kb, kb2, gmid1, dred, dspat)


def last_edge(gmid2, above, below, first0, f_above, f_below, slope1, x, kb, kb2, dred_inner, dspat_inner,
              dred1, dexp0, dexp1, dspat1, gmid1, terms, dred, dspat):
    start_sums([dred_inner, dspat_inner], [dred, dspat])
    last_rows(True, gmid2, (above, below), first0, (f_above, f_below), slope1, x, kb, kb2, gmid1, dred, dspat)
    at = 0
    for value in (dred, dred1, dexp0, dexp1, dspat, dspat1):
        tall, across = value.shape
        terms[at : at + tall, :across] = value[...].astype(BF16)
        if across < terms.shape[1]:
            terms[at : at + tall, across:] = jnp.zeros((tall, terms.shape[1] - across), BF16)
        at += tall


def grad_rows(gmid1_inner, gmid1_edge, gsum_inner, gsum_edge, wr_back, out, held, sems):
    rows, cols = held.shape[0], held.shape[-1]

    def work(row, slot, gmid1, gsum):
        for cut in chunks(cols):
            acc = mm(wr_back[0], gmid1[slot, :, cut]) + gsum[slot, :, cut].astype(F32) * 0.25
            held[row, :, cut] = acc.astype(BF16)
        pltpu.make_async_copy(held.at[row], out.at[row], sems.at[row]).start()

    @pl.loop(1, rows - 1)
    def _(row):
        work(row, row - 1, gmid1_inner, gsum_inner)

    work(0, 0, gmid1_edge, gsum_edge)
    work(rows - 1, 1, gmid1_edge, gsum_edge)
    for r in range(rows):
        pltpu.make_async_copy(held.at[r], out.at[r], sems.at[r]).wait()


def finish(factor, terms, scale_out, g_reduce, g_spatial, g_expand):
    mid = g_reduce.shape[1]
    for k in range(2):
        g_reduce[k] = terms[k * mid : (k + 1) * mid].astype(F32) * factor
        scale = scale_out[k : k + 1, :] * (factor * 0.5 ** (2 - k))
        g_expand[k] = terms[(2 + k) * mid : (3 + k) * mid].astype(F32) * scale
        base = (4 + 3 * k) * mid
        for a in range(3):
            for b in range(3):
                part = terms[base + a * mid : base + (a + 1) * mid, b * mid : (b + 1) * mid]
                g_spatial[k, a, b] = part.astype(F32) * factor


def lanes(vector, count):
    return jnp.broadcast_to(vector, (count, vector.shape[-1])).T


def start(heights, widths, images, red_h, spa_h, exp_h, sm_h, sh_h, so_h, sho_h,
          wr, kf, kf2, we, we_back, kb, kb2, wr_back, b1, b2, b3, x, slope1, top, bottom,
          red, spa, exp, scale_mid, shift_mid, scale_out, shift_out, sems):
    rows, cols = x.shape[0], x.shape[-1]
    params = list(zip((red_h, spa_h, exp_h, sm_h, sh_h, so_h, sho_h),
                      (red, spa, exp, scale_mid, shift_mid, scale_out, shift_out)))
    small = [pltpu.make_async_copy(s, d, sems.at[rows + n]) for n, (s, d) in enumerate(params)]
    strips = [pltpu.make_async_copy(images.at[r], x.at[r], sems.at[r]) for r in range(rows)]
    for copy in small:
        copy.start()
    for r in (0, rows - 1, *range(1, rows - 1)):
        strips[r].start()
    for copy in small:
        copy.wait()
    mid = red.shape[1]
    kf2[...] = jnp.zeros_like(kf2)
    kb2[...] = jnp.zeros_like(kb2)
    for k in range(2):
        twice = 2.0 ** (2 - k)
        s1, s2 = scale_mid[k, 0:1, :], scale_mid[k, 1:2, :]
        so = scale_out[k : k + 1, :]
        r, e = red[k].astype(F32), exp[k].astype(F32)
        chans = r.shape[-1]
        wr[k] = (r * (0.5 * lanes(s1, chans))).astype(BF16)
        wr_back[k] = (r * (1.0 if k == 0 else twice)).T.astype(BF16)
        we[k] = (e * (0.5 * so)).T.astype(BF16)
        we_back[k] = (e * (so * (0.5 / twice)) * lanes(s2, chans)).astype(BF16)
        half = 0.5 * lanes(s1, mid)
        for a in range(3):
            for b in range(3):
                part = spa[k, a, b].astype(F32)
                ahead = (part * (0.5 * s2)).T.astype(BF16)
                back = (part * half).astype(BF16)
                for out, out2, value, at in ((kf, kf2, ahead, a), (kb, kb2, back, 2 - a)):
                    out[k, b * mid : (b + 1) * mid, at * mid : (at + 1) * mid] = value
                    for j in range(2):
                        out2[k, (3 * j + b) * mid : (3 * j + b + 1) * mid, (at + j) * mid : (at + j + 1) * mid] = value
        b1[k] = 0.5 * lanes(shift_mid[k, 0:1, :], b1.shape[-1])
        b2[k] = 0.5 * lanes(shift_mid[k, 1:2, :], b2.shape[-1])
        b3[k] = 0.5 * lanes(shift_out[k : k + 1, :], b3.shape[-1])
    for slot, (row, edge) in enumerate(((0, top), (rows - 1, bottom))):
        strips[row].wait()
        mask = row_mask(heights, widths, row, rows, cols)
        for cut in chunks(cols):
            edge[:, cut], slope1[slot, :, cut] = reduce_part(x[row, :, cut], wr.at[0], b1.at[0], mask[:, cut])
    for r in range(1, rows - 1):
        strips[r].wait()


def call(kernel, outs, args, name, specs=None, out_specs=None, scratch=(), limit=VMEM_LIMIT):
    return pl.pallas_call(
        kernel,
        in_specs=specs or [VMEM] * len(args),
        out_specs=out_specs or [VMEM] * len(outs),
        out_shape=[jax.ShapeDtypeStruct(s, d) for s, d in outs],
        scratch_shapes=list(scratch),
        compiler_params=pltpu.CompilerParams(vmem_limit_bytes=limit),
        name=name,
    )(*args)


def placed_call(kernel, outs, args, name):
    return call(kernel, outs, args, name, [SMEM] * 2 + [VMEM] * (len(args) - 2))


def exchange(top, bottom):
    count = lax.axis_size("space")
    above = lax.ppermute(bottom, "space", [(i, (i + 1) % count) for i in range(count)])
    below = lax.ppermute(top, "space", [((i + 1) % count, i) for i in range(count)])
    return above, below


def all_sum(terms):
    n = lax.axis_size("batch")
    tall, across = terms.shape
    shares = lax.all_to_all(terms.reshape(n, tall // n, across), "batch", 0, 0, tiled=True)
    share = shares.astype(F32).sum(0)
    count = lax.axis_size("space")
    for bit in (2, 6, 1):
        share = share + lax.ppermute(share.astype(BF16), "space", [(i, i ^ bit) for i in range(count)]).astype(F32)
    spread_out = jnp.broadcast_to(share.astype(BF16)[None], (n,) + share.shape)
    return lax.all_to_all(spread_out, "batch", 0, 0, tiled=True).reshape(terms.shape)


def body(images, heights, widths, conv_reduce, conv_spatial, conv_expand, scale_mid, shift_mid,
         scale_out, shift_out, cotangent):
    _, rows, chans, cols = images.shape
    mid = conv_reduce.shape[-1]
    cot = cotangent[0]
    wide_w, tall_w = ((mid, chans), BF16), ((chans, mid), BF16)
    single, double = ((3 * mid, 3 * mid), BF16), ((6 * mid, 4 * mid), BF16)
    bias = ((mid, 128), F32)
    made = [wide_w, single, double, tall_w, wide_w, single, double, tall_w, bias, bias, ((chans, 128), F32)]
    params = [conv_reduce.swapaxes(1, 2), conv_spatial, conv_expand, scale_mid, shift_mid, scale_out, shift_out]

    def small(count):
        return (count, mid, cols), BF16

    def large(count):
        return (count, chans, cols), BF16

    inner, edge = rows - 2, 2
    row = ((mid, cols), BF16)
    acc_c = ((mid, chans), F32)
    acc_s = ((3 * mid, 3 * mid), F32)

    wr, kf, kf2, we, we_back, kb, kb2, wr_back, b1, b2, b3, x0, slope1_0e, top, bottom = call(
        start, [((2,) + s, d) for s, d in made] + [large(rows), small(edge), row, row],
        [heights, widths] + [pltpu.with_memory_space_constraint(a, pltpu.HBM) for a in [images[0]] + params], "start", [SMEM] * 2 + [HBM] * 8,
        scratch=[pltpu.VMEM(p.shape, p.dtype) for p in params] + [pltpu.SemaphoreType.DMA((rows + len(params),))])
    f0a, f0b = exchange(top, bottom)
    hw = [heights, widths]
    fwd = [kf, kf2, b2, we, b3, wr, b1]
    first0, slope1_0i, second0i, slope2_0i, slope3_0i, x1i, slope1_1i, first1i = placed_call(
        forward_inner, [small(rows)] + [small(inner)] * 3 + [large(inner)] * 2 + [small(inner)] * 2,
        hw + [x0, top, bottom] + fwd, "forward_inner")
    second0e, slope2_0e, slope3_0e, x1e, slope1_1e, first1, top, bottom = placed_call(
        forward_edge, [small(edge)] * 2 + [large(edge)] * 2 + [small(edge), small(rows), row, row],
        hw + [x0, first0, f0a, f0b, first1i] + fwd, "forward_edge")
    f1a, f1b = exchange(top, bottom)
    turn = [kf, kf2, b2, we, b3, we_back]
    gsum1i, gmid2_1i, dexp1 = placed_call(
        turn_inner, [large(inner), small(inner), acc_c], hw + [first1, x1i, cot] + turn, "turn_inner")
    gsum1e, gmid2_1, dexp1, top, bottom = placed_call(
        turn_edge, [large(edge), small(rows), acc_c, row, row],
        hw + [first1, f1a, f1b, x1e, cot] + turn + [gmid2_1i, dexp1], "turn_edge")
    g1a, g1b = exchange(top, bottom)
    back = [kb, kb2, wr_back, we_back]
    sums = [acc_c, acc_s, acc_c]
    gsum0i, gmid2_0i, *partial = placed_call(
        backward_inner, [large(inner), small(inner)] + sums,
        hw + [gmid2_1, first1, slope1_1i, x1i, gsum1i, slope3_0i, slope2_0i, second0i] + back, "backward_inner")
    gsum0e, gmid2_0, dred1, dspat1, dexp0, top, bottom = placed_call(
        backward_edge, [large(edge), small(rows)] + sums + [row, row],
        hw + [gmid2_1, g1a, g1b, first1, f1a, f1b, slope1_1e, x1e, gsum1e, slope3_0e, slope2_0e, second0e] + back
        + [gmid2_0i] + partial, "backward_edge")
    g0a, g0b = exchange(top, bottom)
    gmid1_0i, dred0, dspat0 = call(
        last_inner, [small(inner), acc_c, acc_s], [gmid2_0, first0, slope1_0i, x0, kb, kb2], "last_inner")
    gmid1_0e, terms = call(
        last_edge, [small(edge), ((4 * mid + 6 * mid, chans), BF16)],
        [gmid2_0, g0a, g0b, first0, f0a, f0b, slope1_0e, x0, kb, kb2, dred0, dspat0, dred1, dexp0, dexp1, dspat1],
        "last_edge", scratch=[pltpu.VMEM(*acc_c), pltpu.VMEM(*acc_s)])
    (grad,) = call(
        grad_rows, [large(rows)], [gmid1_0i, gmid1_0e, gsum0i, gsum0e, wr_back], "grad_images", out_specs=[HBM],
        scratch=[pltpu.VMEM(*large(rows)), pltpu.SemaphoreType.DMA((rows,))])
    summed = all_sum(terms)
    factor = 1.0 / math.sqrt(lax.axis_size("batch") * rows * lax.axis_size("space") * cols)
    g_reduce, g_spatial, g_expand = call(
        functools.partial(finish, factor),
        [((2, mid, chans), F32), (conv_spatial.shape, F32), ((2, mid, chans), F32)], [summed, scale_out], "finish")
    return grad[None], g_reduce.swapaxes(1, 2), g_spatial, g_expand


def solution(mesh):
    strips = P("batch", "space", None, None)
    placed = (strips, P("batch"), P("batch")) + (P(),) * 7 + (strips,)
    return jax.shard_map(
        body, mesh=mesh, in_specs=placed, out_specs=(strips, P(), P(), P()), check_vma=False)
```

profile of v0, /device:TPU:0, one launch (start us, length us, event | category | flops | bytes accessed | tf_op | source)
XLA Modules:
  0.0 104.5 jit_solution(5678015453494907478)
XLA Ops:
  1.9 2.5 %start.1 = (bf16[2,64,256]{2,1,0:T(8,128)(2,1)S(1)}, bf16[2,192,192]{2,1,0:T(8,128)(2,1)S(1)}, bf16[2,384,256]{2,1,0:T(8,128)(2,1)S(1)}, bf16[2,256,64]{2,1,0:T(...) custom-call(s32[1]{0:T(128)S(6)} %copy.15.heights, ...), custom_call_target="tpu_custom_call" | custom-call | tf_op jit(solution)/shard_map/start/pallas_call | solution.py:377
  4.5 6.5 %collective-permute-start.1 = (bf16[64,1024]{1,0:T(8,128)(2,1)S(1)}, bf16[64,1024]{1,0:T(8,128)(2,1)S(1)}, u32[]{:S(2)}, u32[]{:S(2)}) collective-permute-start(bf16[64,1024]{1,0:T(8,128)(2,1)S(1)} %get-tuple-element.64.top), channel_id=1, source_target_pairs={{1,0},{2,1},{3,2},{4,3},{5,4},{6,5},{7,6},{0,7},{9,8},{10,9},{11,1... | collective-permute-start | bytes 393224 | tf_op jit(solution)/shard_map/ppermute | solution.py:395
  10.9 8.1 %forward_inner.1 = (bf16[8,64,1024]{2,1,0:T(8,128)(2,1)S(1)}, bf16[6,64,1024]{2,1,0:T(8,128)(2,1)S(1)}, bf16[6,64,1024]{2,1,0:T(8,128)(2,1)S(1)}, bf16[6,64,1024...) custom-call(s32[1]{0:T(128)S(6)} %copy.15.heights, ...), custom_call_target="tpu_custom_call" | custom-call | tf_op jit(solution)/shard_map/forward_inner/pallas_call | solution.py:377
  19.5 2.4 %forward_edge.1 = (bf16[2,64,1024]{2,1,0:T(8,128)(2,1)S(1)}, bf16[2,64,1024]{2,1,0:T(8,128)(2,1)S(1)}, bf16[2,256,1024]{2,1,0:T(8,128)(2,1)S(1)}, bf16[2,256,102...) custom-call(s32[1]{0:T(128)S(6)} %copy.15.heights, ...), custom_call_target="tpu_custom_call" | custom-call | tf_op jit(solution)/shard_map/forward_edge/pallas_call | solution.py:377
  21.9 1.6 %collective-permute-start.2 = (bf16[64,1024]{1,0:T(8,128)(2,1)S(1)}, bf16[64,1024]{1,0:T(8,128)(2,1)S(1)}, u32[]{:S(2)}, u32[]{:S(2)}) collective-permute-start(bf16[64,1024]{1,0:T(8,128)(2,1)S(1)} %get-tuple-element.76), channel_id=1, source_target_pairs={{0,1},{1,2},{2,3},{3,4},{4,5},{5,6},{6,7},{7,0},{8,9},{9,10},{10,1... | collective-permute-start | bytes 393224 | tf_op jit(solution)/shard_map/ppermute | solution.py:394
  23.5 4.1 %collective-permute-start.3 = (bf16[64,1024]{1,0:T(8,128)(2,1)S(1)}, bf16[64,1024]{1,0:T(8,128)(2,1)S(1)}, u32[]{:S(2)}, u32[]{:S(2)}) collective-permute-start(bf16[64,1024]{1,0:T(8,128)(2,1)S(1)} %get-tuple-element.77), channel_id=1, source_target_pairs={{1,0},{2,1},{3,2},{4,3},{5,4},{6,5},{7,6},{0,7},{9,8},{10,9},{11,1... | collective-permute-start | bytes 393224 | tf_op jit(solution)/shard_map/ppermute | solution.py:395
  27.7 6.4 %turn_inner.1 = (bf16[6,256,1024]{2,1,0:T(8,128)(2,1)S(1)}, bf16[6,64,1024]{2,1,0:T(8,128)(2,1)S(1)}, f32[64,256]{1,0:T(8,128)S(1)}) custom-call(s32[1]{0:T(128)S(6)} %copy.15.heights, s32[1]{0:T(128)S(6)} %copy.16.widths, bf16[8,64,1024]{2,1,0:T(8,128)(2,1)S(1)} %get-tuple-element.75.first1, bf16[6,256,1024]{2,1,0:T(8,128)(2,1)S(1)} %get-tuple-element.80.x1, ...), custom_call_target="tpu_custom_call" | custom-call | tf_op jit(solution)/shard_map/turn_inner/pallas_call | solution.py:377
  34.1 2.5 %turn_edge.1 = (bf16[2,256,1024]{2,1,0:T(8,128)(2,1)S(1)}, bf16[8,64,1024]{2,1,0:T(8,128)(2,1)S(1)}, f32[64,256]{1,0:T(8,128)S(1)}, bf16[64,1024]{1,0:T(8,128)(2,1)S(1)}, bf16[64,1024]{1,0:T(8,128)(2,1)S(1)}) custom-call(s32[1]{0:T(128)S(6)} %copy.15.heights, s32[1]{0:T(128)S(6)} %copy.16.widths, bf16[8,64,1024]{2,1,0:T(8,128)(2,1)S(1)} %get-tuple-element.75.first1, ...), custom_call_target="tpu_custom_call" | custom-call | tf_op jit(solution)/shard_map/turn_edge/pallas_call | solution.py:377
  36.7 5.6 %collective-permute-start.5 = (bf16[64,1024]{1,0:T(8,128)(2,1)S(1)}, bf16[64,1024]{1,0:T(8,128)(2,1)S(1)}, u32[]{:S(2)}, u32[]{:S(2)}) collective-permute-start(bf16[64,1024]{1,0:T(8,128)(2,1)S(1)} %get-tuple-element.85), channel_id=1, source_target_pairs={{1,0},{2,1},{3,2},{4,3},{5,4},{6,5},{7,6},{0,7},{9,8},{10,9},{11,1... | collective-permute-start | bytes 393224 | tf_op jit(solution)/shard_map/ppermute | solution.py:395
  42.3 8.3 %backward_inner.1 = (bf16[6,256,1024]{2,1,0:T(8,128)(2,1)S(1)}, bf16[6,64,1024]{2,1,0:T(8,128)(2,1)S(1)}, f32[64,256]{1,0:T(8,128)S(1)}, f32[192,192]{1,0:T(8,128)S(1)}, f32[64,256]{1,0:T(8,128)S(1)}) custom-call(s32[1]{0:T(128)S(6)} %copy.15.heights, s32[1]{0:T(128)S(6)} %copy.16.widths, bf16[8,64,1024]{2,1,0:T(8,128)(2,1)S(1)} %get-tuple-element.83.gmid2, ...), custom_call_target="tpu_custom_call" | custom-call | tf_op jit(solution)/shard_map/backward_inner/pallas_call | solution.py:377
  50.7 2.3 %backward_edge.1 = (bf16[2,256,1024]{2,1,0:T(8,128)(2,1)S(1)}, bf16[8,64,1024]{2,1,0:T(8,128)(2,1)S(1)}, f32[64,256]{1,0:T(8,128)S(1)}, f32[192,192]{1,0:T(8,128...) custom-call(s32[1]{0:T(128)S(6)} %copy.15.heights, s32[1]{0:T(128)S(6)} %copy.16.widths, ...), custom_call_target="tpu_custom_call" | custom-call | tf_op jit(solution)/shard_map/backward_edge/pallas_call | solution.py:377
  53.1 5.6 %collective-permute-start.7 = (bf16[64,1024]{1,0:T(8,128)(2,1)S(1)}, bf16[64,1024]{1,0:T(8,128)(2,1)S(1)}, u32[]{:S(2)}, u32[]{:S(2)}) collective-permute-start(bf16[64,1024]{1,0:T(8,128)(2,1)S(1)} %get-tuple-element.107), channel_id=1, source_target_pairs={{1,0},{2,1},{3,2},{4,3},{5,4},{6,5},{7,6},{0,7},{9,8},{10,9},{11,1... | collective-permute-start | bytes 393224 | tf_op jit(solution)/shard_map/ppermute | solution.py:395
  58.7 3.2 %last_inner.1 = (bf16[6,64,1024]{2,1,0:T(8,128)(2,1)S(1)}, f32[64,256]{1,0:T(8,128)S(1)}, f32[192,192]{1,0:T(8,128)S(1)}) custom-call(bf16[8,64,1024]{2,1,0:T(8,128)(2,1)S(1)} %get-tuple-element.103.gmid2, bf16[8,64,1024]{2,1,0:T(8,128)(2,1)S(1)} %get-tuple-element.73.first0, bf16[6,64,1024]{2,1,0:T(8,128)(2,1)S(1)} %get-tuple-element.104.slope1, ...), custom_call_target="tpu_custom_call" | custom-call | tf_op jit(solution)/shard_map/last_inner/pallas_call | solution.py:377
  61.9 1.2 %last_edge.1 = (bf16[2,64,1024]{2,1,0:T(8,128)(2,1)S(1)}, bf16[640,256]{1,0:T(8,128)(2,1)S(1)}) custom-call(bf16[8,64,1024]{2,1,0:T(8,128)(2,1)S(1)} %get-tuple-element.103.gmid2, bf16[64,1024]{1,0:T(8,128)(2,1)S(1)} %collective-permute-done.6.above, bf16[64,1024]{1,0:T(8,128)(2,1)S(1)} %collective-permute-done.7.below, ...), custom_call_target="tpu_custom_call" | custom-call | tf_op jit(solution)/shard_map/last_edge/pallas_call | solution.py:377
  63.2 13.2 %all_to_all.10 = bf16[16,40,256]{2,1,0:T(8,128)(2,1)S(1)} all-to-all(bf16[16,40,256]{2,1,0:T(8,128)(2,1)S(1)} %bitcast.10), channel_id=1, replica_groups=mesh['batch'=16,'space'=8] {'batch'}, dimensions={0} | all-to-all | bytes 655360 | tf_op jit(solution)/shard_map/all_to_all | solution.py:402
  76.5 3.8 %collective-permute-done.8 = bf16[40,256]{1,0:T(8,128)(2,1)S(1)} collective-permute-done((bf16[40,256]{1,0:T(8,128)(2,1)S(1)}, bf16[40,256]{1,0:T(8,128)(2,1)S(1)}, u32[]{:S(2)}, u32[]{:S(2)}) %collective-permute-start.8) | collective-permute-done | bytes 20512 | tf_op jit(solution)/shard_map/ppermute | solution.py:406
  80.6 4.7 %collective-permute-done.9 = bf16[40,256]{1,0:T(8,128)(2,1)S(1)} collective-permute-done((bf16[40,256]{1,0:T(8,128)(2,1)S(1)}, bf16[40,256]{1,0:T(8,128)(2,1)S(1)}, u32[]{:S(2)}, u32[]{:S(2)}) %collective-permute-start.9) | collective-permute-done | bytes 20512 | tf_op jit(solution)/shard_map/ppermute | solution.py:406
  85.3 3.4 %collective-permute-start.10 = (bf16[40,256]{1,0:T(8,128)(2,1)S(1)}, bf16[40,256]{1,0:T(8,128)(2,1)S(1)}, u32[]{:S(2)}, u32[]{:S(2)}) collective-permute-start(bf16[40,256]{1,0:T(8,128)(2,1)S(1)} %fusion.1), channel_id=1, source_target_pairs={{0,1},{1,0},{2,3},{3,2},{4,5},{5,4},{6,7},{7,6},{8,9},{9,8},{10,11... | collective-permute-start | bytes 61448 | tf_op jit(solution)/shard_map/ppermute | solution.py:406
  88.7 2.0 %collective-permute-done.10 = bf16[40,256]{1,0:T(8,128)(2,1)S(1)} collective-permute-done((bf16[40,256]{1,0:T(8,128)(2,1)S(1)}, bf16[40,256]{1,0:T(8,128)(2,1)S(1)}, u32[]{:S(2)}, u32[]{:S(2)}) %collective-permute-start.10) | collective-permute-done | bytes 20512 | tf_op jit(solution)/shard_map/ppermute | solution.py:406
  91.4 3.5 %all-to-all-start.1 = ((bf16[16,40,256]{2,1,0:T(8,128)(2,1)}), bf16[16,40,256]{2,1,0:T(8,128)(2,1)S(1)}, u32[]{:S(2)}, u32[]{:S(2)}) async-start(bf16[16,40,256]{2,1,0:T(8,128)(2,1)} %broadcast_in_dim.10), calls=%async_computation.1 | async-start | bytes 655360 | tf_op jit(solution)/shard_map/all_to_all | solution.py:408
  95.9 1.2 %copy-done.4 = bf16[2,256,1024]{2,1,0:T(8,128)(2,1)S(1)} copy-done((bf16[2,256,1024]{2,1,0:T(8,128)(2,1)S(1)}, bf16[2,256,1024]{2,1,0:T(8,128)(2,1)}, u32[]{:S(2)}) %copy-start.4) | copy-done | bytes 1048600
  97.1 1.1 %copy-done.6 = bf16[6,64,1024]{2,1,0:T(8,128)(2,1)S(1)} copy-done((bf16[6,64,1024]{2,1,0:T(8,128)(2,1)S(1)}, bf16[6,64,1024]{2,1,0:T(8,128)(2,1)}, u32[]{:S(2)}) %copy-start.6) | copy-done | bytes 786456
  99.2 2.9 %grad_images.1 = bf16[8,256,1024]{2,1,0:T(8,128)(2,1)} custom-call(bf16[6,64,1024]{2,1,0:T(8,128)(2,1)S(1)} %copy-done.6, bf16[2,64,1024]{2,1,0:T(8,128)(2,1)S(1)} %copy-done.8, bf16[6,256,1024]{2,1,0:T(8,128)(2,1)S(1)} %get-tuple-element.116.gsum_inner, bf16[2,256,1024]{2,1,0:T(8,128)(2,1)S(1)} %copy-done.4, bf16[2,256,64]{2,1,0:T(8,128)(2,1)S(1)} %copy-done.2), custom_call_target="tpu_custom_call" | custom-call | tf_op jit(solution)/shard_map/grad_images/pallas_call | solution.py:377
  102.2 1.3 %all-to-all-done.1 = bf16[16,40,256]{2,1,0:T(8,128)(2,1)S(1)} async-done(((bf16[16,40,256]{2,1,0:T(8,128)(2,1)}), bf16[16,40,256]{2,1,0:T(8,128)(2,1)S(1)}, u32[]{:S(2)}, u32[]{:S(2)}) %all-to-all-start.1) | async-done | bytes 327712 | tf_op jit(solution)/shard_map/all_to_all | solution.py:408
  (38 shorter events, 4.7 us)
Async XLA Ops:
  4.4 46.2 %copy-start.1 = (bf16[2,256,64]{2,1,0:T(8,128)(2,1)}, bf16[2,256,64]{2,1,0:T(8,128)(2,1)S(1)}, u32[]{:S(2)}) copy-start(bf16[2,256,64]{2,1,0:T(8,128)(2,1)S(1)} %get-tuple-element.93.wr_back) | copy-start | bytes 196612
  4.5 14.6 %collective-permute-start.1 = (bf16[64,1024]{1,0:T(8,128)(2,1)S(1)}, bf16[64,1024]{1,0:T(8,128)(2,1)S(1)}, u32[]{:S(2)}, u32[]{:S(2)}) collective-permute-start(bf16[64,1024]{1,0:T(8,128)(2,1)S(1)} %get-tuple-element.64.top), channel_id=1, source_target_pairs={{1,0},{2,1},{3,2},{4,3},{5,4},{6,5},{7,6},{0,7},{9,8},{10,9},{11,1... | collective-permute-start | bytes 393224 | tf_op jit(solution)/shard_map/ppermute | solution.py:395
  10.9 8.6 %collective-permute-start = (bf16[64,1024]{1,0:T(8,128)(2,1)S(1)}, bf16[64,1024]{1,0:T(8,128)(2,1)S(1)}, u32[]{:S(2)}, u32[]{:S(2)}) collective-permute-start(bf16[64,1024]{1,0:T(8,128)(2,1)S(1)} %get-tuple-element.65.bottom), channel_id=1, source_target_pairs={{0,1},{1,2},{2,3},{3,4},{4,5},{5,6},{6,7},{7,0},{8,9},{9,10},{10,1... | collective-permute-start | bytes 393224 | tf_op jit(solution)/shard_map/ppermute | solution.py:394
  19.0 8.6 %copy-start = (bf16[1,8,256,1024]{3,2,1,0:T(8,128)(2,1)S(1)}, bf16[1,8,256,1024]{3,2,1,0:T(8,128)(2,1)}, u32[]{:S(2)}) copy-start(bf16[1,8,256,1024]{3,2,1,0:T(8,128)(2,1)} %param.21) | copy-start | bytes 12582916
  21.9 12.2 %collective-permute-start.2 = (bf16[64,1024]{1,0:T(8,128)(2,1)S(1)}, bf16[64,1024]{1,0:T(8,128)(2,1)S(1)}, u32[]{:S(2)}, u32[]{:S(2)}) collective-permute-start(bf16[64,1024]{1,0:T(8,128)(2,1)S(1)} %get-tuple-element.76), channel_id=1, source_target_pairs={{0,1},{1,2},{2,3},{3,4},{4,5},{5,6},{6,7},{7,0},{8,9},{9,10},{10,1... | collective-permute-start | bytes 393224 | tf_op jit(solution)/shard_map/ppermute | solution.py:394
  23.5 10.6 %collective-permute-start.3 = (bf16[64,1024]{1,0:T(8,128)(2,1)S(1)}, bf16[64,1024]{1,0:T(8,128)(2,1)S(1)}, u32[]{:S(2)}, u32[]{:S(2)}) collective-permute-start(bf16[64,1024]{1,0:T(8,128)(2,1)S(1)} %get-tuple-element.77), channel_id=1, source_target_pairs={{1,0},{2,1},{3,2},{4,3},{5,4},{6,5},{7,6},{0,7},{9,8},{10,9},{11,1... | collective-permute-start | bytes 393224 | tf_op jit(solution)/shard_map/ppermute | solution.py:395
  36.6 14.0 %collective-permute-start.4 = (bf16[64,1024]{1,0:T(8,128)(2,1)S(1)}, bf16[64,1024]{1,0:T(8,128)(2,1)S(1)}, u32[]{:S(2)}, u32[]{:S(2)}) collective-permute-start(bf16[64,1024]{1,0:T(8,128)(2,1)S(1)} %get-tuple-element.84), channel_id=1, source_target_pairs={{0,1},{1,2},{2,3},{3,4},{4,5},{5,6},{6,7},{7,0},{8,9},{9,10},{10,1... | collective-permute-start | bytes 393224 | tf_op jit(solution)/shard_map/ppermute | solution.py:394
  36.7 14.0 %collective-permute-start.5 = (bf16[64,1024]{1,0:T(8,128)(2,1)S(1)}, bf16[64,1024]{1,0:T(8,128)(2,1)S(1)}, u32[]{:S(2)}, u32[]{:S(2)}) collective-permute-start(bf16[64,1024]{1,0:T(8,128)(2,1)S(1)} %get-tuple-element.85), channel_id=1, source_target_pairs={{1,0},{2,1},{3,2},{4,3},{5,4},{6,5},{7,6},{0,7},{9,8},{10,9},{11,1... | collective-permute-start | bytes 393224 | tf_op jit(solution)/shard_map/ppermute | solution.py:395
  53.0 10.2 %copy-start.3 = (bf16[2,256,1024]{2,1,0:T(8,128)(2,1)}, bf16[2,256,1024]{2,1,0:T(8,128)(2,1)S(1)}, u32[]{:S(2)}) copy-start(bf16[2,256,1024]{2,1,0:T(8,128)(2,1)S(1)} %get-tuple-element.117.gsum_edge) | copy-start | bytes 3145732
  53.0 8.9 %collective-permute-start.6 = (bf16[64,1024]{1,0:T(8,128)(2,1)S(1)}, bf16[64,1024]{1,0:T(8,128)(2,1)S(1)}, u32[]{:S(2)}, u32[]{:S(2)}) collective-permute-start(bf16[64,1024]{1,0:T(8,128)(2,1)S(1)} %get-tuple-element.106), channel_id=1, source_target_pairs={{0,1},{1,2},{2,3},{3,4},{4,5},{5,6},{6,7},{7,0},{8,9},{9,10},{10,1... | collective-permute-start | bytes 393224 | tf_op jit(solution)/shard_map/ppermute | solution.py:394
  53.1 8.8 %collective-permute-start.7 = (bf16[64,1024]{1,0:T(8,128)(2,1)S(1)}, bf16[64,1024]{1,0:T(8,128)(2,1)S(1)}, u32[]{:S(2)}, u32[]{:S(2)}) collective-permute-start(bf16[64,1024]{1,0:T(8,128)(2,1)S(1)} %get-tuple-element.107), channel_id=1, source_target_pairs={{1,0},{2,1},{3,2},{4,3},{5,4},{6,5},{7,6},{0,7},{9,8},{10,9},{11,1... | collective-permute-start | bytes 393224 | tf_op jit(solution)/shard_map/ppermute | solution.py:395
  61.9 14.5 %copy-start.5 = (bf16[6,64,1024]{2,1,0:T(8,128)(2,1)}, bf16[6,64,1024]{2,1,0:T(8,128)(2,1)S(1)}, u32[]{:S(2)}) copy-start(bf16[6,64,1024]{2,1,0:T(8,128)(2,1)S(1)} %get-tuple-element.105.gmid1_inner) | copy-start | bytes 2359300
  63.1 13.3 %copy-start.7 = (bf16[2,64,1024]{2,1,0:T(8,128)(2,1)}, bf16[2,64,1024]{2,1,0:T(8,128)(2,1)S(1)}, u32[]{:S(2)}) copy-start(bf16[2,64,1024]{2,1,0:T(8,128)(2,1)S(1)} %get-tuple-element.115.gmid1_edge) | copy-start | bytes 786436
  76.4 3.9 %collective-permute-start.8 = (bf16[40,256]{1,0:T(8,128)(2,1)S(1)}, bf16[40,256]{1,0:T(8,128)(2,1)S(1)}, u32[]{:S(2)}, u32[]{:S(2)}) collective-permute-start(bf16[40,256]{1,0:T(8,128)(2,1)S(1)} %convert_element_type.25), channel_id=1, source_target_pairs={{0,2},{1,3},{2,0},{3,1},{4,6},{5,7},{6,4},{7,5},{8,10},{9,11},{10,... | collective-permute-start | bytes 61448 | tf_op jit(solution)/shard_map/ppermute | solution.py:406
  80.3 5.0 %collective-permute-start.9 = (bf16[40,256]{1,0:T(8,128)(2,1)S(1)}, bf16[40,256]{1,0:T(8,128)(2,1)S(1)}, u32[]{:S(2)}, u32[]{:S(2)}) collective-permute-start(bf16[40,256]{1,0:T(8,128)(2,1)S(1)} %fusion), channel_id=1, source_target_pairs={{0,6},{1,7},{2,4},{3,5},{4,2},{5,3},{6,0},{7,1},{8,14},{9,15},{10,... | collective-permute-start | bytes 61448 | tf_op jit(solution)/shard_map/ppermute | solution.py:406
  85.3 5.4 %collective-permute-start.10 = (bf16[40,256]{1,0:T(8,128)(2,1)S(1)}, bf16[40,256]{1,0:T(8,128)(2,1)S(1)}, u32[]{:S(2)}, u32[]{:S(2)}) collective-permute-start(bf16[40,256]{1,0:T(8,128)(2,1)S(1)} %fusion.1), channel_id=1, source_target_pairs={{0,1},{1,0},{2,3},{3,2},{4,5},{5,4},{6,7},{7,6},{8,9},{9,8},{10,11... | collective-permute-start | bytes 61448 | tf_op jit(solution)/shard_map/ppermute | solution.py:406
  91.4 12.0 %all-to-all-start.1 = ((bf16[16,40,256]{2,1,0:T(8,128)(2,1)}), bf16[16,40,256]{2,1,0:T(8,128)(2,1)S(1)}, u32[]{:S(2)}, u32[]{:S(2)}) async-start(bf16[16,40,256]{2,1,0:T(8,128)(2,1)} %broadcast_in_dim.10), calls=%async_computation.1 | async-start | bytes 655360 | tf_op jit(solution)/shard_map/all_to_all | solution.py:408
  95.0 0.9 copy-start.2
  95.9 1.2 %copy-start.4 = (bf16[2,256,1024]{2,1,0:T(8,128)(2,1)S(1)}, bf16[2,256,1024]{2,1,0:T(8,128)(2,1)}, u32[]{:S(2)}) copy-start(bf16[2,256,1024]{2,1,0:T(8,128)(2,1)} %copy-done.3) | copy-start | bytes 3145732
  97.1 1.1 %copy-start.6 = (bf16[6,64,1024]{2,1,0:T(8,128)(2,1)S(1)}, bf16[6,64,1024]{2,1,0:T(8,128)(2,1)}, u32[]{:S(2)}) copy-start(bf16[6,64,1024]{2,1,0:T(8,128)(2,1)} %copy-done.5) | copy-start | bytes 2359300
  98.3 0.9 copy-start.8
  99.2 4.3 %copy-start.9 = (f32[2,256]{1,0:T(2,128)S(1)}, f32[2,256]{1,0:T(2,128)}, u32[]{:S(2)}) copy-start(f32[2,256]{1,0:T(2,128)} %scale_out.1) | copy-start | bytes 6148
where the time goes:
time: 105 us; the launch traced here: 104 us
  Pallas kernels  40.8 us (39%)
  starting transfers between devices  30.9 us (29%)
  blocking collectives  13.2 us (13%)
  waiting for transfers between devices  12.2 us (12%)
  local copies, waits for them, and re-layouts  4.98 us (5%)
  between operations  2.18 us (2%)
    pallas_call x11, Pallas kernels, call(): pl.pallas_call(kernel, in_specs=specs or [VMEM] * len(args), out_specs=ou...  40.8 us
    ppermute x4, starting transfers between devices, exchange(): lax.ppermute(top, 'space', [((i + 1) % count, i) for i in range(count)])  21.9 us
    all_to_all x1, blocking collectives, all_sum(): lax.all_to_all(terms.reshape(n, tall // n, across), 'batch', 0, 0, tiled=...  13.2 us
    ppermute x3, waiting for transfers between devices, all_sum(): lax.ppermute(share.astype(BF16), 'space', [(i, i ^ bit) for i in range(co...  10.4 us
    unnamed x20, local copies, waits for them, and re-layouts  4.24 us
    ppermute x3, starting transfers between devices, all_sum(): lax.ppermute(share.astype(BF16), 'space', [(i, i ^ bit) for i in range(co...  3.8 us
    all_to_all x1, starting transfers between devices, all_sum(): lax.all_to_all(spread_out, 'batch', 0, 0, tiled=True).reshape(terms.shape)  3.54 us
  transfers between devices with their start and end apart: 12, of which 5 were waited for; matrix products, arithmetic and copies ran while one was open for 0% of the time, Pallas kernels for 28%

commit v1 on v0

--- a/solution.py
+++ b/solution.py
@@ -11,7 +11,6 @@
 F32 = jnp.float32
 BF16 = jnp.bfloat16
 VMEM_LIMIT = 12 * 1024 * 1024
-CHUNK = 256
 VMEM = pl.BlockSpec(memory_space=pltpu.VMEM)
 SMEM = pl.BlockSpec(memory_space=pltpu.SMEM)
 HBM = pl.BlockSpec(memory_space=pltpu.HBM)
@@ -83,12 +82,12 @@
     return jnp.concatenate([after(v), v, before(v)], axis=0)
 
 
-def chunks(cols):
-    return [slice(c, c + CHUNK) for c in range(0, cols, CHUNK)]
+def chunks(cols, count=1):
+    return [slice(c, c + cols // count) for c in range(0, cols, cols // count)]
 
 
 def reduce_part(x, w_reduce, b_first, mask):
-    h = (mm(w_reduce[...], x) + wide(b_first, CHUNK)).astype(BF16)
+    h = (mm(w_reduce[...], x) + wide(b_first, x.shape[-1])).astype(BF16)
     y, d = gate(h)
     return y * mask, d * mask
 
@@ -135,11 +134,11 @@
     def work(row, slot, pre):
         mask = row_mask(*hw, row, rows, cols)
         for cut in chunks(cols):
-            h = (pre[:, cut] + wide(b_second, CHUNK)).astype(BF16)
+            h = (pre[:, cut] + wide(b_second, cols)).astype(BF16)
             y, d = gate(h)
             second[slot, :, cut] = y
             slope2[slot, :, cut] = d
-            h = (mm(we[...], y) + wide(b_out, CHUNK)).astype(BF16) + x[row, :, cut] * 0.5
+            h = (mm(we[...], y) + wide(b_out, cols)).astype(BF16) + x[row, :, cut] * 0.5
             y, d = gate(h)
             slope3[slot, :, cut] = d
             x1[slot, :, cut] = y
@@ -184,10 +183,10 @@
 
     def work(row, slot, pre):
         mask = row_mask(*hw, row, rows, cols)
-        for cut in chunks(cols):
-            h = (pre[:, cut] + wide(b2.at[1], CHUNK)).astype(BF16)
+        for cut in chunks(cols, 2):
+            h = (pre[:, cut] + wide(b2.at[1], cols // 2)).astype(BF16)
             y2, d2 = gate(h)
-            h = (mm(we[1], y2) + wide(b3.at[1], CHUNK)).astype(BF16) + x1[slot, :, cut] * 0.5
+            h = (mm(we[1], y2) + wide(b3.at[1], cols // 2)).astype(BF16) + x1[slot, :, cut] * 0.5
             _, d3 = gate(h)
             g = cot[row, :, cut] * mask[:, cut] * d3
             gsum[slot, :, cut] = g
@@ -396,7 +395,7 @@
     return above, below
 
 
-def all_sum(terms):
+def all_sum(terms, beside):
     n = lax.axis_size("batch")
     tall, across = terms.shape
     shares = lax.all_to_all(terms.reshape(n, tall // n, across), "batch", 0, 0, tiled=True)
@@ -405,7 +404,8 @@
     for bit in (2, 6, 1):
         share = share + lax.ppermute(share.astype(BF16), "space", [(i, i ^ bit) for i in range(count)]).astype(F32)
     spread_out = jnp.broadcast_to(share.astype(BF16)[None], (n,) + share.shape)
-    return lax.all_to_all(spread_out, "batch", 0, 0, tiled=True).reshape(terms.shape)
+    spread_out, beside = lax.optimization_barrier((spread_out, beside))
+    return lax.all_to_all(spread_out, "batch", 0, 0, tiled=True).reshape(terms.shape), beside
 
 
 def body(images, heights, widths, conv_reduce, conv_spatial, conv_expand, scale_mid, shift_mid,
@@ -470,7 +470,7 @@
     (grad,) = call(
         grad_rows, [large(rows)], [gmid1_0i, gmid1_0e, gsum0i, gsum0e, wr_back], "grad_images", out_specs=[HBM],
         scratch=[pltpu.VMEM(*large(rows)), pltpu.SemaphoreType.DMA((rows,))])
-    summed = all_sum(terms)
+    summed, grad = all_sum(terms, grad)
     factor = 1.0 / math.sqrt(lax.axis_size("batch") * rows * lax.axis_size("space") * cols)
     g_reduce, g_spatial, g_expand = call(
         functools.partial(finish, factor),

time: 105 us -> 99 us (0.943)
  blocking collectives: 13.2 us -> 24.3 us
  Pallas kernels: 40.8 us -> 33.1 us
  local copies, waits for them, and re-layouts: 4.98 us -> 0.03 us
  starting transfers between devices: 30.9 us -> 28.1 us
  waiting for transfers between devices: 12.2 us -> 10.5 us
    all_to_all x0 -> x1, blocking collectives: none -> 11.1 us  [all_sum(): lax.all_to_all(spread_out, 'batch', 0, 0, tiled=True).reshape(terms.shape)]
    pallas_call x11, Pallas kernels: 40.8 us -> 33.1 us  [call(): pl.pallas_call(kernel, in_specs=specs or [VMEM] * len(args), out_specs=ou...]
    unnamed x20 -> x4, local copies, waits for them, and re-layouts: 4.24 us -> 0.01 us
    all_to_all x1 -> x0, starting transfers between devices: 3.54 us -> none  [all_sum(): lax.all_to_all(spread_out, 'batch', 0, 0, tiled=True).reshape(terms.shape)]
    ppermute x3, waiting for transfers between devices: 10.4 us -> 7.71 us  [all_sum(): lax.ppermute(share.astype(BF16), 'space', [(i, i ^ bit) for i in range(co...]
    ppermute x4, waiting for transfers between devices: 0.49 us -> 2.81 us  [exchange(): lax.ppermute(bottom, 'space', [(i, (i + 1) % count) for i in range(count)])]
    ppermute x4, starting transfers between devices: 1.74 us -> 0.23 us  [exchange(): lax.ppermute(bottom, 'space', [(i, (i + 1) % count) for i in range(count)])]
    ppermute x4, starting transfers between devices: 21.9 us -> 23.4 us  [exchange(): lax.ppermute(top, 'space', [((i + 1) % count, i) for i in range(count)])]
  transfers between devices with their start and end apart: 12 -> 11, of which waited for: 5 -> 3; matrix products, arithmetic and copies ran while one was open for 0% -> 0% of each run, Pallas kernels for 28% -> 23%
where the time goes in v1:
time: 99 us; the launch traced here: 98.3 us
  Pallas kernels  33.1 us (33%)
  starting transfers between devices  28.1 us (28%)
  blocking collectives  24.3 us (25%)
  waiting for transfers between devices  10.5 us (11%)
  between operations  2.13 us (2%)
    pallas_call x11, Pallas kernels, call(): pl.pallas_call(kernel, in_specs=specs or [VMEM] * len(args), out_specs=ou...  33.1 us
    ppermute x4, starting transfers between devices, exchange(): lax.ppermute(top, 'space', [((i + 1) % count, i) for i in range(count)])  23.4 us
    all_to_all x1, blocking collectives, all_sum(): lax.all_to_all(terms.reshape(n, tall // n, across), 'batch', 0, 0, tiled=...  13.2 us
    all_to_all x1, blocking collectives, all_sum(): lax.all_to_all(spread_out, 'batch', 0, 0, tiled=True).reshape(terms.shape)  11.1 us
    ppermute x3, waiting for transfers between devices, all_sum(): lax.ppermute(share.astype(BF16), 'space', [(i, i ^ bit) for i in range(co...  7.71 us
    ppermute x3, starting transfers between devices, all_sum(): lax.ppermute(share.astype(BF16), 'space', [(i, i ^ bit) for i in range(co...  4.56 us
    ppermute x4, waiting for transfers between devices, exchange(): lax.ppermute(bottom, 'space', [(i, (i + 1) % count) for i in range(count)])  2.81 us
  transfers between devices with their start and end apart: 11, of which 3 were waited for; matrix products, arithmetic and copies ran while one was open for 0% of the time, Pallas kernels for 23%

profile of v1, /device:TPU:0, one launch (start us, length us, event | category | flops | bytes accessed | tf_op | source)
XLA Modules:
  0.0 98.3 jit_solution(12947443369939194780)
XLA Ops:
  1.9 2.5 %start.1 = (bf16[2,64,256]{2,1,0:T(8,128)(2,1)S(1)}, bf16[2,192,192]{2,1,0:T(8,128)(2,1)S(1)}, bf16[2,384,256]{2,1,0:T(8,128)(2,1)S(1)}, bf16[2,256,64]{2,1,0:T(...) custom-call(s32[1]{0:T(128)S(6)} %copy.15.heights, ...), custom_call_target="tpu_custom_call" | custom-call | tf_op jit(solution)/shard_map/start/pallas_call | solution.py:376
  4.4 6.5 %collective-permute-start.1 = (bf16[64,1024]{1,0:T(8,128)(2,1)S(1)}, bf16[64,1024]{1,0:T(8,128)(2,1)S(1)}, u32[]{:S(2)}, u32[]{:S(2)}) collective-permute-start(bf16[64,1024]{1,0:T(8,128)(2,1)S(1)} %get-tuple-element.66.top), channel_id=1, source_target_pairs={{1,0},{2,1},{3,2},{4,3},{5,4},{6,5},{7,6},{0,7},{9,8},{10,9},{11,1... | collective-permute-start | bytes 393224 | tf_op jit(solution)/shard_map/ppermute | solution.py:394
  10.9 5.7 %forward_inner.1 = (bf16[8,64,1024]{2,1,0:T(8,128)(2,1)S(1)}, bf16[6,64,1024]{2,1,0:T(8,128)(2,1)S(1)}, bf16[6,64,1024]{2,1,0:T(8,128)(2,1)S(1)}, bf16[6,64,1024...) custom-call(s32[1]{0:T(128)S(6)} %copy.15.heights, ...), custom_call_target="tpu_custom_call" | custom-call | tf_op jit(solution)/shard_map/forward_inner/pallas_call | solution.py:376
  16.7 2.8 %collective-permute-done.above.f_above = bf16[64,1024]{1,0:T(8,128)(2,1)S(1)} collective-permute-done((bf16[64,1024]{1,0:T(8,128)(2,1)S(1)}, bf16[64,1024]{1,0:T(8,128)(2,1)S(1)}, u32[]{:S(2)}, u32[]{:S(2)}) %collective-permute-start) | collective-permute-done | bytes 131104 | tf_op jit(solution)/shard_map/ppermute | solution.py:393
  19.5 1.6 %forward_edge.1 = (bf16[2,64,1024]{2,1,0:T(8,128)(2,1)S(1)}, bf16[2,64,1024]{2,1,0:T(8,128)(2,1)S(1)}, bf16[2,256,1024]{2,1,0:T(8,128)(2,1)S(1)}, bf16[2,256,102...) custom-call(s32[1]{0:T(128)S(6)} %copy.15.heights, ...), custom_call_target="tpu_custom_call" | custom-call | tf_op jit(solution)/shard_map/forward_edge/pallas_call | solution.py:376
  21.1 0.1 collective-permute-start.2
  21.2 5.6 %collective-permute-start.3 = (bf16[64,1024]{1,0:T(8,128)(2,1)S(1)}, bf16[64,1024]{1,0:T(8,128)(2,1)S(1)}, u32[]{:S(2)}, u32[]{:S(2)}) collective-permute-start(bf16[64,1024]{1,0:T(8,128)(2,1)S(1)} %get-tuple-element.79), channel_id=1, source_target_pairs={{1,0},{2,1},{3,2},{4,3},{5,4},{6,5},{7,6},{0,7},{9,8},{10,9},{11,1... | collective-permute-start | bytes 393224 | tf_op jit(solution)/shard_map/ppermute | solution.py:394
  26.8 5.0 %turn_inner.1 = (bf16[6,256,1024]{2,1,0:T(8,128)(2,1)S(1)}, bf16[6,64,1024]{2,1,0:T(8,128)(2,1)S(1)}, f32[64,256]{1,0:T(8,128)S(1)}) custom-call(s32[1]{0:T(128)S(6)} %copy.15.heights, s32[1]{0:T(128)S(6)} %copy.16.widths, bf16[8,64,1024]{2,1,0:T(8,128)(2,1)S(1)} %get-tuple-element.77.first1, bf16[6,256,1024]{2,1,0:T(8,128)(2,1)S(1)} %get-tuple-element.82.x1, ...), custom_call_target="tpu_custom_call" | custom-call | tf_op jit(solution)/shard_map/turn_inner/pallas_call | solution.py:376
  31.8 2.1 %turn_edge.1 = (bf16[2,256,1024]{2,1,0:T(8,128)(2,1)S(1)}, bf16[8,64,1024]{2,1,0:T(8,128)(2,1)S(1)}, f32[64,256]{1,0:T(8,128)S(1)}, bf16[64,1024]{1,0:T(8,128)(2,1)S(1)}, bf16[64,1024]{1,0:T(8,128)(2,1)S(1)}) custom-call(s32[1]{0:T(128)S(6)} %copy.15.heights, s32[1]{0:T(128)S(6)} %copy.16.widths, bf16[8,64,1024]{2,1,0:T(8,128)(2,1)S(1)} %get-tuple-element.77.first1, ...), custom_call_target="tpu_custom_call" | custom-call | tf_op jit(solution)/shard_map/turn_edge/pallas_call | solution.py:376
  34.0 5.6 %collective-permute-start.5 = (bf16[64,1024]{1,0:T(8,128)(2,1)S(1)}, bf16[64,1024]{1,0:T(8,128)(2,1)S(1)}, u32[]{:S(2)}, u32[]{:S(2)}) collective-permute-start(bf16[64,1024]{1,0:T(8,128)(2,1)S(1)} %get-tuple-element.87), channel_id=1, source_target_pairs={{1,0},{2,1},{3,2},{4,3},{5,4},{6,5},{7,6},{0,7},{9,8},{10,9},{11,1... | collective-permute-start | bytes 393224 | tf_op jit(solution)/shard_map/ppermute | solution.py:394
  39.6 5.7 %backward_inner.1 = (bf16[6,256,1024]{2,1,0:T(8,128)(2,1)S(1)}, bf16[6,64,1024]{2,1,0:T(8,128)(2,1)S(1)}, f32[64,256]{1,0:T(8,128)S(1)}, f32[192,192]{1,0:T(8,128)S(1)}, f32[64,256]{1,0:T(8,128)S(1)}) custom-call(s32[1]{0:T(128)S(6)} %copy.15.heights, s32[1]{0:T(128)S(6)} %copy.16.widths, bf16[8,64,1024]{2,1,0:T(8,128)(2,1)S(1)} %get-tuple-element.85.gmid2, ...), custom_call_target="tpu_custom_call" | custom-call | tf_op jit(solution)/shard_map/backward_inner/pallas_call | solution.py:376
  45.3 2.2 %backward_edge.1 = (bf16[2,256,1024]{2,1,0:T(8,128)(2,1)S(1)}, bf16[8,64,1024]{2,1,0:T(8,128)(2,1)S(1)}, f32[64,256]{1,0:T(8,128)S(1)}, f32[192,192]{1,0:T(8,128...) custom-call(s32[1]{0:T(128)S(6)} %copy.15.heights, s32[1]{0:T(128)S(6)} %copy.16.widths, ...), custom_call_target="tpu_custom_call" | custom-call | tf_op jit(solution)/shard_map/backward_edge/pallas_call | solution.py:376
  47.6 5.6 %collective-permute-start.7 = (bf16[64,1024]{1,0:T(8,128)(2,1)S(1)}, bf16[64,1024]{1,0:T(8,128)(2,1)S(1)}, u32[]{:S(2)}, u32[]{:S(2)}) collective-permute-start(bf16[64,1024]{1,0:T(8,128)(2,1)S(1)} %get-tuple-element.107), channel_id=1, source_target_pairs={{1,0},{2,1},{3,2},{4,3},{5,4},{6,5},{7,6},{0,7},{9,8},{10,9},{11,1... | collective-permute-start | bytes 393224 | tf_op jit(solution)/shard_map/ppermute | solution.py:394
  53.2 3.2 %last_inner.1 = (bf16[6,64,1024]{2,1,0:T(8,128)(2,1)S(1)}, f32[64,256]{1,0:T(8,128)S(1)}, f32[192,192]{1,0:T(8,128)S(1)}) custom-call(bf16[8,64,1024]{2,1,0:T(8,128)(2,1)S(1)} %get-tuple-element.105.gmid2, bf16[8,64,1024]{2,1,0:T(8,128)(2,1)S(1)} %get-tuple-element.75.first0, bf16[6,64,1024]{2,1,0:T(8,128)(2,1)S(1)} %get-tuple-element.109.slope1, ...), custom_call_target="tpu_custom_call" | custom-call | tf_op jit(solution)/shard_map/last_inner/pallas_call | solution.py:376
  56.4 1.2 %last_edge.1 = (bf16[2,64,1024]{2,1,0:T(8,128)(2,1)S(1)}, bf16[640,256]{1,0:T(8,128)(2,1)S(1)}) custom-call(bf16[8,64,1024]{2,1,0:T(8,128)(2,1)S(1)} %get-tuple-element.105.gmid2, bf16[64,1024]{1,0:T(8,128)(2,1)S(1)} %collective-permute-done.6.above, bf16[64,1024]{1,0:T(8,128)(2,1)S(1)} %collective-permute-done.7.below, ...), custom_call_target="tpu_custom_call" | custom-call | tf_op jit(solution)/shard_map/last_edge/pallas_call | solution.py:376
  57.7 13.2 %all_to_all.10 = bf16[16,40,256]{2,1,0:T(8,128)(2,1)S(1)} all-to-all(bf16[16,40,256]{2,1,0:T(8,128)(2,1)S(1)} %bitcast.10), channel_id=1, replica_groups=mesh['batch'=16,'space'=8] {'batch'}, dimensions={0} | all-to-all | bytes 655360 | tf_op jit(solution)/shard_map/all_to_all | solution.py:401
  70.9 0.1 collective-permute-start.8
  71.0 3.8 %collective-permute-done.8 = bf16[40,256]{1,0:T(8,128)(2,1)S(1)} collective-permute-done((bf16[40,256]{1,0:T(8,128)(2,1)S(1)}, bf16[40,256]{1,0:T(8,128)(2,1)S(1)}, u32[]{:S(2)}, u32[]{:S(2)}) %collective-permute-start.8) | collective-permute-done | bytes 20512 | tf_op jit(solution)/shard_map/ppermute | solution.py:405
  74.8 1.1 %collective-permute-start.9 = (bf16[40,256]{1,0:T(8,128)(2,1)S(1)}, bf16[40,256]{1,0:T(8,128)(2,1)S(1)}, u32[]{:S(2)}, u32[]{:S(2)}) collective-permute-start(bf16[40,256]{1,0:T(8,128)(2,1)S(1)} %fusion), channel_id=1, source_target_pairs={{0,6},{1,7},{2,4},{3,5},{4,2},{5,3},{6,0},{7,1},{8,14},{9,15},{10,... | collective-permute-start | bytes 61448 | tf_op jit(solution)/shard_map/ppermute | solution.py:405
  75.9 3.9 %collective-permute-done.9 = bf16[40,256]{1,0:T(8,128)(2,1)S(1)} collective-permute-done((bf16[40,256]{1,0:T(8,128)(2,1)S(1)}, bf16[40,256]{1,0:T(8,128)(2,1)S(1)}, u32[]{:S(2)}, u32[]{:S(2)}) %collective-permute-start.9) | collective-permute-done | bytes 20512 | tf_op jit(solution)/shard_map/ppermute | solution.py:405
  79.8 3.4 %collective-permute-start.10 = (bf16[40,256]{1,0:T(8,128)(2,1)S(1)}, bf16[40,256]{1,0:T(8,128)(2,1)S(1)}, u32[]{:S(2)}, u32[]{:S(2)}) collective-permute-start(bf16[40,256]{1,0:T(8,128)(2,1)S(1)} %fusion.1), channel_id=1, source_target_pairs={{0,1},{1,0},{2,3},{3,2},{4,5},{5,4},{6,7},{7,6},{8,9},{9,8},{10,11... | collective-permute-start | bytes 61448 | tf_op jit(solution)/shard_map/ppermute | solution.py:405
  83.2 2.9 %grad_images.1 = bf16[8,256,1024]{2,1,0:T(8,128)(2,1)} custom-call(bf16[6,64,1024]{2,1,0:T(8,128)(2,1)S(1)} %get-tuple-element.117.gmid1_inner, bf16[2,64,1024]{2,1,0:T(8,128)(2,1)S(1)} %get-tuple-element.118.gmid1_edge, bf16[6,256,1024]{2,1,0:T(8,128)(2,1)S(1)} %get-tuple-element.119.gsum_inner, bf16[2,256,1024]{2,1,0:T(8,128)(2,1)S(1)} %get-tuple-element.120.gsum_edge, ...), custom_call_target="tpu_custom_call" | custom-call | tf_op jit(solution)/shard_map/grad_images/pallas_call | solution.py:376
  86.2 11.1 %all_to_all.11 = bf16[16,40,256]{2,1,0:T(8,128)(2,1)S(1)} all-to-all(bf16[16,40,256]{2,1,0:T(8,128)(2,1)S(1)} %broadcast_in_dim.4), channel_id=1, replica_groups=mesh['batch'=16,'space'=8] {'batch'}, dimensions={0} | all-to-all | bytes 655360 | tf_op jit(solution)/shard_map/all_to_all | solution.py:408
  97.4 1.0 finish.1
  (21 shorter events, 0.3 us)
Async XLA Ops:
  4.4 12.3 %collective-permute-start.1 = (bf16[64,1024]{1,0:T(8,128)(2,1)S(1)}, bf16[64,1024]{1,0:T(8,128)(2,1)S(1)}, u32[]{:S(2)}, u32[]{:S(2)}) collective-permute-start(bf16[64,1024]{1,0:T(8,128)(2,1)S(1)} %get-tuple-element.66.top), channel_id=1, source_target_pairs={{1,0},{2,1},{3,2},{4,3},{5,4},{6,5},{7,6},{0,7},{9,8},{10,9},{11,1... | collective-permute-start | bytes 393224 | tf_op jit(solution)/shard_map/ppermute | solution.py:394
  10.9 8.6 %collective-permute-start = (bf16[64,1024]{1,0:T(8,128)(2,1)S(1)}, bf16[64,1024]{1,0:T(8,128)(2,1)S(1)}, u32[]{:S(2)}, u32[]{:S(2)}) collective-permute-start(bf16[64,1024]{1,0:T(8,128)(2,1)S(1)} %get-tuple-element.67.bottom), channel_id=1, source_target_pairs={{0,1},{1,2},{2,3},{3,4},{4,5},{5,6},{6,7},{7,0},{8,9},{9,10},{10,1... | collective-permute-start | bytes 393224 | tf_op jit(solution)/shard_map/ppermute | solution.py:393
  16.7 10.1 %copy-start = (bf16[1,8,256,1024]{3,2,1,0:T(8,128)(2,1)S(1)}, bf16[1,8,256,1024]{3,2,1,0:T(8,128)(2,1)}, u32[]{:S(2)}) copy-start(bf16[1,8,256,1024]{3,2,1,0:T(8,128)(2,1)} %param.21) | copy-start | bytes 12582916
  21.1 10.7 %collective-permute-start.2 = (bf16[64,1024]{1,0:T(8,128)(2,1)S(1)}, bf16[64,1024]{1,0:T(8,128)(2,1)S(1)}, u32[]{:S(2)}, u32[]{:S(2)}) collective-permute-start(bf16[64,1024]{1,0:T(8,128)(2,1)S(1)} %get-tuple-element.78), channel_id=1, source_target_pairs={{0,1},{1,2},{2,3},{3,4},{4,5},{5,6},{6,7},{7,0},{8,9},{9,10},{10,1... | collective-permute-start | bytes 393224 | tf_op jit(solution)/shard_map/ppermute | solution.py:393
  21.2 10.6 %collective-permute-start.3 = (bf16[64,1024]{1,0:T(8,128)(2,1)S(1)}, bf16[64,1024]{1,0:T(8,128)(2,1)S(1)}, u32[]{:S(2)}, u32[]{:S(2)}) collective-permute-start(bf16[64,1024]{1,0:T(8,128)(2,1)S(1)} %get-tuple-element.79), channel_id=1, source_target_pairs={{1,0},{2,1},{3,2},{4,3},{5,4},{6,5},{7,6},{0,7},{9,8},{10,9},{11,1... | collective-permute-start | bytes 393224 | tf_op jit(solution)/shard_map/ppermute | solution.py:394
  33.9 11.4 %collective-permute-start.4 = (bf16[64,1024]{1,0:T(8,128)(2,1)S(1)}, bf16[64,1024]{1,0:T(8,128)(2,1)S(1)}, u32[]{:S(2)}, u32[]{:S(2)}) collective-permute-start(bf16[64,1024]{1,0:T(8,128)(2,1)S(1)} %get-tuple-element.86), channel_id=1, source_target_pairs={{0,1},{1,2},{2,3},{3,4},{4,5},{5,6},{6,7},{7,0},{8,9},{9,10},{10,1... | collective-permute-start | bytes 393224 | tf_op jit(solution)/shard_map/ppermute | solution.py:393
  34.0 11.3 %collective-permute-start.5 = (bf16[64,1024]{1,0:T(8,128)(2,1)S(1)}, bf16[64,1024]{1,0:T(8,128)(2,1)S(1)}, u32[]{:S(2)}, u32[]{:S(2)}) collective-permute-start(bf16[64,1024]{1,0:T(8,128)(2,1)S(1)} %get-tuple-element.87), channel_id=1, source_target_pairs={{1,0},{2,1},{3,2},{4,3},{5,4},{6,5},{7,6},{0,7},{9,8},{10,9},{11,1... | collective-permute-start | bytes 393224 | tf_op jit(solution)/shard_map/ppermute | solution.py:394
  47.5 8.9 %collective-permute-start.6 = (bf16[64,1024]{1,0:T(8,128)(2,1)S(1)}, bf16[64,1024]{1,0:T(8,128)(2,1)S(1)}, u32[]{:S(2)}, u32[]{:S(2)}) collective-permute-start(bf16[64,1024]{1,0:T(8,128)(2,1)S(1)} %get-tuple-element.106), channel_id=1, source_target_pairs={{0,1},{1,2},{2,3},{3,4},{4,5},{5,6},{6,7},{7,0},{8,9},{9,10},{10,1... | collective-permute-start | bytes 393224 | tf_op jit(solution)/shard_map/ppermute | solution.py:393
  47.6 8.8 %collective-permute-start.7 = (bf16[64,1024]{1,0:T(8,128)(2,1)S(1)}, bf16[64,1024]{1,0:T(8,128)(2,1)S(1)}, u32[]{:S(2)}, u32[]{:S(2)}) collective-permute-start(bf16[64,1024]{1,0:T(8,128)(2,1)S(1)} %get-tuple-element.107), channel_id=1, source_target_pairs={{1,0},{2,1},{3,2},{4,3},{5,4},{6,5},{7,6},{0,7},{9,8},{10,9},{11,1... | collective-permute-start | bytes 393224 | tf_op jit(solution)/shard_map/ppermute | solution.py:394
  70.9 3.9 %collective-permute-start.8 = (bf16[40,256]{1,0:T(8,128)(2,1)S(1)}, bf16[40,256]{1,0:T(8,128)(2,1)S(1)}, u32[]{:S(2)}, u32[]{:S(2)}) collective-permute-start(bf16[40,256]{1,0:T(8,128)(2,1)S(1)} %convert_element_type.25), channel_id=1, source_target_pairs={{0,2},{1,3},{2,0},{3,1},{4,6},{5,7},{6,4},{7,5},{8,10},{9,11},{10,... | collective-permute-start | bytes 61448 | tf_op jit(solution)/shard_map/ppermute | solution.py:405
  74.8 5.0 %collective-permute-start.9 = (bf16[40,256]{1,0:T(8,128)(2,1)S(1)}, bf16[40,256]{1,0:T(8,128)(2,1)S(1)}, u32[]{:S(2)}, u32[]{:S(2)}) collective-permute-start(bf16[40,256]{1,0:T(8,128)(2,1)S(1)} %fusion), channel_id=1, source_target_pairs={{0,6},{1,7},{2,4},{3,5},{4,2},{5,3},{6,0},{7,1},{8,14},{9,15},{10,... | collective-permute-start | bytes 61448 | tf_op jit(solution)/shard_map/ppermute | solution.py:405
  79.8 6.4 %collective-permute-start.10 = (bf16[40,256]{1,0:T(8,128)(2,1)S(1)}, bf16[40,256]{1,0:T(8,128)(2,1)S(1)}, u32[]{:S(2)}, u32[]{:S(2)}) collective-permute-start(bf16[40,256]{1,0:T(8,128)(2,1)S(1)} %fusion.1), channel_id=1, source_target_pairs={{0,1},{1,0},{2,3},{3,2},{4,5},{5,4},{6,7},{7,6},{8,9},{9,8},{10,11... | collective-permute-start | bytes 61448 | tf_op jit(solution)/shard_map/ppermute | solution.py:405
  83.2 14.1 %copy-start.1 = (f32[2,256]{1,0:T(2,128)S(1)}, f32[2,256]{1,0:T(2,128)}, u32[]{:S(2)}) copy-start(f32[2,256]{1,0:T(2,128)} %scale_out.1) | copy-start | bytes 6148

commit v2 on v1

v2 whole, which is shorter than its diff:
```python
import functools
import math

import jax
import jax.numpy as jnp
from jax import lax
from jax.experimental import pallas as pl
from jax.experimental.pallas import tpu as pltpu
from jax.sharding import PartitionSpec as P

F32 = jnp.float32
BF16 = jnp.bfloat16
VMEM_LIMIT = 12 * 1024 * 1024
BESIDE = 2
VMEM = pl.BlockSpec(memory_space=pltpu.VMEM)
HBM = pl.BlockSpec(memory_space=pltpu.HBM)


def mm(a, b):
    return lax.dot_general(a, b, (((1,), (0,)), ((), ())), preferred_element_type=F32)


def mm_nt(a, b):
    return lax.dot_general(a, b, (((1,), (1,)), ((), ())), preferred_element_type=F32)


def gate(h):
    t = jnp.tanh(h)
    p = 1 + t
    y = h * p
    return y.astype(BF16), (p + y * (1 - t)).astype(BF16)


def wide(bias, cols):
    return jnp.concatenate([bias[...]] * (cols // bias.shape[-1]), axis=1)


def row_mask(limits, row, cols):
    limit = jnp.concatenate([limits[row : row + 1, :]] * (cols // limits.shape[1]), axis=1)
    ids = lax.broadcasted_iota(jnp.int32, (1, cols), 1)
    return jnp.where(ids < limit, 1.0, 0.0).astype(BF16)


def inside(mask, row, chans):
    return jnp.concatenate([mask[row]] * (chans // mask.shape[1]), axis=0)


def before(v):
    v = pltpu.roll(v, 1, 1)
    ids = lax.broadcasted_iota(jnp.int32, (1, 128), 1)
    edge = v[:, :128] * jnp.where(ids > 0, 1.0, 0.0).astype(v.dtype)
    return jnp.concatenate([edge, v[:, 128:]], axis=1)


def after(v):
    cols = v.shape[-1]
    v = pltpu.roll(v, cols - 1, 1)
    ids = lax.broadcasted_iota(jnp.int32, (1, 128), 1)
    edge = v[:, cols - 128 :] * jnp.where(ids < 127, 1.0, 0.0).astype(v.dtype)
    return jnp.concatenate([v[:, : cols - 128], edge], axis=1)


def edge_taps(strip, halo_above, halo_below, last):
    me = lax.axis_index("space")
    rows = strip.shape[0]
    if last:
        have = jnp.where(me < lax.axis_size("space") - 1, 1.0, 0.0).astype(BF16)
        parts = [strip[rows - 2], strip[rows - 1], halo_below[...] * have]
    else:
        have = jnp.where(me > 0, 1.0, 0.0).astype(BF16)
        parts = [halo_above[...] * have, strip[0], strip[1]]
    return jnp.concatenate(parts, axis=0)


def inner_taps(strip, row, count):
    part = strip[pl.ds(row - 1, count)]
    return part.reshape(part.shape[0] * part.shape[1], part.shape[2])


def join(out, flip):
    mid = out.shape[0] // 3
    first, centre, last = out[:mid], out[mid : 2 * mid], out[2 * mid :]
    if flip:
        first, last = last, first
    return before(first) + centre + after(last)


def spread(v):
    return jnp.concatenate([after(v), v, before(v)], axis=0)


def chunks(cols, count=1):
    return [slice(c, c + cols // count) for c in range(0, cols, cols // count)]


def reduce_part(x, w_reduce, b_first, mask):
    h = mm(w_reduce[...], x) + wide(b_first, x.shape[-1])
    y, d = gate(h)
    return y * mask, d * mask


def conv_rows(edges, rows, strip, halos, single, double, flip, work, unroll=True):
    if edges:
        ends = [mm(single[...], edge_taps(strip, *halos, last)) for last in (False, True)]
        work([(0, 0, join(ends[0], flip)), (rows - 1, 1, join(ends[1], flip))])
        return

    def pair(i, carry):
        row = 1 + 2 * i
        out = mm(double[...], inner_taps(strip, row, 4))
        half = out.shape[0] // 2
        work([(row, row - 1, join(out[:half], flip)), (row + 1, row, join(out[half:], flip))])
        return carry

    lax.fori_loop(0, (rows - 2) // 2, pair, 0, unroll=unroll)


def both(weights, pair):
    out = mm(weights, jnp.concatenate(pair, axis=0))
    half = out.shape[0] // 2
    return out[:half], out[half:]


def mm_nt_sum(pairs):
    return mm_nt(*(jnp.concatenate(side, axis=1) for side in zip(*pairs)))


def tap_terms(first, gmid2, rows):
    return mm_nt_sum([(inner_taps(first, row, 3), spread(gmid2[row])) for row in rows])


def edge_tap_terms(first, halos, gmid2):
    ends = ((False, 0), (True, first.shape[0] - 1))
    return mm_nt_sum([(edge_taps(first, *halos, last), spread(gmid2[row])) for last, row in ends])


def start_sums(have, sums):
    for value, out in zip(have or [None] * len(sums), sums):
        out[...] = jnp.zeros_like(out) if value is None else value[...]


def gather_rows(full, inner, top, bottom):
    rows = full.shape[0]
    full[0] = top[...]
    full[rows - 1] = bottom[...]
    for r in range(1, rows - 1):
        full[r] = inner[r - 1]


def forward_rows(edges, mask, rows, strip, halos, x, kf, kf2, b_second, we, b_out, w_reduce, b_first,
                 second, slope2, slope3, x1, slope1, put_first):
    cols = x.shape[-1]

    def work(pair):
        seconds = []
        for _, slot, pre in pair:
            y, d = gate(pre + wide(b_second, cols))
            second[slot] = y
            slope2[slot] = d
            seconds.append(y)
        for (row, slot, _), expanded in zip(pair, both(we[...], seconds)):
            y, d = gate(expanded + wide(b_out, cols) + x[row].astype(F32) * 0.5)
            slope3[slot] = d
            x1[slot] = y
            first, slope1[slot] = reduce_part(y, w_reduce, b_first, inside(mask, row, slope1.shape[1]))
            put_first(row, slot, first)

    conv_rows(edges, rows, strip, halos, kf, kf2, False, work)


def forward_inner(mask, x, top, bottom, wr_0, b1_0, red, spa, exp, scale_mid, shift_mid, scale_out, shift_out,
                  first0, slope1_0, second, slope2, slope3, x1, slope1_1, first1,
                  wr, kf, kf2, we, we_back, kb, kb2, wr_back, b1, b2, b3):
    rows, cols = x.shape[0], x.shape[-1]
    prepare(red, spa, exp, scale_mid, shift_mid, scale_out, shift_out, wr, kf, kf2, we, we_back, kb, kb2, wr_back, b1, b2, b3)
    first0[0] = top[...]
    first0[rows - 1] = bottom[...]

    @pl.loop(1, rows - 1, unroll=True)
    def _(row):
        first0[row], slope1_0[row - 1] = reduce_part(x[row], wr_0, b1_0, inside(mask, row, first0.shape[1]))

    def put_first(row, slot, value):
        first1[slot] = value

    forward_rows(False, mask, rows, first0, None, x, kf.at[0], kf2.at[0], b2.at[0], we.at[0], b3.at[0],
                 wr, b1, second, slope2, slope3, x1, slope1_1, put_first)


def forward_edge(mask, x, first0, above, below, first1_inner, kf, kf2, b2, we, b3, wr, b1,
                 second, slope2, slope3, x1, slope1_1, first1, top, bottom):
    def put_first(row, slot, value):
        (bottom if slot else top)[...] = value

    forward_rows(True, mask, first0.shape[0], first0, (above, below), x, kf.at[0], kf2.at[0], b2.at[0], we.at[0],
                 b3.at[0], wr, b1, second, slope2, slope3, x1, slope1_1, put_first)
    gather_rows(first1, first1_inner, top, bottom)


def turn_rows(edges, mask, first1, halos, x1, cot, kf, kf2, b2, we, b3, we_back, gsum, dexp, put_mid2, second=None):
    rows, cols = cot.shape[0], cot.shape[-1]

    def work(pair):
        gates = [gate(pre + wide(b2.at[1], cols)) for _, _, pre in pair]
        expanded = both(we[1], [y2 for y2, _ in gates])
        terms = []
        for (row, slot, _), (y2, d2), pre3 in zip(pair, gates, expanded):
            _, d3 = gate(pre3 + wide(b3.at[1], cols) + x1[slot].astype(F32) * 0.5)
            g = cot[row] * inside(mask, row, cot.shape[1]) * d3
            gsum[slot] = g
            put_mid2(row, slot, mm(we_back[1], g).astype(BF16) * d2)
            terms.append((y2, g))
            if edges:
                second[slot] = y2
        if not edges:
            dexp[...] += mm_nt_sum(terms)

    conv_rows(edges, rows, first1, halos, kf.at[1], kf2.at[1], False, work)


def turn_inner(mask, first1, x1, cot, kf, kf2, b2, we, b3, we_back, gsum, gmid2, dexp):
    start_sums(None, [dexp])

    def put_mid2(row, slot, value):
        gmid2[slot] = value

    turn_rows(False, mask, first1, None, x1, cot, kf, kf2, b2, we, b3, we_back, gsum, dexp, put_mid2)


def turn_edge(mask, first1, above, below, x1, cot, kf, kf2, b2, we, b3, we_back, gmid2_inner,
              gsum, gmid2, second, top, bottom):

    def put_mid2(row, slot, value):
        (bottom if slot else top)[...] = value

    turn_rows(True, mask, first1, (above, below), x1, cot, kf, kf2, b2, we, b3, we_back, gsum, None, put_mid2, second)
    gather_rows(gmid2, gmid2_inner, top, bottom)


def backward_rows(edges, mask, gmid2, g_halos, first1, slope1, x1, gsum1, slope3, slope2,
                  kb, kb2, wr_back, we_back, gsum0, dred, dspat, put_mid2):
    rows, cols = gmid2.shape[0], gmid2.shape[-1]

    def work(pair):
        firsts = [back.astype(BF16) * slope1[slot] for _, slot, back in pair]
        dred[...] += mm_nt_sum([(g1, x1[slot]) for g1, (_, slot, _) in zip(firsts, pair)])
        if not edges:
            dspat[...] += tap_terms(first1, gmid2, [row for row, _, _ in pair])
        ups = both(wr_back[1], firsts)
        for (row, slot, _), g1, up in zip(pair, firsts, ups):
            g = (up + gsum1[slot].astype(F32)).astype(BF16) * slope3[slot] * inside(mask, row, slope3.shape[1])
            gsum0[slot] = g
            put_mid2(row, slot, mm(we_back[0], g).astype(BF16) * slope2[slot])

    conv_rows(edges, rows, gmid2, g_halos, kb.at[1], kb2.at[1], True, work)


def backward_inner(mask, gmid2, first1, f_above, f_below, second_edge, gsum_edge, dexp_turn, slope1, x1, gsum1, slope3, slope2, kb, kb2, wr_back, we_back,
                   gsum0, gmid2_0, dred, dspat, dexp):
    start_sums(None, [dred])
    dspat[...] = edge_tap_terms(first1, (f_above, f_below), gmid2)
    dexp[...] = dexp_turn[...] + mm_nt_sum([(second_edge[n], gsum_edge[n]) for n in range(2)])

    def put_mid2(row, slot, value):
        gmid2_0[slot] = value

    backward_rows(False, mask, gmid2, None, first1, slope1, x1, gsum1, slope3, slope2,
                  kb, kb2, wr_back, we_back, gsum0, dred, dspat, put_mid2)


def backward_edge(mask, gmid2, above, below, slope1, x1, gsum1, slope3, slope2,
                  kb, kb2, wr_back, we_back, gmid2_inner, dred_inner,
                  gsum0, gmid2_0, dred, top, bottom):
    start_sums([dred_inner], [dred])

    def put_mid2(row, slot, value):
        (bottom if slot else top)[...] = value

    backward_rows(True, mask, gmid2, (above, below), None, slope1, x1, gsum1, slope3,
                  slope2, kb, kb2, wr_back, we_back, gsum0, dred, None, put_mid2)
    gather_rows(gmid2_0, gmid2_inner, top, bottom)


def last_rows(edges, gmid2, g_halos, first0, slope1, x, kb, kb2, gmid1, dred, dspat):
    def work(pair):
        firsts = []
        for row, slot, back in pair:
            g1 = back.astype(BF16) * slope1[slot]
            gmid1[slot] = g1
            firsts.append((g1, x[row]))
        dred[...] += mm_nt_sum(firsts)
        if not edges:
            dspat[...] += tap_terms(first0, gmid2, [row for row, _, _ in pair])

    conv_rows(edges, gmid2.shape[0], gmid2, g_halos, kb.at[0], kb2.at[0], True, work, False)


def last_inner(gmid2, first0, f_above, f_below, slope1, x, second_inner, second_edge, gsum_inner, gsum_edge, kb, kb2,
               gmid1, dred, dspat, dexp):
    start_sums(None, [dred])
    dspat[...] = edge_tap_terms(first0, (f_above, f_below), gmid2)
    dexp[...] = mm_nt(second_edge[0], gsum_edge[0]) + mm_nt(second_edge[1], gsum_edge[1])

    @pl.loop(0, second_inner.shape[0] // 2)
    def _(i):
        dexp[...] += mm_nt_sum([(second_inner[2 * i], gsum_inner[2 * i]), (second_inner[2 * i + 1], gsum_inner[2 * i + 1])])

    last_rows(False, gmid2, None, first0, slope1, x, kb, kb2, gmid1, dred, dspat)


def tap_places(mid):
    places = []
    for n in range(9):
        a, b = divmod(n, 3)
        if n < 8:
            base, at = (2 + n // 4) * mid, n % 4
            places.append((slice(a * mid, (a + 1) * mid), slice(b * mid, (b + 1) * mid),
                           slice(base, base + mid), slice(at * mid, (at + 1) * mid)))
        else:
            part = mid // 4
            for q in range(4):
                places.append((slice(a * mid + q * part, a * mid + (q + 1) * part), slice(b * mid, (b + 1) * mid),
                               slice(4 * mid, 4 * mid + part), slice(q * mid, (q + 1) * mid)))
    return places


def last_edge(gmid2, above, below, slope1, x, kb, kb2, dred_inner, dspat,
              dred1, dexp0, dexp1, dspat1, gmid1, keep, send, dred):
    start_sums([dred_inner], [dred])
    last_rows(True, gmid2, (above, below), None, slope1, x, kb, kb2, gmid1, dred, None)
    core = lax.axis_index("batch") % 2

    def pack(out, reduce_term, expand_term, spatial_term):
        mid = reduce_term.shape[0]
        out[:mid] = reduce_term[...].astype(BF16)
        out[mid : 2 * mid] = expand_term[...].astype(BF16)
        for rows_in, cols_in, rows_out, cols_out in tap_places(mid):
            out[rows_out, cols_out] = spatial_term[rows_in, cols_in].astype(BF16)

    for own in range(2):
        @pl.when(core == own)
        def _():
            blocks = ((dred, dexp0, dspat), (dred1, dexp1, dspat1))
            pack(keep, *blocks[own])
            pack(send, *blocks[1 - own])


def grad_rows(gmid1_inner, gmid1_edge, gsum_inner, gsum_edge, wr_back, out, held, sems):
    rows = held.shape[0]

    def work(at, slots, gmid1, gsum):
        for row, slot, acc in zip(at, slots, both(wr_back[0], [gmid1[slot] for slot in slots])):
            held[row] = (acc + gsum[slot].astype(F32) * 0.25).astype(BF16)
            pltpu.make_async_copy(held.at[row], out.at[row], sems.at[row]).start()

    @pl.loop(0, (rows - 2) // 2, unroll=True)
    def _(i):
        work((2 * i + 1, 2 * i + 2), (2 * i, 2 * i + 1), gmid1_inner, gsum_inner)

    work((0, rows - 1), (0, 1), gmid1_edge, gsum_edge)
    for r in range(rows):
        pltpu.make_async_copy(held.at[r], out.at[r], sems.at[r]).wait()


def finish(factor, mine, other, scale_out, g_reduce, g_spatial, g_expand):
    mid = g_reduce.shape[1]
    core = lax.axis_index("batch") % 2
    for terms, k in ((mine, core), (other, 1 - core)):
        g_reduce[k] = terms[:mid].astype(F32) * factor
        scale = jnp.where(k == 0, scale_out[0:1, :] * (factor * 0.25), scale_out[1:2, :] * (factor * 0.5))
        g_expand[k] = terms[mid : 2 * mid].astype(F32) * scale
        for rows_in, cols_in, rows_out, cols_out in tap_places(mid):
            a, b = rows_in.start // mid, cols_in.start // mid
            part = terms[rows_out, cols_out].astype(F32) * factor
            g_spatial[k, a, b, rows_in.start - a * mid : rows_in.stop - a * mid] = part


def lanes(vector, count):
    return jnp.broadcast_to(vector, (count, vector.shape[-1])).T


def twin(out, k, value):
    tall, across = value.shape
    out[k, :tall, :across] = value
    out[k, tall:, across:] = value


def start(limits, images, red_h, spa_h, exp_h, sm_h, sh_h, so_h, sho_h,
          mask, wr, b1, red, spa, exp, scale_mid, shift_mid, scale_out, shift_out, slope1, top, bottom, x, sems):
    rows, cols = images.shape[0], x.shape[-1]
    copies = [pltpu.make_async_copy(s, d, sems.at[n]) for n, (s, d) in enumerate(
        ((sm_h, scale_mid), (sh_h, shift_mid), (red_h, red), (images.at[0], x.at[0]), (images.at[rows - 1], x.at[1]),
         (spa_h, spa), (exp_h, exp), (so_h, scale_out), (sho_h, shift_out)))]
    for copy in copies:
        copy.start()
    for copy in copies[:3]:
        copy.wait()
    for row in range(rows):
        mask[row] = jnp.broadcast_to(row_mask(limits, row, cols), mask.shape[1:])
    wr[...] = (red[0].astype(F32) * (0.5 * lanes(scale_mid[0, 0:1, :], red.shape[-1]))).astype(BF16)
    b1[...] = 0.5 * lanes(shift_mid[0, 0:1, :], b1.shape[-1])
    for slot, (row, edge) in enumerate(((0, top), (rows - 1, bottom))):
        copies[3 + slot].wait()
        edge[...], slope1[slot] = reduce_part(x[slot], wr, b1, inside(mask, row, edge.shape[0]))
    for copy in copies[5:]:
        copy.wait()


def prepare(red, spa, exp, scale_mid, shift_mid, scale_out, shift_out,
            wr, kf, kf2, we, we_back, kb, kb2, wr_back, b1, b2, b3):
    mid = red.shape[1]
    for out in (kf2, kb2, we, wr_back):
        out[...] = jnp.zeros_like(out)
    for k in range(2):
        twice = 2.0 ** (2 - k)
        s1, s2 = scale_mid[k, 0:1, :], scale_mid[k, 1:2, :]
        so = scale_out[k : k + 1, :]
        r, e = red[k].astype(F32), exp[k].astype(F32)
        chans = r.shape[-1]
        if k == 1:
            wr[...] = (r * (0.5 * lanes(s1, chans))).astype(BF16)
            b1[...] = 0.5 * lanes(shift_mid[k, 0:1, :], b1.shape[-1])
        twin(wr_back, k, (r * (1.0 if k == 0 else twice)).T.astype(BF16))
        twin(we, k, (e * (0.5 * so)).T.astype(BF16))
        we_back[k] = (e * (so * (0.5 / twice)) * lanes(s2, chans)).astype(BF16)
        half = 0.5 * lanes(s1, mid)
        for a in range(3):
            for b in range(3):
                part = spa[k, a, b].astype(F32)
                ahead = (part * (0.5 * s2)).T.astype(BF16)
                back = (part * half).astype(BF16)
                for out, out2, value, at in ((kf, kf2, ahead, a), (kb, kb2, back, 2 - a)):
                    out[k, b * mid : (b + 1) * mid, at * mid : (at + 1) * mid] = value
                    for j in range(2):
                        out2[k, (3 * j + b) * mid : (3 * j + b + 1) * mid, (at + j) * mid : (at + j + 1) * mid] = value
        b2[k] = 0.5 * lanes(shift_mid[k, 1:2, :], b2.shape[-1])
        b3[k] = 0.5 * lanes(shift_out[k : k + 1, :], b3.shape[-1])


def call(kernel, outs, args, name, specs=None, out_specs=None, scratch=(), limit=VMEM_LIMIT):
    return pl.pallas_call(
        kernel,
        in_specs=specs or [VMEM] * len(args),
        out_specs=out_specs or [VMEM] * len(outs),
        out_shape=[jax.ShapeDtypeStruct(s, d) for s, d in outs],
        scratch_shapes=list(scratch),
        compiler_params=pltpu.CompilerParams(vmem_limit_bytes=limit),
        name=name,
    )(*args)


def exchange(top, bottom):
    count = lax.axis_size("space")
    above = lax.ppermute(bottom, "space", [(i, (i + 1) % count) for i in range(count)])
    below = lax.ppermute(top, "space", [((i + 1) % count, i) for i in range(count)])
    return above, below


def swaps():
    def flat(z, x, core, y):
        return ((z % 2 * 4 + x) * 2 + core) * 8 + y * 2 + z // 2

    places = [(z, x, core, y) for z in range(4) for x in range(4) for core in range(2) for y in range(4)]
    orders = ((1, 3, 0), (3, 0, 1))
    steps = []
    for turn in range(3):
        for mirror in (1, 3):
            steps.append([(flat(*at), flat(*(c ^ mirror if n == orders[at[2]][turn] else c for n, c in enumerate(at))))
                          for at in places])
    return steps


def all_sum(keep, send, beside):
    cores = [(i, i ^ 1) for i in range(lax.axis_size("batch"))]
    value = keep.astype(F32) + lax.ppermute(send, "batch", cores).astype(F32)
    for step, pairs in enumerate(swaps()):
        if step == BESIDE:
            value, beside = lax.optimization_barrier((value, beside))
        value = value + lax.ppermute(value.astype(BF16), ("batch", "space"), pairs).astype(F32)
    mine = value.astype(BF16)
    return mine, lax.ppermute(mine, "batch", cores), beside


def body(images, heights, widths, conv_reduce, conv_spatial, conv_expand, scale_mid, shift_mid,
         scale_out, shift_out, cotangent):
    _, rows, chans, cols = images.shape
    mid = conv_reduce.shape[-1]
    cot = cotangent[0]
    wide_w, tall_w = ((mid, chans), BF16), ((2 * chans, 2 * mid), BF16)
    single, double = ((3 * mid, 3 * mid), BF16), ((6 * mid, 4 * mid), BF16)
    bias = ((mid, 128), F32)
    made = [single, double, tall_w, wide_w, single, double, tall_w]
    params = [conv_reduce.swapaxes(1, 2), conv_spatial, conv_expand, scale_mid, shift_mid, scale_out, shift_out]

    def small(count):
        return (count, mid, cols), BF16

    def large(count):
        return (count, chans, cols), BF16

    inner, edge = rows - 2, 2
    row = ((mid, cols), BF16)
    acc_c = ((mid, chans), F32)
    acc_s = ((3 * mid, 3 * mid), F32)

    ids = lax.axis_index("space") * rows + lax.broadcasted_iota(jnp.int32, (rows, 128), 0)
    limits = jnp.where(ids < heights, widths, 0)
    strip = pltpu.with_memory_space_constraint(images[0], pltpu.HBM)
    mask, wr_0, b1_0, *held, slope1_0e, top, bottom = call(
        start, [((rows, 16, cols), BF16), wide_w, bias] + [(p.shape, p.dtype) for p in params] + [small(edge), row, row],
        [limits, strip] + [pltpu.with_memory_space_constraint(p, pltpu.HBM) for p in params],
        "start", [VMEM] + [HBM] * 8, scratch=[pltpu.VMEM(*large(edge)), pltpu.SemaphoreType.DMA((2 + len(params),))])
    f0a, f0b = exchange(top, bottom)
    hw = [mask]
    first0, slope1_0i, second0i, slope2_0i, slope3_0i, x1i, slope1_1i, first1i, *weights = call(
        forward_inner, [small(rows)] + [small(inner)] * 3 + [large(inner)] * 2 + [small(inner)] * 2
        + [wide_w] + [((2,) + s, d) for s, d in made] + [bias] + [((2,) + s, d) for s, d in (bias, ((chans, 128), F32))],
        hw + [images[0], top, bottom, wr_0, b1_0] + held, "forward_inner")
    wr, kf, kf2, we, we_back, kb, kb2, wr_back, b1, b2, b3 = weights
    second0e, slope2_0e, slope3_0e, x1e, slope1_1e, first1, top, bottom = call(
        forward_edge, [small(edge)] * 2 + [large(edge)] * 2 + [small(edge), small(rows), row, row],
        hw + [images[0], first0, f0a, f0b, first1i, kf, kf2, b2, we, b3, wr, b1], "forward_edge")
    f1a, f1b = exchange(top, bottom)
    turn = [kf, kf2, b2, we, b3, we_back]
    gsum1i, gmid2_1i, dexp1 = call(
        turn_inner, [large(inner), small(inner), acc_c], hw + [first1, x1i, cot] + turn, "turn_inner")
    gsum1e, gmid2_1, second1e, top, bottom = call(
        turn_edge, [large(edge), small(rows), small(edge), row, row],
        hw + [first1, f1a, f1b, x1e, cot] + turn + [gmid2_1i], "turn_edge")
    g1a, g1b = exchange(top, bottom)
    back = [kb, kb2, wr_back, we_back]
    gsum0i, gmid2_0i, dred1, dspat1, dexp1 = call(
        backward_inner, [large(inner), small(inner), acc_c, acc_s, acc_c],
        hw + [gmid2_1, first1, f1a, f1b, second1e, gsum1e, dexp1, slope1_1i, x1i, gsum1i, slope3_0i, slope2_0i] + back, "backward_inner")
    gsum0e, gmid2_0, dred1, top, bottom = call(
        backward_edge, [large(edge), small(rows), acc_c, row, row],
        hw + [gmid2_1, g1a, g1b, slope1_1e, x1e, gsum1e, slope3_0e, slope2_0e] + back + [gmid2_0i, dred1], "backward_edge")
    g0a, g0b = exchange(top, bottom)
    gmid1_0i, dred0, dspat0, dexp0 = call(
        last_inner, [small(inner), acc_c, acc_s, acc_c],
        [gmid2_0, first0, f0a, f0b, slope1_0i, images[0], second0i, second0e, gsum0i, gsum0e, kb, kb2], "last_inner")
    gmid1_0e, keep, send = call(
        last_edge, [small(edge), ((4 * mid + mid // 4, chans), BF16), ((4 * mid + mid // 4, chans), BF16)],
        [gmid2_0, g0a, g0b, slope1_0e, images[0], kb, kb2, dred0, dspat0, dred1, dexp0, dexp1, dspat1],
        "last_edge", scratch=[pltpu.VMEM(*acc_c)])
    (grad,) = call(
        grad_rows, [large(rows)], [gmid1_0i, gmid1_0e, gsum0i, gsum0e, wr_back], "grad_images", out_specs=[HBM],
        scratch=[pltpu.VMEM(*large(rows)), pltpu.SemaphoreType.DMA((rows,))])
    mine, other, grad = all_sum(keep, send, grad)
    factor = 1.0 / math.sqrt(lax.axis_size("batch") * rows * lax.axis_size("space") * cols)
    g_reduce, g_spatial, g_expand = call(
        functools.partial(finish, factor),
        [((2, mid, chans), F32), (conv_spatial.shape, F32), ((2, mid, chans), F32)], [mine, other, scale_out], "finish")
    return grad[None], g_reduce.swapaxes(1, 2), g_spatial, g_expand


def solution(mesh):
    strips = P("batch", "space", None, None)
    placed = (strips, P("batch"), P("batch")) + (P(),) * 7 + (strips,)
    return jax.shard_map(
        body, mesh=mesh, in_specs=placed, out_specs=(strips, P(), P(), P()), check_vma=False)
```

time: 99 us -> 96.8 us (0.978)
  blocking collectives: 24.3 us -> 0 us
  waiting for transfers between devices: 10.5 us -> 30.7 us
  starting transfers between devices: 28.1 us -> 30.4 us
  Pallas kernels: 33.1 us -> 31.8 us
    all_to_all x2 -> x0, blocking collectives: 24.3 us -> none  [the longest x1 13.2 us: all_sum(): lax.all_to_all(terms.reshape(n, tall // n, across), 'batch', 0, 0, tiled=...]
    ppermute x3 -> x8, waiting for transfers between devices: 7.71 us -> 28.1 us  [the longest x6 25.4 us: all_sum(): lax.ppermute(value.astype(BF16), ('batch', 'space'), pairs).astype(F32)]
    ppermute x3 -> x8, starting transfers between devices: 4.56 us -> 6.78 us  [the longest x6 6.61 us: all_sum(): lax.ppermute(value.astype(BF16), ('batch', 'space'), pairs).astype(F32)]
    pallas_call x11, Pallas kernels: 33.1 us -> 31.8 us  [call(): pl.pallas_call(kernel, in_specs=specs or [VMEM] * len(args), out_specs=ou...]
  transfers between devices with their start and end apart: 11 -> 16, of which waited for: 3 -> 9; matrix products, arithmetic and copies ran while one was open for 0% -> 0% of each run, Pallas kernels for 23% -> 25%
where the time goes in v2:
time: 96.8 us; the launch traced here: 95.6 us
  Pallas kernels  31.8 us (33%)
  waiting for transfers between devices  30.7 us (32%)
  starting transfers between devices  30.4 us (31%)
  between operations  2.17 us (2%)
    pallas_call x11, Pallas kernels, call(): pl.pallas_call(kernel, in_specs=specs or [VMEM] * len(args), out_specs=ou...  31.8 us
    ppermute x6, waiting for transfers between devices, all_sum(): lax.ppermute(value.astype(BF16), ('batch', 'space'), pairs).astype(F32)  25.4 us
    ppermute x4, starting transfers between devices, exchange(): lax.ppermute(top, 'space', [((i + 1) % count, i) for i in range(count)])  23.4 us
    ppermute x6, starting transfers between devices, all_sum(): lax.ppermute(value.astype(BF16), ('batch', 'space'), pairs).astype(F32)  6.61 us
    ppermute x4, waiting for transfers between devices, exchange(): lax.ppermute(bottom, 'space', [(i, (i + 1) % count) for i in range(count)])  2.65 us
  transfers between devices with their start and end apart: 16, of which 9 were waited for; matrix products, arithmetic and copies ran while one was open for 0% of the time, Pallas kernels for 25%

profile of v2, /device:TPU:0, one launch (start us, length us, event | category | flops | bytes accessed | tf_op | source)
XLA Modules:
  0.0 95.6 jit_solution(16470777116371355308)
XLA Ops:
  2.0 1.9 %start.1 = (bf16[8,16,1024]{2,1,0:T(8,128)(2,1)S(1)}, bf16[64,256]{1,0:T(8,128)(2,1)S(1)}, f32[64,128]{1,0:T(8,128)S(1)}, bf16[2,64,256]{2,1,0:T(8,128)(2,1)S(1)...) custom-call(s32[8,128]{1,0:T(8,128)S(1)} %iota.7.limits, ...), custom_call_target="tpu_custom_call" | custom-call | tf_op jit(solution)/shard_map/start/pallas_call | solution.py:441
  3.9 6.5 %collective-permute-start.1 = (bf16[64,1024]{1,0:T(8,128)(2,1)S(1)}, bf16[64,1024]{1,0:T(8,128)(2,1)S(1)}, u32[]{:S(2)}, u32[]{:S(2)}) collective-permute-start(bf16[64,1024]{1,0:T(8,128)(2,1)S(1)} %get-tuple-element.75.top), channel_id=1, source_target_pairs={{1,0},{2,1},{3,2},{4,3},{5,4},{6,5},{7,6},{0,7},{9,8},{10,9},{11,1... | collective-permute-start | bytes 393224 | tf_op jit(solution)/shard_map/ppermute | solution.py:455
  10.4 5.9 %forward_inner.1 = (bf16[8,64,1024]{2,1,0:T(8,128)(2,1)S(1)}, bf16[6,64,1024]{2,1,0:T(8,128)(2,1)S(1)}, bf16[6,64,1024]{2,1,0:T(8,128)(2,1)S(1)}, bf16[6,64,1024...) custom-call(bf16[8,16,1024]{2,1,0:T(8,128)(2,1)S(1)} %get-tuple-elem, ...), custom_call_target="tpu_custom_call" | custom-call | tf_op jit(solution)/shard_map/forward_inner/pallas_call | solution.py:441
  16.3 2.6 %collective-permute-done.above.f_above = bf16[64,1024]{1,0:T(8,128)(2,1)S(1)} collective-permute-done((bf16[64,1024]{1,0:T(8,128)(2,1)S(1)}, bf16[64,1024]{1,0:T(8,128)(2,1)S(1)}, u32[]{:S(2)}, u32[]{:S(2)}) %collective-permute-start) | collective-permute-done | bytes 131104 | tf_op jit(solution)/shard_map/ppermute | solution.py:454
  18.9 1.6 %forward_edge.1 = (bf16[2,64,1024]{2,1,0:T(8,128)(2,1)S(1)}, bf16[2,64,1024]{2,1,0:T(8,128)(2,1)S(1)}, bf16[2,256,1024]{2,1,0:T(8,128)(2,1)S(1)}, bf16[2,256,102...) custom-call(bf16[8,16,1024]{2,1,0:T(8,128)(2,1)S(1)} %get-tuple-elem, ...), custom_call_target="tpu_custom_call" | custom-call | tf_op jit(solution)/shard_map/forward_edge/pallas_call | solution.py:441
  20.6 5.6 %collective-permute-start.3 = (bf16[64,1024]{1,0:T(8,128)(2,1)S(1)}, bf16[64,1024]{1,0:T(8,128)(2,1)S(1)}, u32[]{:S(2)}, u32[]{:S(2)}) collective-permute-start(bf16[64,1024]{1,0:T(8,128)(2,1)S(1)} %get-tuple-element.97), channel_id=1, source_target_pairs={{1,0},{2,1},{3,2},{4,3},{5,4},{6,5},{7,6},{0,7},{9,8},{10,9},{11,1... | collective-permute-start | bytes 393224 | tf_op jit(solution)/shard_map/ppermute | solution.py:455
  26.3 5.2 %turn_inner.1 = (bf16[6,256,1024]{2,1,0:T(8,128)(2,1)S(1)}, bf16[6,64,1024]{2,1,0:T(8,128)(2,1)S(1)}, f32[64,256]{1,0:T(8,128)S(1)}) custom-call(bf16[8,16,1024]{2,1,0:T(8,128)(2,1)S(1)} %get-tuple-element.74.mask, bf16[8,64,1024]{2,1,0:T(8,128)(2,1)S(1)} %get-tuple-element.95.first1, bf16[6,256,1024]{2,1,0:T(8,128)(2,1)S(1)} %get-tuple-element.100.x1, ...), custom_call_target="tpu_custom_call" | custom-call | tf_op jit(solution)/shard_map/turn_inner/pallas_call | solution.py:441
  31.5 1.6 %turn_edge.1 = (bf16[2,256,1024]{2,1,0:T(8,128)(2,1)S(1)}, bf16[8,64,1024]{2,1,0:T(8,128)(2,1)S(1)}, bf16[2,64,1024]{2,1,0:T(8,128)(2,1)S(1)}, bf16[64,1024]{1,0:T(8,128)(2,1)S(1)}, bf16[64,1024]{1,0:T(8,128)(2,1)S(1)}) custom-call(bf16[8,16,1024]{2,1,0:T(8,128)(2,1)S(1)} %get-tuple-element.74.mask, bf16[8,64,1024]{2,1,0:T(8,128)(2,1)S(1)} %get-tuple-element.95.first1, ...), custom_call_target="tpu_custom_call" | custom-call | tf_op jit(solution)/shard_map/turn_edge/pallas_call | solution.py:441
  33.2 5.6 %collective-permute-start.5 = (bf16[64,1024]{1,0:T(8,128)(2,1)S(1)}, bf16[64,1024]{1,0:T(8,128)(2,1)S(1)}, u32[]{:S(2)}, u32[]{:S(2)}) collective-permute-start(bf16[64,1024]{1,0:T(8,128)(2,1)S(1)} %get-tuple-element.104), channel_id=1, source_target_pairs={{1,0},{2,1},{3,2},{4,3},{5,4},{6,5},{7,6},{0,7},{9,8},{10,9},{11,1... | collective-permute-start | bytes 393224 | tf_op jit(solution)/shard_map/ppermute | solution.py:455
  38.8 4.8 %backward_inner.1 = (bf16[6,256,1024]{2,1,0:T(8,128)(2,1)S(1)}, bf16[6,64,1024]{2,1,0:T(8,128)(2,1)S(1)}, f32[64,256]{1,0:T(8,128)S(1)}, f32[192,192]{1,0:T(8,128)S(1)}, f32[64,256]{1,0:T(8,128)S(1)}) custom-call(bf16[8,16,1024]{2,1,0:T(8,128)(2,1)S(1)} %get-tuple-element.74.mask, bf16[8,64,1024]{2,1,0:T(8,128)(2,1)S(1)} %get-tuple-element.102.gmid2, ...), custom_call_target="tpu_custom_call" | custom-call | tf_op jit(solution)/shard_map/backward_inner/pallas_call | solution.py:441
  43.7 1.3 %backward_edge.1 = (bf16[2,256,1024]{2,1,0:T(8,128)(2,1)S(1)}, bf16[8,64,1024]{2,1,0:T(8,128)(2,1)S(1)}, f32[64,256]{1,0:T(8,128)S(1)}, bf16[64,1024]{1,0:T(8,128)(2,1)S(1)}, bf16[64,1024]{1,0:T(8,128)(2,1)S(1)}) custom-call(bf16[8,16,1024]{2,1,0:T(8,128)(2,1)S(1)} %get-tuple-element.74.mask, bf16[8,64,1024]{2,1,0:T(8,128)(2,1)S(1)} %get-tuple-element.102.gmid2, ...), custom_call_target="tpu_custom_call" | custom-call | tf_op jit(solution)/shard_map/backward_edge/pallas_call | solution.py:441
  45.1 5.6 %collective-permute-start.7 = (bf16[64,1024]{1,0:T(8,128)(2,1)S(1)}, bf16[64,1024]{1,0:T(8,128)(2,1)S(1)}, u32[]{:S(2)}, u32[]{:S(2)}) collective-permute-start(bf16[64,1024]{1,0:T(8,128)(2,1)S(1)} %get-tuple-element.122), channel_id=1, source_target_pairs={{1,0},{2,1},{3,2},{4,3},{5,4},{6,5},{7,6},{0,7},{9,8},{10,9},{11,1... | collective-permute-start | bytes 393224 | tf_op jit(solution)/shard_map/ppermute | solution.py:455
  50.7 5.2 %last_inner.1 = (bf16[6,64,1024]{2,1,0:T(8,128)(2,1)S(1)}, f32[64,256]{1,0:T(8,128)S(1)}, f32[192,192]{1,0:T(8,128)S(1)}, f32[64,256]{1,0:T(8,128)S(1)}) custom-call(bf16[8,64,1024]{2,1,0:T(8,128)(2,1)S(1)} %get-tuple-element.120.gmid2, bf16[8,64,1024]{2,1,0:T(8,128)(2,1)S(1)} %get-tuple-element.86.first0, ...), custom_call_target="tpu_custom_call" | custom-call | tf_op jit(solution)/shard_map/last_inner/pallas_call | solution.py:441
  56.9 1.3 %collective-permute-done.8 = bf16[272,256]{1,0:T(8,128)(2,1)S(1)} collective-permute-done((bf16[272,256]{1,0:T(8,128)(2,1)S(1)}, bf16[272,256]{1,0:T(8,128)(2,1)S(1)}, u32[]{:S(2)}, u32[]{:S(2)}) %collective-permute-start.8) | collective-permute-done | bytes 139296 | tf_op jit(solution)/shard_map/ppermute | solution.py:475
  58.3 1.6 %collective-permute-start.9 = (bf16[272,256]{1,0:T(8,128)(2,1)S(1)}, bf16[272,256]{1,0:T(8,128)(2,1)S(1)}, u32[]{:S(2)}, u32[]{:S(2)}) collective-permute-start(bf16[272,256]{1,0:T(8,128)(2,1)S(1)} %fusion), channel_id=1, source_target_pairs={{0,16},{2,18},{4,20},{6,22},{8,10},{10,8},{12,14},{14,12},{16,0},{... | collective-permute-start | bytes 417800 | tf_op jit(solution)/shard_map/ppermute | solution.py:479
  59.9 3.6 %collective-permute-done.9 = bf16[272,256]{1,0:T(8,128)(2,1)S(1)} collective-permute-done((bf16[272,256]{1,0:T(8,128)(2,1)S(1)}, bf16[272,256]{1,0:T(8,128)(2,1)S(1)}, u32[]{:S(2)}, u32[]{:S(2)}) %collective-permute-start.9) | collective-permute-done | bytes 139296 | tf_op jit(solution)/shard_map/ppermute | solution.py:479
  63.5 2.8 %collective-permute-start.10 = (bf16[272,256]{1,0:T(8,128)(2,1)S(1)}, bf16[272,256]{1,0:T(8,128)(2,1)S(1)}, u32[]{:S(2)}, u32[]{:S(2)}) collective-permute-start(bf16[272,256]{1,0:T(8,128)(2,1)S(1)} %fusion.3), channel_id=1, source_target_pairs={{0,48},{2,50},{4,52},{6,54},{8,14},{10,12},{12,10},{14,8},{16,32},... | collective-permute-start | bytes 417800 | tf_op jit(solution)/shard_map/ppermute | solution.py:479
  66.4 2.4 %grad_images.1 = bf16[8,256,1024]{2,1,0:T(8,128)(2,1)} custom-call(bf16[6,64,1024]{2,1,0:T(8,128)(2,1)S(1)} %get-tuple-element.137.gmid1_inner, bf16[2,64,1024]{2,1,0:T(8,128)(2,1)S(1)} %get-tuple-element.138.gmid1_edge, bf16[6,256,1024]{2,1,0:T(8,128)(2,1)S(1)} %get-tuple-element.127.gsum_inner, bf16[2,256,1024]{2,1,0:T(8,128)(2,1)S(1)} %get-tuple-element.128.gsum_edge, ...), custom_call_target="tpu_custom_call" | custom-call | tf_op jit(solution)/shard_map/grad_images/pallas_call | solution.py:441
  70.1 5.0 %collective-permute-done.11 = bf16[272,256]{1,0:T(8,128)(2,1)S(1)} collective-permute-done((bf16[272,256]{1,0:T(8,128)(2,1)S(1)}, bf16[272,256]{1,0:T(8,128)(2,1)S(1)}, u32[]{:S(2)}, u32[]{:S(2)}) %collective-permute-start.11) | collective-permute-done | bytes 139296 | tf_op jit(solution)/shard_map/ppermute | solution.py:479
  75.2 6.3 %collective-permute-done.12 = bf16[272,256]{1,0:T(8,128)(2,1)S(1)} collective-permute-done((bf16[272,256]{1,0:T(8,128)(2,1)S(1)}, bf16[272,256]{1,0:T(8,128)(2,1)S(1)}, u32[]{:S(2)}, u32[]{:S(2)}) %collective-permute-start.12) | collective-permute-done | bytes 139296 | tf_op jit(solution)/shard_map/ppermute | solution.py:479
  81.5 1.1 %collective-permute-start.13 = (bf16[272,256]{1,0:T(8,128)(2,1)S(1)}, bf16[272,256]{1,0:T(8,128)(2,1)S(1)}, u32[]{:S(2)}, u32[]{:S(2)}) collective-permute-start(bf16[272,256]{1,0:T(8,128)(2,1)S(1)} %fusion.4), channel_id=1, source_target_pairs={{0,64},{2,66},{4,68},{6,70},{8,24},{10,26},{12,28},{14,30},{16,80}... | collective-permute-start | bytes 417800 | tf_op jit(solution)/shard_map/ppermute | solution.py:479
  82.6 4.0 %collective-permute-done.13 = bf16[272,256]{1,0:T(8,128)(2,1)S(1)} collective-permute-done((bf16[272,256]{1,0:T(8,128)(2,1)S(1)}, bf16[272,256]{1,0:T(8,128)(2,1)S(1)}, u32[]{:S(2)}, u32[]{:S(2)}) %collective-permute-start.13) | collective-permute-done | bytes 139296 | tf_op jit(solution)/shard_map/ppermute | solution.py:479
  87.7 5.4 %collective-permute-done.14 = bf16[272,256]{1,0:T(8,128)(2,1)S(1)} collective-permute-done((bf16[272,256]{1,0:T(8,128)(2,1)S(1)}, bf16[272,256]{1,0:T(8,128)(2,1)S(1)}, u32[]{:S(2)}, u32[]{:S(2)}) %collective-permute-start.14) | collective-permute-done | bytes 139296 | tf_op jit(solution)/shard_map/ppermute | solution.py:479
  93.3 1.3 %collective-permute-done.15.other = bf16[272,256]{1,0:T(8,128)(2,1)S(1)} collective-permute-done((bf16[272,256]{1,0:T(8,128)(2,1)S(1)}, bf16[272,256]{1,0:T(8,128)(2,1)S(1)}, u32[]{:S(2)}, u32[]{:S(2)}) %collective-permute-start.15) | collective-permute-done | bytes 139296 | tf_op jit(solution)/shard_map/ppermute | solution.py:481
  (35 shorter events, 5.0 us)
Async XLA Ops:
  1.9 8.4 %copy-start = (bf16[1,8,256,1024]{3,2,1,0:T(8,128)(2,1)S(1)}, bf16[1,8,256,1024]{3,2,1,0:T(8,128)(2,1)}, u32[]{:S(2)}) copy-start(bf16[1,8,256,1024]{3,2,1,0:T(8,128)(2,1)} %param.11) | copy-start | bytes 12582916
  3.9 12.4 %collective-permute-start.1 = (bf16[64,1024]{1,0:T(8,128)(2,1)S(1)}, bf16[64,1024]{1,0:T(8,128)(2,1)S(1)}, u32[]{:S(2)}, u32[]{:S(2)}) collective-permute-start(bf16[64,1024]{1,0:T(8,128)(2,1)S(1)} %get-tuple-element.75.top), channel_id=1, source_target_pairs={{1,0},{2,1},{3,2},{4,3},{5,4},{6,5},{7,6},{0,7},{9,8},{10,9},{11,1... | collective-permute-start | bytes 393224 | tf_op jit(solution)/shard_map/ppermute | solution.py:455
  10.4 8.6 %collective-permute-start = (bf16[64,1024]{1,0:T(8,128)(2,1)S(1)}, bf16[64,1024]{1,0:T(8,128)(2,1)S(1)}, u32[]{:S(2)}, u32[]{:S(2)}) collective-permute-start(bf16[64,1024]{1,0:T(8,128)(2,1)S(1)} %get-tuple-element.76.bottom), channel_id=1, source_target_pairs={{0,1},{1,2},{2,3},{3,4},{4,5},{5,6},{6,7},{7,0},{8,9},{9,10},{10,1... | collective-permute-start | bytes 393224 | tf_op jit(solution)/shard_map/ppermute | solution.py:454
  18.9 7.3 %copy-start.1 = (bf16[1,8,256,1024]{3,2,1,0:T(8,128)(2,1)S(1)}, bf16[1,8,256,1024]{3,2,1,0:T(8,128)(2,1)}, u32[]{:S(2)}) copy-start(bf16[1,8,256,1024]{3,2,1,0:T(8,128)(2,1)} %param.21) | copy-start | bytes 12582916
  20.6 10.9 %collective-permute-start.2 = (bf16[64,1024]{1,0:T(8,128)(2,1)S(1)}, bf16[64,1024]{1,0:T(8,128)(2,1)S(1)}, u32[]{:S(2)}, u32[]{:S(2)}) collective-permute-start(bf16[64,1024]{1,0:T(8,128)(2,1)S(1)} %get-tuple-element.96), channel_id=1, source_target_pairs={{0,1},{1,2},{2,3},{3,4},{4,5},{5,6},{6,7},{7,0},{8,9},{9,10},{10,1... | collective-permute-start | bytes 393224 | tf_op jit(solution)/shard_map/ppermute | solution.py:454
  20.6 10.8 %collective-permute-start.3 = (bf16[64,1024]{1,0:T(8,128)(2,1)S(1)}, bf16[64,1024]{1,0:T(8,128)(2,1)S(1)}, u32[]{:S(2)}, u32[]{:S(2)}) collective-permute-start(bf16[64,1024]{1,0:T(8,128)(2,1)S(1)} %get-tuple-element.97), channel_id=1, source_target_pairs={{1,0},{2,1},{3,2},{4,3},{5,4},{6,5},{7,6},{0,7},{9,8},{10,9},{11,1... | collective-permute-start | bytes 393224 | tf_op jit(solution)/shard_map/ppermute | solution.py:455
  33.1 10.6 %collective-permute-start.4 = (bf16[64,1024]{1,0:T(8,128)(2,1)S(1)}, bf16[64,1024]{1,0:T(8,128)(2,1)S(1)}, u32[]{:S(2)}, u32[]{:S(2)}) collective-permute-start(bf16[64,1024]{1,0:T(8,128)(2,1)S(1)} %get-tuple-element.103), channel_id=1, source_target_pairs={{0,1},{1,2},{2,3},{3,4},{4,5},{5,6},{6,7},{7,0},{8,9},{9,10},{10,1... | collective-permute-start | bytes 393224 | tf_op jit(solution)/shard_map/ppermute | solution.py:454
  33.2 10.5 %collective-permute-start.5 = (bf16[64,1024]{1,0:T(8,128)(2,1)S(1)}, bf16[64,1024]{1,0:T(8,128)(2,1)S(1)}, u32[]{:S(2)}, u32[]{:S(2)}) collective-permute-start(bf16[64,1024]{1,0:T(8,128)(2,1)S(1)} %get-tuple-element.104), channel_id=1, source_target_pairs={{1,0},{2,1},{3,2},{4,3},{5,4},{6,5},{7,6},{0,7},{9,8},{10,9},{11,1... | collective-permute-start | bytes 393224 | tf_op jit(solution)/shard_map/ppermute | solution.py:455
  45.0 10.9 %collective-permute-start.6 = (bf16[64,1024]{1,0:T(8,128)(2,1)S(1)}, bf16[64,1024]{1,0:T(8,128)(2,1)S(1)}, u32[]{:S(2)}, u32[]{:S(2)}) collective-permute-start(bf16[64,1024]{1,0:T(8,128)(2,1)S(1)} %get-tuple-element.121), channel_id=1, source_target_pairs={{0,1},{1,2},{2,3},{3,4},{4,5},{5,6},{6,7},{7,0},{8,9},{9,10},{10,1... | collective-permute-start | bytes 393224 | tf_op jit(solution)/shard_map/ppermute | solution.py:454
  45.1 10.8 %collective-permute-start.7 = (bf16[64,1024]{1,0:T(8,128)(2,1)S(1)}, bf16[64,1024]{1,0:T(8,128)(2,1)S(1)}, u32[]{:S(2)}, u32[]{:S(2)}) collective-permute-start(bf16[64,1024]{1,0:T(8,128)(2,1)S(1)} %get-tuple-element.122), channel_id=1, source_target_pairs={{1,0},{2,1},{3,2},{4,3},{5,4},{6,5},{7,6},{0,7},{9,8},{10,9},{11,1... | collective-permute-start | bytes 393224 | tf_op jit(solution)/shard_map/ppermute | solution.py:455
  56.8 1.4 %collective-permute-start.8 = (bf16[272,256]{1,0:T(8,128)(2,1)S(1)}, bf16[272,256]{1,0:T(8,128)(2,1)S(1)}, u32[]{:S(2)}, u32[]{:S(2)}) collective-permute-start(bf16[272,256]{1,0:T(8,128)(2,1)S(1)} %get-tuple-element.136), channel_id=1, source_target_pairs={{0,8},{8,0},{16,24},{24,16},{32,40},{40,32},{48,56},{56,48},{64,72... | collective-permute-start | bytes 417800 | tf_op jit(solution)/shard_map/ppermute | solution.py:475
  58.3 5.1 %collective-permute-start.9 = (bf16[272,256]{1,0:T(8,128)(2,1)S(1)}, bf16[272,256]{1,0:T(8,128)(2,1)S(1)}, u32[]{:S(2)}, u32[]{:S(2)}) collective-permute-start(bf16[272,256]{1,0:T(8,128)(2,1)S(1)} %fusion), channel_id=1, source_target_pairs={{0,16},{2,18},{4,20},{6,22},{8,10},{10,8},{12,14},{14,12},{16,0},{... | collective-permute-start | bytes 417800 | tf_op jit(solution)/shard_map/ppermute | solution.py:479
  63.5 6.3 %collective-permute-start.10 = (bf16[272,256]{1,0:T(8,128)(2,1)S(1)}, bf16[272,256]{1,0:T(8,128)(2,1)S(1)}, u32[]{:S(2)}, u32[]{:S(2)}) collective-permute-start(bf16[272,256]{1,0:T(8,128)(2,1)S(1)} %fusion.3), channel_id=1, source_target_pairs={{0,48},{2,50},{4,52},{6,54},{8,14},{10,12},{12,10},{14,8},{16,32},... | collective-permute-start | bytes 417800 | tf_op jit(solution)/shard_map/ppermute | solution.py:479
  68.8 25.8 %copy-start.2 = (f32[2,256]{1,0:T(2,128)S(1)}, f32[2,256]{1,0:T(2,128)}, u32[]{:S(2)}) copy-start(f32[2,256]{1,0:T(2,128)} %scale_out.1) | copy-start | bytes 6148
  70.0 5.1 %collective-permute-start.11 = (bf16[272,256]{1,0:T(8,128)(2,1)S(1)}, bf16[272,256]{1,0:T(8,128)(2,1)S(1)}, u32[]{:S(2)}, u32[]{:S(2)}) collective-permute-start(bf16[272,256]{1,0:T(8,128)(2,1)S(1)} %convert_element_type.51), channel_id=1, source_target_pairs={{0,2},{2,0},{4,6},{6,4},{8,72},{10,74},{12,76},{14,78},{16,18},{18... | collective-permute-start | bytes 417800 | tf_op jit(solution)/shard_map/ppermute | solution.py:479
  75.1 6.3 %collective-permute-start.12 = (bf16[272,256]{1,0:T(8,128)(2,1)S(1)}, bf16[272,256]{1,0:T(8,128)(2,1)S(1)}, u32[]{:S(2)}, u32[]{:S(2)}) collective-permute-start(bf16[272,256]{1,0:T(8,128)(2,1)S(1)} %fusion.1), channel_id=1, source_target_pairs={{0,6},{2,4},{4,2},{6,0},{8,73},{10,75},{12,77},{14,79},{16,22},{18... | collective-permute-start | bytes 417800 | tf_op jit(solution)/shard_map/ppermute | solution.py:479
  81.5 5.1 %collective-permute-start.13 = (bf16[272,256]{1,0:T(8,128)(2,1)S(1)}, bf16[272,256]{1,0:T(8,128)(2,1)S(1)}, u32[]{:S(2)}, u32[]{:S(2)}) collective-permute-start(bf16[272,256]{1,0:T(8,128)(2,1)S(1)} %fusion.4), channel_id=1, source_target_pairs={{0,64},{2,66},{4,68},{6,70},{8,24},{10,26},{12,28},{14,30},{16,80}... | collective-permute-start | bytes 417800 | tf_op jit(solution)/shard_map/ppermute | solution.py:479
  86.7 6.3 %collective-permute-start.14 = (bf16[272,256]{1,0:T(8,128)(2,1)S(1)}, bf16[272,256]{1,0:T(8,128)(2,1)S(1)}, u32[]{:S(2)}, u32[]{:S(2)}) collective-permute-start(bf16[272,256]{1,0:T(8,128)(2,1)S(1)} %fusion.2), channel_id=1, source_target_pairs={{0,65},{2,67},{4,69},{6,71},{8,56},{10,58},{12,60},{14,62},{16,81}... | collective-permute-start | bytes 417800 | tf_op jit(solution)/shard_map/ppermute | solution.py:479
  93.2 1.4 %collective-permute-start.15 = (bf16[272,256]{1,0:T(8,128)(2,1)S(1)}, bf16[272,256]{1,0:T(8,128)(2,1)S(1)}, u32[]{:S(2)}, u32[]{:S(2)}) collective-permute-start(bf16[272,256]{1,0:T(8,128)(2,1)S(1)} %add_convert_fusion.mine), channel_id=1, source_target_pairs={{0,8},{8,0},{16,24},{24,16},{32,40},{40,32},{48,56},{56,48},{64,72... | collective-permute-start | bytes 417800 | tf_op jit(solution)/shard_map/ppermute | solution.py:481

commit v3 on v2

--- a/solution.py
+++ b/solution.py
@@ -11,7 +11,7 @@
 F32 = jnp.float32
 BF16 = jnp.bfloat16
 VMEM_LIMIT = 12 * 1024 * 1024
-BESIDE = 2
+BESIDE = 1
 VMEM = pl.BlockSpec(memory_space=pltpu.VMEM)
 HBM = pl.BlockSpec(memory_space=pltpu.HBM)
 
@@ -464,19 +464,20 @@
     orders = ((1, 3, 0), (3, 0, 1))
     steps = []
     for turn in range(3):
-        for mirror in (1, 3):
-            steps.append([(flat(*at), flat(*(c ^ mirror if n == orders[at[2]][turn] else c for n, c in enumerate(at))))
-                          for at in places])
+        steps.append([[(flat(*at), flat(*(c ^ mirror if n == orders[at[2]][turn] else c for n, c in enumerate(at))))
+                       for at in places] for mirror in (2, 1, 3)])
     return steps
 
 
 def all_sum(keep, send, beside):
     cores = [(i, i ^ 1) for i in range(lax.axis_size("batch"))]
     value = keep.astype(F32) + lax.ppermute(send, "batch", cores).astype(F32)
-    for step, pairs in enumerate(swaps()):
+    for step, ring in enumerate(swaps()):
         if step == BESIDE:
             value, beside = lax.optimization_barrier((value, beside))
-        value = value + lax.ppermute(value.astype(BF16), ("batch", "space"), pairs).astype(F32)
+        rounded = value.astype(BF16)
+        for got in [lax.ppermute(rounded, ("batch", "space"), pairs) for pairs in ring]:
+            value = value + got.astype(F32)
     mine = value.astype(BF16)
     return mine, lax.ppermute(mine, "batch", cores), beside
 

time: 96.8 us -> 90.5 us (0.935)
  waiting for transfers between devices: 30.7 us -> 16.8 us
  starting transfers between devices: 30.4 us -> 38.1 us
    ppermute x6 -> x9, waiting for transfers between devices: 25.4 us -> 11.4 us  [all_sum(): lax.ppermute(rounded, ('batch', 'space'), pairs)]
    ppermute x6 -> x9, starting transfers between devices: 6.61 us -> 14.3 us  [all_sum(): lax.ppermute(rounded, ('batch', 'space'), pairs)]
  transfers between devices with their start and end apart: 16 -> 19, of which waited for: 9 -> 10; matrix products, arithmetic and copies ran while one was open for 0% -> 0% of each run, Pallas kernels for 25% -> 26%
where the time goes in v3:
time: 90.5 us; the launch traced here: 89.3 us
  starting transfers between devices  38.1 us (42%)
  Pallas kernels  31.8 us (35%)
  waiting for transfers between devices  16.8 us (19%)
  between operations  2.17 us (2%)
    pallas_call x11, Pallas kernels, call(): pl.pallas_call(kernel, in_specs=specs or [VMEM] * len(args), out_specs=ou...  31.8 us
    ppermute x4, starting transfers between devices, exchange(): lax.ppermute(top, 'space', [((i + 1) % count, i) for i in range(count)])  23.4 us
    ppermute x9, starting transfers between devices, all_sum(): lax.ppermute(rounded, ('batch', 'space'), pairs)  14.3 us
    ppermute x9, waiting for transfers between devices, all_sum(): lax.ppermute(rounded, ('batch', 'space'), pairs)  11.4 us
    ppermute x4, waiting for transfers between devices, exchange(): lax.ppermute(bottom, 'space', [(i, (i + 1) % count) for i in range(count)])  2.65 us
  transfers between devices with their start and end apart: 19, of which 10 were waited for; matrix products, arithmetic and copies ran while one was open for 0% of the time, Pallas kernels for 26%

profile of v3, /device:TPU:0, one launch (start us, length us, event | category | flops | bytes accessed | tf_op | source)
XLA Modules:
  0.0 89.3 jit_solution(1787431396544916536)
XLA Ops:
  2.0 1.9 %start.1 = (bf16[8,16,1024]{2,1,0:T(8,128)(2,1)S(1)}, bf16[64,256]{1,0:T(8,128)(2,1)S(1)}, f32[64,128]{1,0:T(8,128)S(1)}, bf16[2,64,256]{2,1,0:T(8,128)(2,1)S(1)...) custom-call(s32[8,128]{1,0:T(8,128)S(1)} %iota.7.limits, ...), custom_call_target="tpu_custom_call" | custom-call | tf_op jit(solution)/shard_map/start/pallas_call | solution.py:441
  3.9 6.5 %collective-permute-start.1 = (bf16[64,1024]{1,0:T(8,128)(2,1)S(1)}, bf16[64,1024]{1,0:T(8,128)(2,1)S(1)}, u32[]{:S(2)}, u32[]{:S(2)}) collective-permute-start(bf16[64,1024]{1,0:T(8,128)(2,1)S(1)} %get-tuple-element.75.top), channel_id=1, source_target_pairs={{1,0},{2,1},{3,2},{4,3},{5,4},{6,5},{7,6},{0,7},{9,8},{10,9},{11,1... | collective-permute-start | bytes 393224 | tf_op jit(solution)/shard_map/ppermute | solution.py:455
  10.4 5.9 %forward_inner.1 = (bf16[8,64,1024]{2,1,0:T(8,128)(2,1)S(1)}, bf16[6,64,1024]{2,1,0:T(8,128)(2,1)S(1)}, bf16[6,64,1024]{2,1,0:T(8,128)(2,1)S(1)}, bf16[6,64,1024...) custom-call(bf16[8,16,1024]{2,1,0:T(8,128)(2,1)S(1)} %get-tuple-elem, ...), custom_call_target="tpu_custom_call" | custom-call | tf_op jit(solution)/shard_map/forward_inner/pallas_call | solution.py:441
  16.3 2.6 %collective-permute-done.above.f_above = bf16[64,1024]{1,0:T(8,128)(2,1)S(1)} collective-permute-done((bf16[64,1024]{1,0:T(8,128)(2,1)S(1)}, bf16[64,1024]{1,0:T(8,128)(2,1)S(1)}, u32[]{:S(2)}, u32[]{:S(2)}) %collective-permute-start) | collective-permute-done | bytes 131104 | tf_op jit(solution)/shard_map/ppermute | solution.py:454
  18.9 1.6 %forward_edge.1 = (bf16[2,64,1024]{2,1,0:T(8,128)(2,1)S(1)}, bf16[2,64,1024]{2,1,0:T(8,128)(2,1)S(1)}, bf16[2,256,1024]{2,1,0:T(8,128)(2,1)S(1)}, bf16[2,256,102...) custom-call(bf16[8,16,1024]{2,1,0:T(8,128)(2,1)S(1)} %get-tuple-elem, ...), custom_call_target="tpu_custom_call" | custom-call | tf_op jit(solution)/shard_map/forward_edge/pallas_call | solution.py:441
  20.6 5.6 %collective-permute-start.3 = (bf16[64,1024]{1,0:T(8,128)(2,1)S(1)}, bf16[64,1024]{1,0:T(8,128)(2,1)S(1)}, u32[]{:S(2)}, u32[]{:S(2)}) collective-permute-start(bf16[64,1024]{1,0:T(8,128)(2,1)S(1)} %get-tuple-element.97), channel_id=1, source_target_pairs={{1,0},{2,1},{3,2},{4,3},{5,4},{6,5},{7,6},{0,7},{9,8},{10,9},{11,1... | collective-permute-start | bytes 393224 | tf_op jit(solution)/shard_map/ppermute | solution.py:455
  26.3 5.2 %turn_inner.1 = (bf16[6,256,1024]{2,1,0:T(8,128)(2,1)S(1)}, bf16[6,64,1024]{2,1,0:T(8,128)(2,1)S(1)}, f32[64,256]{1,0:T(8,128)S(1)}) custom-call(bf16[8,16,1024]{2,1,0:T(8,128)(2,1)S(1)} %get-tuple-element.74.mask, bf16[8,64,1024]{2,1,0:T(8,128)(2,1)S(1)} %get-tuple-element.95.first1, bf16[6,256,1024]{2,1,0:T(8,128)(2,1)S(1)} %get-tuple-element.100.x1, ...), custom_call_target="tpu_custom_call" | custom-call | tf_op jit(solution)/shard_map/turn_inner/pallas_call | solution.py:441
  31.5 1.6 %turn_edge.1 = (bf16[2,256,1024]{2,1,0:T(8,128)(2,1)S(1)}, bf16[8,64,1024]{2,1,0:T(8,128)(2,1)S(1)}, bf16[2,64,1024]{2,1,0:T(8,128)(2,1)S(1)}, bf16[64,1024]{1,0:T(8,128)(2,1)S(1)}, bf16[64,1024]{1,0:T(8,128)(2,1)S(1)}) custom-call(bf16[8,16,1024]{2,1,0:T(8,128)(2,1)S(1)} %get-tuple-element.74.mask, bf16[8,64,1024]{2,1,0:T(8,128)(2,1)S(1)} %get-tuple-element.95.first1, ...), custom_call_target="tpu_custom_call" | custom-call | tf_op jit(solution)/shard_map/turn_edge/pallas_call | solution.py:441
  33.2 5.6 %collective-permute-start.5 = (bf16[64,1024]{1,0:T(8,128)(2,1)S(1)}, bf16[64,1024]{1,0:T(8,128)(2,1)S(1)}, u32[]{:S(2)}, u32[]{:S(2)}) collective-permute-start(bf16[64,1024]{1,0:T(8,128)(2,1)S(1)} %get-tuple-element.104), channel_id=1, source_target_pairs={{1,0},{2,1},{3,2},{4,3},{5,4},{6,5},{7,6},{0,7},{9,8},{10,9},{11,1... | collective-permute-start | bytes 393224 | tf_op jit(solution)/shard_map/ppermute | solution.py:455
  38.8 4.8 %backward_inner.1 = (bf16[6,256,1024]{2,1,0:T(8,128)(2,1)S(1)}, bf16[6,64,1024]{2,1,0:T(8,128)(2,1)S(1)}, f32[64,256]{1,0:T(8,128)S(1)}, f32[192,192]{1,0:T(8,128)S(1)}, f32[64,256]{1,0:T(8,128)S(1)}) custom-call(bf16[8,16,1024]{2,1,0:T(8,128)(2,1)S(1)} %get-tuple-element.74.mask, bf16[8,64,1024]{2,1,0:T(8,128)(2,1)S(1)} %get-tuple-element.102.gmid2, ...), custom_call_target="tpu_custom_call" | custom-call | tf_op jit(solution)/shard_map/backward_inner/pallas_call | solution.py:441
  45.1 5.6 %collective-permute-start.7 = (bf16[64,1024]{1,0:T(8,128)(2,1)S(1)}, bf16[64,1024]{1,0:T(8,128)(2,1)S(1)}, u32[]{:S(2)}, u32[]{:S(2)}) collective-permute-start(bf16[64,1024]{1,0:T(8,128)(2,1)S(1)} %get-tuple-element.122), channel_id=1, source_target_pairs={{1,0},{2,1},{3,2},{4,3},{5,4},{6,5},{7,6},{0,7},{9,8},{10,9},{11,1... | collective-permute-start | bytes 393224 | tf_op jit(solution)/shard_map/ppermute | solution.py:455
  50.7 5.2 %last_inner.1 = (bf16[6,64,1024]{2,1,0:T(8,128)(2,1)S(1)}, f32[64,256]{1,0:T(8,128)S(1)}, f32[192,192]{1,0:T(8,128)S(1)}, f32[64,256]{1,0:T(8,128)S(1)}) custom-call(bf16[8,64,1024]{2,1,0:T(8,128)(2,1)S(1)} %get-tuple-element.120.gmid2, bf16[8,64,1024]{2,1,0:T(8,128)(2,1)S(1)} %get-tuple-element.86.first0, ...), custom_call_target="tpu_custom_call" | custom-call | tf_op jit(solution)/shard_map/last_inner/pallas_call | solution.py:441
  56.9 1.3 %collective-permute-done.8 = bf16[272,256]{1,0:T(8,128)(2,1)S(1)} collective-permute-done((bf16[272,256]{1,0:T(8,128)(2,1)S(1)}, bf16[272,256]{1,0:T(8,128)(2,1)S(1)}, u32[]{:S(2)}, u32[]{:S(2)}) %collective-permute-start.8) | collective-permute-done | bytes 139296 | tf_op jit(solution)/shard_map/ppermute | solution.py:474
  58.3 2.8 %collective-permute-start.11 = (bf16[272,256]{1,0:T(8,128)(2,1)S(1)}, bf16[272,256]{1,0:T(8,128)(2,1)S(1)}, u32[]{:S(2)}, u32[]{:S(2)}) collective-permute-start(bf16[272,256]{1,0:T(8,128)(2,1)S(1)} %fusion), channel_id=1, source_target_pairs={{0,48},{2,50},{4,52},{6,54},{8,14},{10,12},{12,10},{14,8},{16,32},... | collective-permute-start | bytes 417800 | tf_op jit(solution)/shard_map/ppermute | solution.py:479
  61.4 1.7 %collective-permute-start.9 = (bf16[272,256]{1,0:T(8,128)(2,1)S(1)}, bf16[272,256]{1,0:T(8,128)(2,1)S(1)}, u32[]{:S(2)}, u32[]{:S(2)}) collective-permute-start(bf16[272,256]{1,0:T(8,128)(2,1)S(1)} %fusion), channel_id=1, source_target_pairs={{0,32},{2,34},{4,36},{6,38},{8,12},{10,14},{12,8},{14,10},{16,48},... | collective-permute-start | bytes 417800 | tf_op jit(solution)/shard_map/ppermute | solution.py:479
  63.1 2.4 %grad_images.1 = bf16[8,256,1024]{2,1,0:T(8,128)(2,1)} custom-call(bf16[6,64,1024]{2,1,0:T(8,128)(2,1)S(1)} %get-tuple-element.137.gmid1_inner, bf16[2,64,1024]{2,1,0:T(8,128)(2,1)S(1)} %get-tuple-element.138.gmid1_edge, bf16[6,256,1024]{2,1,0:T(8,128)(2,1)S(1)} %get-tuple-element.127.gsum_inner, bf16[2,256,1024]{2,1,0:T(8,128)(2,1)S(1)} %get-tuple-element.128.gsum_edge, ...), custom_call_target="tpu_custom_call" | custom-call | tf_op jit(solution)/shard_map/grad_images/pallas_call | solution.py:441
  66.2 1.7 %collective-permute-done.9 = bf16[272,256]{1,0:T(8,128)(2,1)S(1)} collective-permute-done((bf16[272,256]{1,0:T(8,128)(2,1)S(1)}, bf16[272,256]{1,0:T(8,128)(2,1)S(1)}, u32[]{:S(2)}, u32[]{:S(2)}) %collective-permute-start.9) | collective-permute-done | bytes 139296 | tf_op jit(solution)/shard_map/ppermute | solution.py:479
  68.2 4.6 %collective-permute-start.12 = (bf16[272,256]{1,0:T(8,128)(2,1)S(1)}, bf16[272,256]{1,0:T(8,128)(2,1)S(1)}, u32[]{:S(2)}, u32[]{:S(2)}) collective-permute-start(bf16[272,256]{1,0:T(8,128)(2,1)S(1)} %convert_element_type.51), channel_id=1, source_target_pairs={{0,4},{2,6},{4,0},{6,2},{8,9},{10,11},{12,13},{14,15},{16,20},{18,... | collective-permute-start | bytes 417800 | tf_op jit(solution)/shard_map/ppermute | solution.py:479
  72.8 1.6 %collective-permute-done.14 = bf16[272,256]{1,0:T(8,128)(2,1)S(1)} collective-permute-done((bf16[272,256]{1,0:T(8,128)(2,1)S(1)}, bf16[272,256]{1,0:T(8,128)(2,1)S(1)}, u32[]{:S(2)}, u32[]{:S(2)}) %collective-permute-start.14) | collective-permute-done | bytes 139296 | tf_op jit(solution)/shard_map/ppermute | solution.py:479
  74.4 3.0 %collective-permute-done.12 = bf16[272,256]{1,0:T(8,128)(2,1)S(1)} collective-permute-done((bf16[272,256]{1,0:T(8,128)(2,1)S(1)}, bf16[272,256]{1,0:T(8,128)(2,1)S(1)}, u32[]{:S(2)}, u32[]{:S(2)}) %collective-permute-start.12) | collective-permute-done | bytes 139296 | tf_op jit(solution)/shard_map/ppermute | solution.py:479
  77.4 1.5 %collective-permute-start.17 = (bf16[272,256]{1,0:T(8,128)(2,1)S(1)}, bf16[272,256]{1,0:T(8,128)(2,1)S(1)}, u32[]{:S(2)}, u32[]{:S(2)}) collective-permute-start(bf16[272,256]{1,0:T(8,128)(2,1)S(1)} %fusion.1), channel_id=1, source_target_pairs={{0,65},{2,67},{4,69},{6,71},{8,56},{10,58},{12,60},{14,62},{16,81}... | collective-permute-start | bytes 417800 | tf_op jit(solution)/shard_map/ppermute | solution.py:479
  78.9 3.3 %collective-permute-start.15 = (bf16[272,256]{1,0:T(8,128)(2,1)S(1)}, bf16[272,256]{1,0:T(8,128)(2,1)S(1)}, u32[]{:S(2)}, u32[]{:S(2)}) collective-permute-start(bf16[272,256]{1,0:T(8,128)(2,1)S(1)} %fusion.1), channel_id=1, source_target_pairs={{0,1},{2,3},{4,5},{6,7},{8,40},{10,42},{12,44},{14,46},{16,17},{18... | collective-permute-start | bytes 417800 | tf_op jit(solution)/shard_map/ppermute | solution.py:479
  82.2 1.6 %collective-permute-done.17 = bf16[272,256]{1,0:T(8,128)(2,1)S(1)} collective-permute-done((bf16[272,256]{1,0:T(8,128)(2,1)S(1)}, bf16[272,256]{1,0:T(8,128)(2,1)S(1)}, u32[]{:S(2)}, u32[]{:S(2)}) %collective-permute-start.17) | collective-permute-done | bytes 139296 | tf_op jit(solution)/shard_map/ppermute | solution.py:479
  84.0 2.7 %collective-permute-done.15 = bf16[272,256]{1,0:T(8,128)(2,1)S(1)} collective-permute-done((bf16[272,256]{1,0:T(8,128)(2,1)S(1)}, bf16[272,256]{1,0:T(8,128)(2,1)S(1)}, u32[]{:S(2)}, u32[]{:S(2)}) %collective-permute-start.15) | collective-permute-done | bytes 139296 | tf_op jit(solution)/shard_map/ppermute | solution.py:479
  (38 shorter events, 6.7 us)
Async XLA Ops:
  1.9 8.4 %copy-start = (bf16[1,8,256,1024]{3,2,1,0:T(8,128)(2,1)S(1)}, bf16[1,8,256,1024]{3,2,1,0:T(8,128)(2,1)}, u32[]{:S(2)}) copy-start(bf16[1,8,256,1024]{3,2,1,0:T(8,128)(2,1)} %param.11) | copy-start | bytes 12582916
  3.9 12.4 %collective-permute-start.1 = (bf16[64,1024]{1,0:T(8,128)(2,1)S(1)}, bf16[64,1024]{1,0:T(8,128)(2,1)S(1)}, u32[]{:S(2)}, u32[]{:S(2)}) collective-permute-start(bf16[64,1024]{1,0:T(8,128)(2,1)S(1)} %get-tuple-element.75.top), channel_id=1, source_target_pairs={{1,0},{2,1},{3,2},{4,3},{5,4},{6,5},{7,6},{0,7},{9,8},{10,9},{11,1... | collective-permute-start | bytes 393224 | tf_op jit(solution)/shard_map/ppermute | solution.py:455
  10.4 8.6 %collective-permute-start = (bf16[64,1024]{1,0:T(8,128)(2,1)S(1)}, bf16[64,1024]{1,0:T(8,128)(2,1)S(1)}, u32[]{:S(2)}, u32[]{:S(2)}) collective-permute-start(bf16[64,1024]{1,0:T(8,128)(2,1)S(1)} %get-tuple-element.76.bottom), channel_id=1, source_target_pairs={{0,1},{1,2},{2,3},{3,4},{4,5},{5,6},{6,7},{7,0},{8,9},{9,10},{10,1... | collective-permute-start | bytes 393224 | tf_op jit(solution)/shard_map/ppermute | solution.py:454
  18.9 7.3 %copy-start.1 = (bf16[1,8,256,1024]{3,2,1,0:T(8,128)(2,1)S(1)}, bf16[1,8,256,1024]{3,2,1,0:T(8,128)(2,1)}, u32[]{:S(2)}) copy-start(bf16[1,8,256,1024]{3,2,1,0:T(8,128)(2,1)} %param.21) | copy-start | bytes 12582916
  20.6 10.9 %collective-permute-start.2 = (bf16[64,1024]{1,0:T(8,128)(2,1)S(1)}, bf16[64,1024]{1,0:T(8,128)(2,1)S(1)}, u32[]{:S(2)}, u32[]{:S(2)}) collective-permute-start(bf16[64,1024]{1,0:T(8,128)(2,1)S(1)} %get-tuple-element.96), channel_id=1, source_target_pairs={{0,1},{1,2},{2,3},{3,4},{4,5},{5,6},{6,7},{7,0},{8,9},{9,10},{10,1... | collective-permute-start | bytes 393224 | tf_op jit(solution)/shard_map/ppermute | solution.py:454
  20.6 10.8 %collective-permute-start.3 = (bf16[64,1024]{1,0:T(8,128)(2,1)S(1)}, bf16[64,1024]{1,0:T(8,128)(2,1)S(1)}, u32[]{:S(2)}, u32[]{:S(2)}) collective-permute-start(bf16[64,1024]{1,0:T(8,128)(2,1)S(1)} %get-tuple-element.97), channel_id=1, source_target_pairs={{1,0},{2,1},{3,2},{4,3},{5,4},{6,5},{7,6},{0,7},{9,8},{10,9},{11,1... | collective-permute-start | bytes 393224 | tf_op jit(solution)/shard_map/ppermute | solution.py:455
  33.1 10.6 %collective-permute-start.4 = (bf16[64,1024]{1,0:T(8,128)(2,1)S(1)}, bf16[64,1024]{1,0:T(8,128)(2,1)S(1)}, u32[]{:S(2)}, u32[]{:S(2)}) collective-permute-start(bf16[64,1024]{1,0:T(8,128)(2,1)S(1)} %get-tuple-element.103), channel_id=1, source_target_pairs={{0,1},{1,2},{2,3},{3,4},{4,5},{5,6},{6,7},{7,0},{8,9},{9,10},{10,1... | collective-permute-start | bytes 393224 | tf_op jit(solution)/shard_map/ppermute | solution.py:454
  33.2 10.5 %collective-permute-start.5 = (bf16[64,1024]{1,0:T(8,128)(2,1)S(1)}, bf16[64,1024]{1,0:T(8,128)(2,1)S(1)}, u32[]{:S(2)}, u32[]{:S(2)}) collective-permute-start(bf16[64,1024]{1,0:T(8,128)(2,1)S(1)} %get-tuple-element.104), channel_id=1, source_target_pairs={{1,0},{2,1},{3,2},{4,3},{5,4},{6,5},{7,6},{0,7},{9,8},{10,9},{11,1... | collective-permute-start | bytes 393224 | tf_op jit(solution)/shard_map/ppermute | solution.py:455
  45.0 10.9 %collective-permute-start.6 = (bf16[64,1024]{1,0:T(8,128)(2,1)S(1)}, bf16[64,1024]{1,0:T(8,128)(2,1)S(1)}, u32[]{:S(2)}, u32[]{:S(2)}) collective-permute-start(bf16[64,1024]{1,0:T(8,128)(2,1)S(1)} %get-tuple-element.121), channel_id=1, source_target_pairs={{0,1},{1,2},{2,3},{3,4},{4,5},{5,6},{6,7},{7,0},{8,9},{9,10},{10,1... | collective-permute-start | bytes 393224 | tf_op jit(solution)/shard_map/ppermute | solution.py:454
  45.1 10.8 %collective-permute-start.7 = (bf16[64,1024]{1,0:T(8,128)(2,1)S(1)}, bf16[64,1024]{1,0:T(8,128)(2,1)S(1)}, u32[]{:S(2)}, u32[]{:S(2)}) collective-permute-start(bf16[64,1024]{1,0:T(8,128)(2,1)S(1)} %get-tuple-element.122), channel_id=1, source_target_pairs={{1,0},{2,1},{3,2},{4,3},{5,4},{6,5},{7,6},{0,7},{9,8},{10,9},{11,1... | collective-permute-start | bytes 393224 | tf_op jit(solution)/shard_map/ppermute | solution.py:455
  56.8 1.4 %collective-permute-start.8 = (bf16[272,256]{1,0:T(8,128)(2,1)S(1)}, bf16[272,256]{1,0:T(8,128)(2,1)S(1)}, u32[]{:S(2)}, u32[]{:S(2)}) collective-permute-start(bf16[272,256]{1,0:T(8,128)(2,1)S(1)} %get-tuple-element.136), channel_id=1, source_target_pairs={{0,8},{8,0},{16,24},{24,16},{32,40},{40,32},{48,56},{56,48},{64,72... | collective-permute-start | bytes 417800 | tf_op jit(solution)/shard_map/ppermute | solution.py:474
  58.3 7.2 %collective-permute-start.11 = (bf16[272,256]{1,0:T(8,128)(2,1)S(1)}, bf16[272,256]{1,0:T(8,128)(2,1)S(1)}, u32[]{:S(2)}, u32[]{:S(2)}) collective-permute-start(bf16[272,256]{1,0:T(8,128)(2,1)S(1)} %fusion), channel_id=1, source_target_pairs={{0,48},{2,50},{4,52},{6,54},{8,14},{10,12},{12,10},{14,8},{16,32},... | collective-permute-start | bytes 417800 | tf_op jit(solution)/shard_map/ppermute | solution.py:479
  61.2 5.1 %collective-permute-start.10 = (bf16[272,256]{1,0:T(8,128)(2,1)S(1)}, bf16[272,256]{1,0:T(8,128)(2,1)S(1)}, u32[]{:S(2)}, u32[]{:S(2)}) collective-permute-start(bf16[272,256]{1,0:T(8,128)(2,1)S(1)} %fusion), channel_id=1, source_target_pairs={{0,16},{2,18},{4,20},{6,22},{8,10},{10,8},{12,14},{14,12},{16,0},{... | collective-permute-start | bytes 417800 | tf_op jit(solution)/shard_map/ppermute | solution.py:479
  61.4 6.6 %collective-permute-start.9 = (bf16[272,256]{1,0:T(8,128)(2,1)S(1)}, bf16[272,256]{1,0:T(8,128)(2,1)S(1)}, u32[]{:S(2)}, u32[]{:S(2)}) collective-permute-start(bf16[272,256]{1,0:T(8,128)(2,1)S(1)} %fusion), channel_id=1, source_target_pairs={{0,32},{2,34},{4,36},{6,38},{8,12},{10,14},{12,8},{14,10},{16,48},... | collective-permute-start | bytes 417800 | tf_op jit(solution)/shard_map/ppermute | solution.py:479
  65.5 22.8 %copy-start.2 = (f32[2,256]{1,0:T(2,128)S(1)}, f32[2,256]{1,0:T(2,128)}, u32[]{:S(2)}) copy-start(f32[2,256]{1,0:T(2,128)} %scale_out.1) | copy-start | bytes 6148
  68.1 6.3 %collective-permute-start.14 = (bf16[272,256]{1,0:T(8,128)(2,1)S(1)}, bf16[272,256]{1,0:T(8,128)(2,1)S(1)}, u32[]{:S(2)}, u32[]{:S(2)}) collective-permute-start(bf16[272,256]{1,0:T(8,128)(2,1)S(1)} %convert_element_type.51), channel_id=1, source_target_pairs={{0,6},{2,4},{4,2},{6,0},{8,73},{10,75},{12,77},{14,79},{16,22},{18... | collective-permute-start | bytes 417800 | tf_op jit(solution)/shard_map/ppermute | solution.py:479
  68.1 6.3 %collective-permute-start.13 = (bf16[272,256]{1,0:T(8,128)(2,1)S(1)}, bf16[272,256]{1,0:T(8,128)(2,1)S(1)}, u32[]{:S(2)}, u32[]{:S(2)}) collective-permute-start(bf16[272,256]{1,0:T(8,128)(2,1)S(1)} %convert_element_type.51), channel_id=1, source_target_pairs={{0,2},{2,0},{4,6},{6,4},{8,72},{10,74},{12,76},{14,78},{16,18},{18... | collective-permute-start | bytes 417800 | tf_op jit(solution)/shard_map/ppermute | solution.py:479
  68.2 9.1 %collective-permute-start.12 = (bf16[272,256]{1,0:T(8,128)(2,1)S(1)}, bf16[272,256]{1,0:T(8,128)(2,1)S(1)}, u32[]{:S(2)}, u32[]{:S(2)}) collective-permute-start(bf16[272,256]{1,0:T(8,128)(2,1)S(1)} %convert_element_type.51), channel_id=1, source_target_pairs={{0,4},{2,6},{4,0},{6,2},{8,9},{10,11},{12,13},{14,15},{16,20},{18,... | collective-permute-start | bytes 417800 | tf_op jit(solution)/shard_map/ppermute | solution.py:479
  77.4 6.3 %collective-permute-start.17 = (bf16[272,256]{1,0:T(8,128)(2,1)S(1)}, bf16[272,256]{1,0:T(8,128)(2,1)S(1)}, u32[]{:S(2)}, u32[]{:S(2)}) collective-permute-start(bf16[272,256]{1,0:T(8,128)(2,1)S(1)} %fusion.1), channel_id=1, source_target_pairs={{0,65},{2,67},{4,69},{6,71},{8,56},{10,58},{12,60},{14,62},{16,81}... | collective-permute-start | bytes 417800 | tf_op jit(solution)/shard_map/ppermute | solution.py:479
  78.9 5.1 %collective-permute-start.16 = (bf16[272,256]{1,0:T(8,128)(2,1)S(1)}, bf16[272,256]{1,0:T(8,128)(2,1)S(1)}, u32[]{:S(2)}, u32[]{:S(2)}) collective-permute-start(bf16[272,256]{1,0:T(8,128)(2,1)S(1)} %fusion.1), channel_id=1, source_target_pairs={{0,64},{2,66},{4,68},{6,70},{8,24},{10,26},{12,28},{14,30},{16,80}... | collective-permute-start | bytes 417800 | tf_op jit(solution)/shard_map/ppermute | solution.py:479
  78.9 7.8 %collective-permute-start.15 = (bf16[272,256]{1,0:T(8,128)(2,1)S(1)}, bf16[272,256]{1,0:T(8,128)(2,1)S(1)}, u32[]{:S(2)}, u32[]{:S(2)}) collective-permute-start(bf16[272,256]{1,0:T(8,128)(2,1)S(1)} %fusion.1), channel_id=1, source_target_pairs={{0,1},{2,3},{4,5},{6,7},{8,40},{10,42},{12,44},{14,46},{16,17},{18... | collective-permute-start | bytes 417800 | tf_op jit(solution)/shard_map/ppermute | solution.py:479
  86.9 1.4 %collective-permute-start.18 = (bf16[272,256]{1,0:T(8,128)(2,1)S(1)}, bf16[272,256]{1,0:T(8,128)(2,1)S(1)}, u32[]{:S(2)}, u32[]{:S(2)}) collective-permute-start(bf16[272,256]{1,0:T(8,128)(2,1)S(1)} %add_convert_fusion.mine), channel_id=1, source_target_pairs={{0,8},{8,0},{16,24},{24,16},{32,40},{40,32},{48,56},{56,48},{64,72... | collective-permute-start | bytes 417800 | tf_op jit(solution)/shard_map/ppermute | solution.py:482

commit v4 on v3

--- a/solution.py
+++ b/solution.py
@@ -465,7 +465,7 @@
     steps = []
     for turn in range(3):
         steps.append([[(flat(*at), flat(*(c ^ mirror if n == orders[at[2]][turn] else c for n, c in enumerate(at))))
-                       for at in places] for mirror in (2, 1, 3)])
+                       for at in places] for mirror in (1, 3, 2)])
     return steps
 
 

time: 90.5 us -> 88.4 us (0.977)
  starting transfers between devices: 38.1 us -> 35.3 us
    ppermute x9, starting transfers between devices: 14.3 us -> 11.6 us  [all_sum(): lax.ppermute(rounded, ('batch', 'space'), pairs)]
  transfers between devices with their start and end apart: 19 -> 19, of which waited for: 10 -> 9; matrix products, arithmetic and copies ran while one was open for 0% -> 0% of each run, Pallas kernels for 26% -> 27%
where the time goes in v4:
time: 88.4 us; the launch traced here: 87.2 us
  starting transfers between devices  35.3 us (40%)
  Pallas kernels  31.8 us (36%)
  waiting for transfers between devices  17.4 us (20%)
  between operations  2.18 us (2%)
    pallas_call x11, Pallas kernels, call(): pl.pallas_call(kernel, in_specs=specs or [VMEM] * len(args), out_specs=ou...  31.8 us
    ppermute x4, starting transfers between devices, exchange(): lax.ppermute(top, 'space', [((i + 1) % count, i) for i in range(count)])  23.4 us
    ppermute x9, waiting for transfers between devices, all_sum(): lax.ppermute(rounded, ('batch', 'space'), pairs)  12.1 us
    ppermute x9, starting transfers between devices, all_sum(): lax.ppermute(rounded, ('batch', 'space'), pairs)  11.6 us
    ppermute x4, waiting for transfers between devices, exchange(): lax.ppermute(bottom, 'space', [(i, (i + 1) % count) for i in range(count)])  2.65 us
  transfers between devices with their start and end apart: 19, of which 9 were waited for; matrix products, arithmetic and copies ran while one was open for 0% of the time, Pallas kernels for 27%

profile of v4, /device:TPU:0, one launch (start us, length us, event | category | flops | bytes accessed | tf_op | source)
XLA Modules:
  0.0 87.2 jit_solution(10331871152302281620)
XLA Ops:
  2.0 1.9 %start.1 = (bf16[8,16,1024]{2,1,0:T(8,128)(2,1)S(1)}, bf16[64,256]{1,0:T(8,128)(2,1)S(1)}, f32[64,128]{1,0:T(8,128)S(1)}, bf16[2,64,256]{2,1,0:T(8,128)(2,1)S(1)...) custom-call(s32[8,128]{1,0:T(8,128)S(1)} %iota.7.limits, ...), custom_call_target="tpu_custom_call" | custom-call | tf_op jit(solution)/shard_map/start/pallas_call | solution.py:441
  3.9 6.5 %collective-permute-start.1 = (bf16[64,1024]{1,0:T(8,128)(2,1)S(1)}, bf16[64,1024]{1,0:T(8,128)(2,1)S(1)}, u32[]{:S(2)}, u32[]{:S(2)}) collective-permute-start(bf16[64,1024]{1,0:T(8,128)(2,1)S(1)} %get-tuple-element.75.top), channel_id=1, source_target_pairs={{1,0},{2,1},{3,2},{4,3},{5,4},{6,5},{7,6},{0,7},{9,8},{10,9},{11,1... | collective-permute-start | bytes 393224 | tf_op jit(solution)/shard_map/ppermute | solution.py:455
  10.4 5.9 %forward_inner.1 = (bf16[8,64,1024]{2,1,0:T(8,128)(2,1)S(1)}, bf16[6,64,1024]{2,1,0:T(8,128)(2,1)S(1)}, bf16[6,64,1024]{2,1,0:T(8,128)(2,1)S(1)}, bf16[6,64,1024...) custom-call(bf16[8,16,1024]{2,1,0:T(8,128)(2,1)S(1)} %get-tuple-elem, ...), custom_call_target="tpu_custom_call" | custom-call | tf_op jit(solution)/shard_map/forward_inner/pallas_call | solution.py:441
  16.3 2.6 %collective-permute-done.above.f_above = bf16[64,1024]{1,0:T(8,128)(2,1)S(1)} collective-permute-done((bf16[64,1024]{1,0:T(8,128)(2,1)S(1)}, bf16[64,1024]{1,0:T(8,128)(2,1)S(1)}, u32[]{:S(2)}, u32[]{:S(2)}) %collective-permute-start) | collective-permute-done | bytes 131104 | tf_op jit(solution)/shard_map/ppermute | solution.py:454
  18.9 1.6 %forward_edge.1 = (bf16[2,64,1024]{2,1,0:T(8,128)(2,1)S(1)}, bf16[2,64,1024]{2,1,0:T(8,128)(2,1)S(1)}, bf16[2,256,1024]{2,1,0:T(8,128)(2,1)S(1)}, bf16[2,256,102...) custom-call(bf16[8,16,1024]{2,1,0:T(8,128)(2,1)S(1)} %get-tuple-elem, ...), custom_call_target="tpu_custom_call" | custom-call | tf_op jit(solution)/shard_map/forward_edge/pallas_call | solution.py:441
  20.6 5.6 %collective-permute-start.3 = (bf16[64,1024]{1,0:T(8,128)(2,1)S(1)}, bf16[64,1024]{1,0:T(8,128)(2,1)S(1)}, u32[]{:S(2)}, u32[]{:S(2)}) collective-permute-start(bf16[64,1024]{1,0:T(8,128)(2,1)S(1)} %get-tuple-element.97), channel_id=1, source_target_pairs={{1,0},{2,1},{3,2},{4,3},{5,4},{6,5},{7,6},{0,7},{9,8},{10,9},{11,1... | collective-permute-start | bytes 393224 | tf_op jit(solution)/shard_map/ppermute | solution.py:455
  26.3 5.2 %turn_inner.1 = (bf16[6,256,1024]{2,1,0:T(8,128)(2,1)S(1)}, bf16[6,64,1024]{2,1,0:T(8,128)(2,1)S(1)}, f32[64,256]{1,0:T(8,128)S(1)}) custom-call(bf16[8,16,1024]{2,1,0:T(8,128)(2,1)S(1)} %get-tuple-element.74.mask, bf16[8,64,1024]{2,1,0:T(8,128)(2,1)S(1)} %get-tuple-element.95.first1, bf16[6,256,1024]{2,1,0:T(8,128)(2,1)S(1)} %get-tuple-element.100.x1, ...), custom_call_target="tpu_custom_call" | custom-call | tf_op jit(solution)/shard_map/turn_inner/pallas_call | solution.py:441
  31.5 1.6 %turn_edge.1 = (bf16[2,256,1024]{2,1,0:T(8,128)(2,1)S(1)}, bf16[8,64,1024]{2,1,0:T(8,128)(2,1)S(1)}, bf16[2,64,1024]{2,1,0:T(8,128)(2,1)S(1)}, bf16[64,1024]{1,0:T(8,128)(2,1)S(1)}, bf16[64,1024]{1,0:T(8,128)(2,1)S(1)}) custom-call(bf16[8,16,1024]{2,1,0:T(8,128)(2,1)S(1)} %get-tuple-element.74.mask, bf16[8,64,1024]{2,1,0:T(8,128)(2,1)S(1)} %get-tuple-element.95.first1, ...), custom_call_target="tpu_custom_call" | custom-call | tf_op jit(solution)/shard_map/turn_edge/pallas_call | solution.py:441
  33.2 5.6 %collective-permute-start.5 = (bf16[64,1024]{1,0:T(8,128)(2,1)S(1)}, bf16[64,1024]{1,0:T(8,128)(2,1)S(1)}, u32[]{:S(2)}, u32[]{:S(2)}) collective-permute-start(bf16[64,1024]{1,0:T(8,128)(2,1)S(1)} %get-tuple-element.104), channel_id=1, source_target_pairs={{1,0},{2,1},{3,2},{4,3},{5,4},{6,5},{7,6},{0,7},{9,8},{10,9},{11,1... | collective-permute-start | bytes 393224 | tf_op jit(solution)/shard_map/ppermute | solution.py:455
  38.8 4.8 %backward_inner.1 = (bf16[6,256,1024]{2,1,0:T(8,128)(2,1)S(1)}, bf16[6,64,1024]{2,1,0:T(8,128)(2,1)S(1)}, f32[64,256]{1,0:T(8,128)S(1)}, f32[192,192]{1,0:T(8,128)S(1)}, f32[64,256]{1,0:T(8,128)S(1)}) custom-call(bf16[8,16,1024]{2,1,0:T(8,128)(2,1)S(1)} %get-tuple-element.74.mask, bf16[8,64,1024]{2,1,0:T(8,128)(2,1)S(1)} %get-tuple-element.102.gmid2, ...), custom_call_target="tpu_custom_call" | custom-call | tf_op jit(solution)/shard_map/backward_inner/pallas_call | solution.py:441
  43.7 1.3 %backward_edge.1 = (bf16[2,256,1024]{2,1,0:T(8,128)(2,1)S(1)}, bf16[8,64,1024]{2,1,0:T(8,128)(2,1)S(1)}, f32[64,256]{1,0:T(8,128)S(1)}, bf16[64,1024]{1,0:T(8,128)(2,1)S(1)}, bf16[64,1024]{1,0:T(8,128)(2,1)S(1)}) custom-call(bf16[8,16,1024]{2,1,0:T(8,128)(2,1)S(1)} %get-tuple-element.74.mask, bf16[8,64,1024]{2,1,0:T(8,128)(2,1)S(1)} %get-tuple-element.102.gmid2, ...), custom_call_target="tpu_custom_call" | custom-call | tf_op jit(solution)/shard_map/backward_edge/pallas_call | solution.py:441
  45.1 5.6 %collective-permute-start.7 = (bf16[64,1024]{1,0:T(8,128)(2,1)S(1)}, bf16[64,1024]{1,0:T(8,128)(2,1)S(1)}, u32[]{:S(2)}, u32[]{:S(2)}) collective-permute-start(bf16[64,1024]{1,0:T(8,128)(2,1)S(1)} %get-tuple-element.122), channel_id=1, source_target_pairs={{1,0},{2,1},{3,2},{4,3},{5,4},{6,5},{7,6},{0,7},{9,8},{10,9},{11,1... | collective-permute-start | bytes 393224 | tf_op jit(solution)/shard_map/ppermute | solution.py:455
  50.7 5.2 %last_inner.1 = (bf16[6,64,1024]{2,1,0:T(8,128)(2,1)S(1)}, f32[64,256]{1,0:T(8,128)S(1)}, f32[192,192]{1,0:T(8,128)S(1)}, f32[64,256]{1,0:T(8,128)S(1)}) custom-call(bf16[8,64,1024]{2,1,0:T(8,128)(2,1)S(1)} %get-tuple-element.120.gmid2, bf16[8,64,1024]{2,1,0:T(8,128)(2,1)S(1)} %get-tuple-element.86.first0, ...), custom_call_target="tpu_custom_call" | custom-call | tf_op jit(solution)/shard_map/last_inner/pallas_call | solution.py:441
  56.9 1.3 %collective-permute-done.8 = bf16[272,256]{1,0:T(8,128)(2,1)S(1)} collective-permute-done((bf16[272,256]{1,0:T(8,128)(2,1)S(1)}, bf16[272,256]{1,0:T(8,128)(2,1)S(1)}, u32[]{:S(2)}, u32[]{:S(2)}) %collective-permute-start.8) | collective-permute-done | bytes 139296 | tf_op jit(solution)/shard_map/ppermute | solution.py:474
  58.3 3.1 %collective-permute-start.11 = (bf16[272,256]{1,0:T(8,128)(2,1)S(1)}, bf16[272,256]{1,0:T(8,128)(2,1)S(1)}, u32[]{:S(2)}, u32[]{:S(2)}) collective-permute-start(bf16[272,256]{1,0:T(8,128)(2,1)S(1)} %fusion), channel_id=1, source_target_pairs={{0,32},{2,34},{4,36},{6,38},{8,12},{10,14},{12,8},{14,10},{16,48},... | collective-permute-start | bytes 417800 | tf_op jit(solution)/shard_map/ppermute | solution.py:479
  62.6 2.4 %grad_images.1 = bf16[8,256,1024]{2,1,0:T(8,128)(2,1)} custom-call(bf16[6,64,1024]{2,1,0:T(8,128)(2,1)S(1)} %get-tuple-element.137.gmid1_inner, bf16[2,64,1024]{2,1,0:T(8,128)(2,1)S(1)} %get-tuple-element.138.gmid1_edge, bf16[6,256,1024]{2,1,0:T(8,128)(2,1)S(1)} %get-tuple-element.127.gsum_inner, bf16[2,256,1024]{2,1,0:T(8,128)(2,1)S(1)} %get-tuple-element.128.gsum_edge, ...), custom_call_target="tpu_custom_call" | custom-call | tf_op jit(solution)/shard_map/grad_images/pallas_call | solution.py:441
  65.0 2.7 %collective-permute-done.10 = bf16[272,256]{1,0:T(8,128)(2,1)S(1)} collective-permute-done((bf16[272,256]{1,0:T(8,128)(2,1)S(1)}, bf16[272,256]{1,0:T(8,128)(2,1)S(1)}, u32[]{:S(2)}, u32[]{:S(2)}) %collective-permute-start.10) | collective-permute-done | bytes 139296 | tf_op jit(solution)/shard_map/ppermute | solution.py:479
  68.0 3.4 %collective-permute-start.12 = (bf16[272,256]{1,0:T(8,128)(2,1)S(1)}, bf16[272,256]{1,0:T(8,128)(2,1)S(1)}, u32[]{:S(2)}, u32[]{:S(2)}) collective-permute-start(bf16[272,256]{1,0:T(8,128)(2,1)S(1)} %convert_element_type.51), channel_id=1, source_target_pairs={{0,2},{2,0},{4,6},{6,4},{8,72},{10,74},{12,76},{14,78},{16,18},{18... | collective-permute-start | bytes 417800 | tf_op jit(solution)/shard_map/ppermute | solution.py:479
  71.4 3.2 %collective-permute-done.14 = bf16[272,256]{1,0:T(8,128)(2,1)S(1)} collective-permute-done((bf16[272,256]{1,0:T(8,128)(2,1)S(1)}, bf16[272,256]{1,0:T(8,128)(2,1)S(1)}, u32[]{:S(2)}, u32[]{:S(2)}) %collective-permute-start.14) | collective-permute-done | bytes 139296 | tf_op jit(solution)/shard_map/ppermute | solution.py:479
  75.8 1.6 %collective-permute-start.17 = (bf16[272,256]{1,0:T(8,128)(2,1)S(1)}, bf16[272,256]{1,0:T(8,128)(2,1)S(1)}, u32[]{:S(2)}, u32[]{:S(2)}) collective-permute-start(bf16[272,256]{1,0:T(8,128)(2,1)S(1)} %fusion.1), channel_id=1, source_target_pairs={{0,1},{2,3},{4,5},{6,7},{8,40},{10,42},{12,44},{14,46},{16,17},{18... | collective-permute-start | bytes 417800 | tf_op jit(solution)/shard_map/ppermute | solution.py:479
  77.4 2.2 %collective-permute-start.16 = (bf16[272,256]{1,0:T(8,128)(2,1)S(1)}, bf16[272,256]{1,0:T(8,128)(2,1)S(1)}, u32[]{:S(2)}, u32[]{:S(2)}) collective-permute-start(bf16[272,256]{1,0:T(8,128)(2,1)S(1)} %fusion.1), channel_id=1, source_target_pairs={{0,65},{2,67},{4,69},{6,71},{8,56},{10,58},{12,60},{14,62},{16,81}... | collective-permute-start | bytes 417800 | tf_op jit(solution)/shard_map/ppermute | solution.py:479
  79.6 2.9 %collective-permute-done.17 = bf16[272,256]{1,0:T(8,128)(2,1)S(1)} collective-permute-done((bf16[272,256]{1,0:T(8,128)(2,1)S(1)}, bf16[272,256]{1,0:T(8,128)(2,1)S(1)}, u32[]{:S(2)}, u32[]{:S(2)}) %collective-permute-start.17) | collective-permute-done | bytes 139296 | tf_op jit(solution)/shard_map/ppermute | solution.py:479
  82.5 1.5 %collective-permute-done.16 = bf16[272,256]{1,0:T(8,128)(2,1)S(1)} collective-permute-done((bf16[272,256]{1,0:T(8,128)(2,1)S(1)}, bf16[272,256]{1,0:T(8,128)(2,1)S(1)}, u32[]{:S(2)}, u32[]{:S(2)}) %collective-permute-start.16) | collective-permute-done | bytes 139296 | tf_op jit(solution)/shard_map/ppermute | solution.py:479
  84.9 1.3 %collective-permute-done.18.other = bf16[272,256]{1,0:T(8,128)(2,1)S(1)} collective-permute-done((bf16[272,256]{1,0:T(8,128)(2,1)S(1)}, bf16[272,256]{1,0:T(8,128)(2,1)S(1)}, u32[]{:S(2)}, u32[]{:S(2)}) %collective-permute-start.18) | collective-permute-done | bytes 139296 | tf_op jit(solution)/shard_map/ppermute | solution.py:482
  (38 shorter events, 6.0 us)
Async XLA Ops:
  1.9 8.4 %copy-start = (bf16[1,8,256,1024]{3,2,1,0:T(8,128)(2,1)S(1)}, bf16[1,8,256,1024]{3,2,1,0:T(8,128)(2,1)}, u32[]{:S(2)}) copy-start(bf16[1,8,256,1024]{3,2,1,0:T(8,128)(2,1)} %param.11) | copy-start | bytes 12582916
  3.9 12.4 %collective-permute-start.1 = (bf16[64,1024]{1,0:T(8,128)(2,1)S(1)}, bf16[64,1024]{1,0:T(8,128)(2,1)S(1)}, u32[]{:S(2)}, u32[]{:S(2)}) collective-permute-start(bf16[64,1024]{1,0:T(8,128)(2,1)S(1)} %get-tuple-element.75.top), channel_id=1, source_target_pairs={{1,0},{2,1},{3,2},{4,3},{5,4},{6,5},{7,6},{0,7},{9,8},{10,9},{11,1... | collective-permute-start | bytes 393224 | tf_op jit(solution)/shard_map/ppermute | solution.py:455
  10.4 8.6 %collective-permute-start = (bf16[64,1024]{1,0:T(8,128)(2,1)S(1)}, bf16[64,1024]{1,0:T(8,128)(2,1)S(1)}, u32[]{:S(2)}, u32[]{:S(2)}) collective-permute-start(bf16[64,1024]{1,0:T(8,128)(2,1)S(1)} %get-tuple-element.76.bottom), channel_id=1, source_target_pairs={{0,1},{1,2},{2,3},{3,4},{4,5},{5,6},{6,7},{7,0},{8,9},{9,10},{10,1... | collective-permute-start | bytes 393224 | tf_op jit(solution)/shard_map/ppermute | solution.py:454
  18.9 7.3 %copy-start.1 = (bf16[1,8,256,1024]{3,2,1,0:T(8,128)(2,1)S(1)}, bf16[1,8,256,1024]{3,2,1,0:T(8,128)(2,1)}, u32[]{:S(2)}) copy-start(bf16[1,8,256,1024]{3,2,1,0:T(8,128)(2,1)} %param.21) | copy-start | bytes 12582916
  20.6 10.9 %collective-permute-start.2 = (bf16[64,1024]{1,0:T(8,128)(2,1)S(1)}, bf16[64,1024]{1,0:T(8,128)(2,1)S(1)}, u32[]{:S(2)}, u32[]{:S(2)}) collective-permute-start(bf16[64,1024]{1,0:T(8,128)(2,1)S(1)} %get-tuple-element.96), channel_id=1, source_target_pairs={{0,1},{1,2},{2,3},{3,4},{4,5},{5,6},{6,7},{7,0},{8,9},{9,10},{10,1... | collective-permute-start | bytes 393224 | tf_op jit(solution)/shard_map/ppermute | solution.py:454
  20.6 10.8 %collective-permute-start.3 = (bf16[64,1024]{1,0:T(8,128)(2,1)S(1)}, bf16[64,1024]{1,0:T(8,128)(2,1)S(1)}, u32[]{:S(2)}, u32[]{:S(2)}) collective-permute-start(bf16[64,1024]{1,0:T(8,128)(2,1)S(1)} %get-tuple-element.97), channel_id=1, source_target_pairs={{1,0},{2,1},{3,2},{4,3},{5,4},{6,5},{7,6},{0,7},{9,8},{10,9},{11,1... | collective-permute-start | bytes 393224 | tf_op jit(solution)/shard_map/ppermute | solution.py:455
  33.1 10.6 %collective-permute-start.4 = (bf16[64,1024]{1,0:T(8,128)(2,1)S(1)}, bf16[64,1024]{1,0:T(8,128)(2,1)S(1)}, u32[]{:S(2)}, u32[]{:S(2)}) collective-permute-start(bf16[64,1024]{1,0:T(8,128)(2,1)S(1)} %get-tuple-element.103), channel_id=1, source_target_pairs={{0,1},{1,2},{2,3},{3,4},{4,5},{5,6},{6,7},{7,0},{8,9},{9,10},{10,1... | collective-permute-start | bytes 393224 | tf_op jit(solution)/shard_map/ppermute | solution.py:454
  33.2 10.5 %collective-permute-start.5 = (bf16[64,1024]{1,0:T(8,128)(2,1)S(1)}, bf16[64,1024]{1,0:T(8,128)(2,1)S(1)}, u32[]{:S(2)}, u32[]{:S(2)}) collective-permute-start(bf16[64,1024]{1,0:T(8,128)(2,1)S(1)} %get-tuple-element.104), channel_id=1, source_target_pairs={{1,0},{2,1},{3,2},{4,3},{5,4},{6,5},{7,6},{0,7},{9,8},{10,9},{11,1... | collective-permute-start | bytes 393224 | tf_op jit(solution)/shard_map/ppermute | solution.py:455
  45.0 10.9 %collective-permute-start.6 = (bf16[64,1024]{1,0:T(8,128)(2,1)S(1)}, bf16[64,1024]{1,0:T(8,128)(2,1)S(1)}, u32[]{:S(2)}, u32[]{:S(2)}) collective-permute-start(bf16[64,1024]{1,0:T(8,128)(2,1)S(1)} %get-tuple-element.121), channel_id=1, source_target_pairs={{0,1},{1,2},{2,3},{3,4},{4,5},{5,6},{6,7},{7,0},{8,9},{9,10},{10,1... | collective-permute-start | bytes 393224 | tf_op jit(solution)/shard_map/ppermute | solution.py:454
  45.1 10.8 %collective-permute-start.7 = (bf16[64,1024]{1,0:T(8,128)(2,1)S(1)}, bf16[64,1024]{1,0:T(8,128)(2,1)S(1)}, u32[]{:S(2)}, u32[]{:S(2)}) collective-permute-start(bf16[64,1024]{1,0:T(8,128)(2,1)S(1)} %get-tuple-element.122), channel_id=1, source_target_pairs={{1,0},{2,1},{3,2},{4,3},{5,4},{6,5},{7,6},{0,7},{9,8},{10,9},{11,1... | collective-permute-start | bytes 393224 | tf_op jit(solution)/shard_map/ppermute | solution.py:455
  56.8 1.4 %collective-permute-start.8 = (bf16[272,256]{1,0:T(8,128)(2,1)S(1)}, bf16[272,256]{1,0:T(8,128)(2,1)S(1)}, u32[]{:S(2)}, u32[]{:S(2)}) collective-permute-start(bf16[272,256]{1,0:T(8,128)(2,1)S(1)} %get-tuple-element.136), channel_id=1, source_target_pairs={{0,8},{8,0},{16,24},{24,16},{32,40},{40,32},{48,56},{56,48},{64,72... | collective-permute-start | bytes 417800 | tf_op jit(solution)/shard_map/ppermute | solution.py:474
  58.3 6.7 %collective-permute-start.11 = (bf16[272,256]{1,0:T(8,128)(2,1)S(1)}, bf16[272,256]{1,0:T(8,128)(2,1)S(1)}, u32[]{:S(2)}, u32[]{:S(2)}) collective-permute-start(bf16[272,256]{1,0:T(8,128)(2,1)S(1)} %fusion), channel_id=1, source_target_pairs={{0,32},{2,34},{4,36},{6,38},{8,12},{10,14},{12,8},{14,10},{16,48},... | collective-permute-start | bytes 417800 | tf_op jit(solution)/shard_map/ppermute | solution.py:479
  61.4 6.3 %collective-permute-start.10 = (bf16[272,256]{1,0:T(8,128)(2,1)S(1)}, bf16[272,256]{1,0:T(8,128)(2,1)S(1)}, u32[]{:S(2)}, u32[]{:S(2)}) collective-permute-start(bf16[272,256]{1,0:T(8,128)(2,1)S(1)} %fusion), channel_id=1, source_target_pairs={{0,48},{2,50},{4,52},{6,54},{8,14},{10,12},{12,10},{14,8},{16,32},... | collective-permute-start | bytes 417800 | tf_op jit(solution)/shard_map/ppermute | solution.py:479
  62.6 5.1 %collective-permute-start.9 = (bf16[272,256]{1,0:T(8,128)(2,1)S(1)}, bf16[272,256]{1,0:T(8,128)(2,1)S(1)}, u32[]{:S(2)}, u32[]{:S(2)}) collective-permute-start(bf16[272,256]{1,0:T(8,128)(2,1)S(1)} %fusion), channel_id=1, source_target_pairs={{0,16},{2,18},{4,20},{6,22},{8,10},{10,8},{12,14},{14,12},{16,0},{... | collective-permute-start | bytes 417800 | tf_op jit(solution)/shard_map/ppermute | solution.py:479
  65.0 21.2 %copy-start.2 = (f32[2,256]{1,0:T(2,128)S(1)}, f32[2,256]{1,0:T(2,128)}, u32[]{:S(2)}) copy-start(f32[2,256]{1,0:T(2,128)} %scale_out.1) | copy-start | bytes 6148
  67.8 6.7 %collective-permute-start.14 = (bf16[272,256]{1,0:T(8,128)(2,1)S(1)}, bf16[272,256]{1,0:T(8,128)(2,1)S(1)}, u32[]{:S(2)}, u32[]{:S(2)}) collective-permute-start(bf16[272,256]{1,0:T(8,128)(2,1)S(1)} %convert_element_type.51), channel_id=1, source_target_pairs={{0,4},{2,6},{4,0},{6,2},{8,9},{10,11},{12,13},{14,15},{16,20},{18,... | collective-permute-start | bytes 417800 | tf_op jit(solution)/shard_map/ppermute | solution.py:479
  67.9 7.8 %collective-permute-start.13 = (bf16[272,256]{1,0:T(8,128)(2,1)S(1)}, bf16[272,256]{1,0:T(8,128)(2,1)S(1)}, u32[]{:S(2)}, u32[]{:S(2)}) collective-permute-start(bf16[272,256]{1,0:T(8,128)(2,1)S(1)} %convert_element_type.51), channel_id=1, source_target_pairs={{0,6},{2,4},{4,2},{6,0},{8,73},{10,75},{12,77},{14,79},{16,22},{18... | collective-permute-start | bytes 417800 | tf_op jit(solution)/shard_map/ppermute | solution.py:479
  68.0 7.7 %collective-permute-start.12 = (bf16[272,256]{1,0:T(8,128)(2,1)S(1)}, bf16[272,256]{1,0:T(8,128)(2,1)S(1)}, u32[]{:S(2)}, u32[]{:S(2)}) collective-permute-start(bf16[272,256]{1,0:T(8,128)(2,1)S(1)} %convert_element_type.51), channel_id=1, source_target_pairs={{0,2},{2,0},{4,6},{6,4},{8,72},{10,74},{12,76},{14,78},{16,18},{18... | collective-permute-start | bytes 417800 | tf_op jit(solution)/shard_map/ppermute | solution.py:479
  75.8 6.7 %collective-permute-start.17 = (bf16[272,256]{1,0:T(8,128)(2,1)S(1)}, bf16[272,256]{1,0:T(8,128)(2,1)S(1)}, u32[]{:S(2)}, u32[]{:S(2)}) collective-permute-start(bf16[272,256]{1,0:T(8,128)(2,1)S(1)} %fusion.1), channel_id=1, source_target_pairs={{0,1},{2,3},{4,5},{6,7},{8,40},{10,42},{12,44},{14,46},{16,17},{18... | collective-permute-start | bytes 417800 | tf_op jit(solution)/shard_map/ppermute | solution.py:479
  77.4 6.5 %collective-permute-start.16 = (bf16[272,256]{1,0:T(8,128)(2,1)S(1)}, bf16[272,256]{1,0:T(8,128)(2,1)S(1)}, u32[]{:S(2)}, u32[]{:S(2)}) collective-permute-start(bf16[272,256]{1,0:T(8,128)(2,1)S(1)} %fusion.1), channel_id=1, source_target_pairs={{0,65},{2,67},{4,69},{6,71},{8,56},{10,58},{12,60},{14,62},{16,81}... | collective-permute-start | bytes 417800 | tf_op jit(solution)/shard_map/ppermute | solution.py:479
  79.6 5.1 %collective-permute-start.15 = (bf16[272,256]{1,0:T(8,128)(2,1)S(1)}, bf16[272,256]{1,0:T(8,128)(2,1)S(1)}, u32[]{:S(2)}, u32[]{:S(2)}) collective-permute-start(bf16[272,256]{1,0:T(8,128)(2,1)S(1)} %fusion.1), channel_id=1, source_target_pairs={{0,64},{2,66},{4,68},{6,70},{8,24},{10,26},{12,28},{14,30},{16,80}... | collective-permute-start | bytes 417800 | tf_op jit(solution)/shard_map/ppermute | solution.py:479
  84.8 1.4 %collective-permute-start.18 = (bf16[272,256]{1,0:T(8,128)(2,1)S(1)}, bf16[272,256]{1,0:T(8,128)(2,1)S(1)}, u32[]{:S(2)}, u32[]{:S(2)}) collective-permute-start(bf16[272,256]{1,0:T(8,128)(2,1)S(1)} %add_convert_fusion.mine), channel_id=1, source_target_pairs={{0,8},{8,0},{16,24},{24,16},{32,40},{40,32},{48,56},{56,48},{64,72... | collective-permute-start | bytes 417800 | tf_op jit(solution)/shard_map/ppermute | solution.py:482

commit v5 on v4

--- a/solution.py
+++ b/solution.py
@@ -451,8 +451,8 @@
 
 def exchange(top, bottom):
     count = lax.axis_size("space")
+    below = lax.ppermute(top, "space", [((i + 1) % count, i) for i in range(count)])
     above = lax.ppermute(bottom, "space", [(i, (i + 1) % count) for i in range(count)])
-    below = lax.ppermute(top, "space", [((i + 1) % count, i) for i in range(count)])
     return above, below
 
 

time: 88.4 us -> 88.4 us (level)
  no operation moved by 1% of the time
where the time goes in v5:
time: 88.4 us; the launch traced here: 87.2 us
  starting transfers between devices  35.3 us (40%)
  Pallas kernels  31.8 us (36%)
  waiting for transfers between devices  17.4 us (20%)
  between operations  2.18 us (2%)
    pallas_call x11, Pallas kernels, call(): pl.pallas_call(kernel, in_specs=specs or [VMEM] * len(args), out_specs=ou...  31.8 us
    ppermute x4, starting transfers between devices, exchange(): lax.ppermute(top, 'space', [((i + 1) % count, i) for i in range(count)])  23.4 us
    ppermute x9, waiting for transfers between devices, all_sum(): lax.ppermute(rounded, ('batch', 'space'), pairs)  12.1 us
    ppermute x9, starting transfers between devices, all_sum(): lax.ppermute(rounded, ('batch', 'space'), pairs)  11.6 us
    ppermute x4, waiting for transfers between devices, exchange(): lax.ppermute(bottom, 'space', [(i, (i + 1) % count) for i in range(count)])  2.65 us
  transfers between devices with their start and end apart: 19, of which 9 were waited for; matrix products, arithmetic and copies ran while one was open for 0% of the time, Pallas kernels for 27%

profile of v5, /device:TPU:0, one launch (start us, length us, event | category | flops | bytes accessed | tf_op | source)
XLA Modules:
  0.0 87.2 jit_solution(10331871152302281620)
XLA Ops:
  2.0 1.9 %start.1 = (bf16[8,16,1024]{2,1,0:T(8,128)(2,1)S(1)}, bf16[64,256]{1,0:T(8,128)(2,1)S(1)}, f32[64,128]{1,0:T(8,128)S(1)}, bf16[2,64,256]{2,1,0:T(8,128)(2,1)S(1)...) custom-call(s32[8,128]{1,0:T(8,128)S(1)} %iota.7.limits, ...), custom_call_target="tpu_custom_call" | custom-call | tf_op jit(solution)/shard_map/start/pallas_call | solution.py:441
  3.9 6.5 %collective-permute-start.1 = (bf16[64,1024]{1,0:T(8,128)(2,1)S(1)}, bf16[64,1024]{1,0:T(8,128)(2,1)S(1)}, u32[]{:S(2)}, u32[]{:S(2)}) collective-permute-start(bf16[64,1024]{1,0:T(8,128)(2,1)S(1)} %get-tuple-element.75.top), channel_id=1, source_target_pairs={{1,0},{2,1},{3,2},{4,3},{5,4},{6,5},{7,6},{0,7},{9,8},{10,9},{11,1... | collective-permute-start | bytes 393224 | tf_op jit(solution)/shard_map/ppermute | solution.py:454
  10.4 5.9 %forward_inner.1 = (bf16[8,64,1024]{2,1,0:T(8,128)(2,1)S(1)}, bf16[6,64,1024]{2,1,0:T(8,128)(2,1)S(1)}, bf16[6,64,1024]{2,1,0:T(8,128)(2,1)S(1)}, bf16[6,64,1024...) custom-call(bf16[8,16,1024]{2,1,0:T(8,128)(2,1)S(1)} %get-tuple-elem, ...), custom_call_target="tpu_custom_call" | custom-call | tf_op jit(solution)/shard_map/forward_inner/pallas_call | solution.py:441
  16.3 2.6 %collective-permute-done.above.f_above = bf16[64,1024]{1,0:T(8,128)(2,1)S(1)} collective-permute-done((bf16[64,1024]{1,0:T(8,128)(2,1)S(1)}, bf16[64,1024]{1,0:T(8,128)(2,1)S(1)}, u32[]{:S(2)}, u32[]{:S(2)}) %collective-permute-start) | collective-permute-done | bytes 131104 | tf_op jit(solution)/shard_map/ppermute | solution.py:455
  18.9 1.6 %forward_edge.1 = (bf16[2,64,1024]{2,1,0:T(8,128)(2,1)S(1)}, bf16[2,64,1024]{2,1,0:T(8,128)(2,1)S(1)}, bf16[2,256,1024]{2,1,0:T(8,128)(2,1)S(1)}, bf16[2,256,102...) custom-call(bf16[8,16,1024]{2,1,0:T(8,128)(2,1)S(1)} %get-tuple-elem, ...), custom_call_target="tpu_custom_call" | custom-call | tf_op jit(solution)/shard_map/forward_edge/pallas_call | solution.py:441
  20.6 5.6 %collective-permute-start.3 = (bf16[64,1024]{1,0:T(8,128)(2,1)S(1)}, bf16[64,1024]{1,0:T(8,128)(2,1)S(1)}, u32[]{:S(2)}, u32[]{:S(2)}) collective-permute-start(bf16[64,1024]{1,0:T(8,128)(2,1)S(1)} %get-tuple-element.97), channel_id=1, source_target_pairs={{1,0},{2,1},{3,2},{4,3},{5,4},{6,5},{7,6},{0,7},{9,8},{10,9},{11,1... | collective-permute-start | bytes 393224 | tf_op jit(solution)/shard_map/ppermute | solution.py:454
  26.3 5.2 %turn_inner.1 = (bf16[6,256,1024]{2,1,0:T(8,128)(2,1)S(1)}, bf16[6,64,1024]{2,1,0:T(8,128)(2,1)S(1)}, f32[64,256]{1,0:T(8,128)S(1)}) custom-call(bf16[8,16,1024]{2,1,0:T(8,128)(2,1)S(1)} %get-tuple-element.74.mask, bf16[8,64,1024]{2,1,0:T(8,128)(2,1)S(1)} %get-tuple-element.95.first1, bf16[6,256,1024]{2,1,0:T(8,128)(2,1)S(1)} %get-tuple-element.100.x1, ...), custom_call_target="tpu_custom_call" | custom-call | tf_op jit(solution)/shard_map/turn_inner/pallas_call | solution.py:441
  31.5 1.6 %turn_edge.1 = (bf16[2,256,1024]{2,1,0:T(8,128)(2,1)S(1)}, bf16[8,64,1024]{2,1,0:T(8,128)(2,1)S(1)}, bf16[2,64,1024]{2,1,0:T(8,128)(2,1)S(1)}, bf16[64,1024]{1,0:T(8,128)(2,1)S(1)}, bf16[64,1024]{1,0:T(8,128)(2,1)S(1)}) custom-call(bf16[8,16,1024]{2,1,0:T(8,128)(2,1)S(1)} %get-tuple-element.74.mask, bf16[8,64,1024]{2,1,0:T(8,128)(2,1)S(1)} %get-tuple-element.95.first1, ...), custom_call_target="tpu_custom_call" | custom-call | tf_op jit(solution)/shard_map/turn_edge/pallas_call | solution.py:441
  33.2 5.6 %collective-permute-start.5 = (bf16[64,1024]{1,0:T(8,128)(2,1)S(1)}, bf16[64,1024]{1,0:T(8,128)(2,1)S(1)}, u32[]{:S(2)}, u32[]{:S(2)}) collective-permute-start(bf16[64,1024]{1,0:T(8,128)(2,1)S(1)} %get-tuple-element.104), channel_id=1, source_target_pairs={{1,0},{2,1},{3,2},{4,3},{5,4},{6,5},{7,6},{0,7},{9,8},{10,9},{11,1... | collective-permute-start | bytes 393224 | tf_op jit(solution)/shard_map/ppermute | solution.py:454
  38.8 4.8 %backward_inner.1 = (bf16[6,256,1024]{2,1,0:T(8,128)(2,1)S(1)}, bf16[6,64,1024]{2,1,0:T(8,128)(2,1)S(1)}, f32[64,256]{1,0:T(8,128)S(1)}, f32[192,192]{1,0:T(8,128)S(1)}, f32[64,256]{1,0:T(8,128)S(1)}) custom-call(bf16[8,16,1024]{2,1,0:T(8,128)(2,1)S(1)} %get-tuple-element.74.mask, bf16[8,64,1024]{2,1,0:T(8,128)(2,1)S(1)} %get-tuple-element.102.gmid2, ...), custom_call_target="tpu_custom_call" | custom-call | tf_op jit(solution)/shard_map/backward_inner/pallas_call | solution.py:441
  43.7 1.3 %backward_edge.1 = (bf16[2,256,1024]{2,1,0:T(8,128)(2,1)S(1)}, bf16[8,64,1024]{2,1,0:T(8,128)(2,1)S(1)}, f32[64,256]{1,0:T(8,128)S(1)}, bf16[64,1024]{1,0:T(8,128)(2,1)S(1)}, bf16[64,1024]{1,0:T(8,128)(2,1)S(1)}) custom-call(bf16[8,16,1024]{2,1,0:T(8,128)(2,1)S(1)} %get-tuple-element.74.mask, bf16[8,64,1024]{2,1,0:T(8,128)(2,1)S(1)} %get-tuple-element.102.gmid2, ...), custom_call_target="tpu_custom_call" | custom-call | tf_op jit(solution)/shard_map/backward_edge/pallas_call | solution.py:441
  45.1 5.6 %collective-permute-start.7 = (bf16[64,1024]{1,0:T(8,128)(2,1)S(1)}, bf16[64,1024]{1,0:T(8,128)(2,1)S(1)}, u32[]{:S(2)}, u32[]{:S(2)}) collective-permute-start(bf16[64,1024]{1,0:T(8,128)(2,1)S(1)} %get-tuple-element.122), channel_id=1, source_target_pairs={{1,0},{2,1},{3,2},{4,3},{5,4},{6,5},{7,6},{0,7},{9,8},{10,9},{11,1... | collective-permute-start | bytes 393224 | tf_op jit(solution)/shard_map/ppermute | solution.py:454
  50.7 5.2 %last_inner.1 = (bf16[6,64,1024]{2,1,0:T(8,128)(2,1)S(1)}, f32[64,256]{1,0:T(8,128)S(1)}, f32[192,192]{1,0:T(8,128)S(1)}, f32[64,256]{1,0:T(8,128)S(1)}) custom-call(bf16[8,64,1024]{2,1,0:T(8,128)(2,1)S(1)} %get-tuple-element.120.gmid2, bf16[8,64,1024]{2,1,0:T(8,128)(2,1)S(1)} %get-tuple-element.86.first0, ...), custom_call_target="tpu_custom_call" | custom-call | tf_op jit(solution)/shard_map/last_inner/pallas_call | solution.py:441
  56.9 1.3 %collective-permute-done.8 = bf16[272,256]{1,0:T(8,128)(2,1)S(1)} collective-permute-done((bf16[272,256]{1,0:T(8,128)(2,1)S(1)}, bf16[272,256]{1,0:T(8,128)(2,1)S(1)}, u32[]{:S(2)}, u32[]{:S(2)}) %collective-permute-start.8) | collective-permute-done | bytes 139296 | tf_op jit(solution)/shard_map/ppermute | solution.py:474
  58.3 3.1 %collective-permute-start.11 = (bf16[272,256]{1,0:T(8,128)(2,1)S(1)}, bf16[272,256]{1,0:T(8,128)(2,1)S(1)}, u32[]{:S(2)}, u32[]{:S(2)}) collective-permute-start(bf16[272,256]{1,0:T(8,128)(2,1)S(1)} %fusion), channel_id=1, source_target_pairs={{0,32},{2,34},{4,36},{6,38},{8,12},{10,14},{12,8},{14,10},{16,48},... | collective-permute-start | bytes 417800 | tf_op jit(solution)/shard_map/ppermute | solution.py:479
  62.6 2.4 %grad_images.1 = bf16[8,256,1024]{2,1,0:T(8,128)(2,1)} custom-call(bf16[6,64,1024]{2,1,0:T(8,128)(2,1)S(1)} %get-tuple-element.137.gmid1_inner, bf16[2,64,1024]{2,1,0:T(8,128)(2,1)S(1)} %get-tuple-element.138.gmid1_edge, bf16[6,256,1024]{2,1,0:T(8,128)(2,1)S(1)} %get-tuple-element.127.gsum_inner, bf16[2,256,1024]{2,1,0:T(8,128)(2,1)S(1)} %get-tuple-element.128.gsum_edge, ...), custom_call_target="tpu_custom_call" | custom-call | tf_op jit(solution)/shard_map/grad_images/pallas_call | solution.py:441
  65.0 2.7 %collective-permute-done.10 = bf16[272,256]{1,0:T(8,128)(2,1)S(1)} collective-permute-done((bf16[272,256]{1,0:T(8,128)(2,1)S(1)}, bf16[272,256]{1,0:T(8,128)(2,1)S(1)}, u32[]{:S(2)}, u32[]{:S(2)}) %collective-permute-start.10) | collective-permute-done | bytes 139296 | tf_op jit(solution)/shard_map/ppermute | solution.py:479
  68.0 3.4 %collective-permute-start.12 = (bf16[272,256]{1,0:T(8,128)(2,1)S(1)}, bf16[272,256]{1,0:T(8,128)(2,1)S(1)}, u32[]{:S(2)}, u32[]{:S(2)}) collective-permute-start(bf16[272,256]{1,0:T(8,128)(2,1)S(1)} %convert_element_type.51), channel_id=1, source_target_pairs={{0,2},{2,0},{4,6},{6,4},{8,72},{10,74},{12,76},{14,78},{16,18},{18... | collective-permute-start | bytes 417800 | tf_op jit(solution)/shard_map/ppermute | solution.py:479
  71.4 3.2 %collective-permute-done.14 = bf16[272,256]{1,0:T(8,128)(2,1)S(1)} collective-permute-done((bf16[272,256]{1,0:T(8,128)(2,1)S(1)}, bf16[272,256]{1,0:T(8,128)(2,1)S(1)}, u32[]{:S(2)}, u32[]{:S(2)}) %collective-permute-start.14) | collective-permute-done | bytes 139296 | tf_op jit(solution)/shard_map/ppermute | solution.py:479
  75.8 1.6 %collective-permute-start.17 = (bf16[272,256]{1,0:T(8,128)(2,1)S(1)}, bf16[272,256]{1,0:T(8,128)(2,1)S(1)}, u32[]{:S(2)}, u32[]{:S(2)}) collective-permute-start(bf16[272,256]{1,0:T(8,128)(2,1)S(1)} %fusion.1), channel_id=1, source_target_pairs={{0,1},{2,3},{4,5},{6,7},{8,40},{10,42},{12,44},{14,46},{16,17},{18... | collective-permute-start | bytes 417800 | tf_op jit(solution)/shard_map/ppermute | solution.py:479
  77.4 2.2 %collective-permute-start.16 = (bf16[272,256]{1,0:T(8,128)(2,1)S(1)}, bf16[272,256]{1,0:T(8,128)(2,1)S(1)}, u32[]{:S(2)}, u32[]{:S(2)}) collective-permute-start(bf16[272,256]{1,0:T(8,128)(2,1)S(1)} %fusion.1), channel_id=1, source_target_pairs={{0,65},{2,67},{4,69},{6,71},{8,56},{10,58},{12,60},{14,62},{16,81}... | collective-permute-start | bytes 417800 | tf_op jit(solution)/shard_map/ppermute | solution.py:479
  79.6 2.9 %collective-permute-done.17 = bf16[272,256]{1,0:T(8,128)(2,1)S(1)} collective-permute-done((bf16[272,256]{1,0:T(8,128)(2,1)S(1)}, bf16[272,256]{1,0:T(8,128)(2,1)S(1)}, u32[]{:S(2)}, u32[]{:S(2)}) %collective-permute-start.17) | collective-permute-done | bytes 139296 | tf_op jit(solution)/shard_map/ppermute | solution.py:479
  82.5 1.5 %collective-permute-done.16 = bf16[272,256]{1,0:T(8,128)(2,1)S(1)} collective-permute-done((bf16[272,256]{1,0:T(8,128)(2,1)S(1)}, bf16[272,256]{1,0:T(8,128)(2,1)S(1)}, u32[]{:S(2)}, u32[]{:S(2)}) %collective-permute-start.16) | collective-permute-done | bytes 139296 | tf_op jit(solution)/shard_map/ppermute | solution.py:479
  84.9 1.3 %collective-permute-done.18.other = bf16[272,256]{1,0:T(8,128)(2,1)S(1)} collective-permute-done((bf16[272,256]{1,0:T(8,128)(2,1)S(1)}, bf16[272,256]{1,0:T(8,128)(2,1)S(1)}, u32[]{:S(2)}, u32[]{:S(2)}) %collective-permute-start.18) | collective-permute-done | bytes 139296 | tf_op jit(solution)/shard_map/ppermute | solution.py:482
  (38 shorter events, 6.0 us)
Async XLA Ops:
  1.9 8.4 %copy-start = (bf16[1,8,256,1024]{3,2,1,0:T(8,128)(2,1)S(1)}, bf16[1,8,256,1024]{3,2,1,0:T(8,128)(2,1)}, u32[]{:S(2)}) copy-start(bf16[1,8,256,1024]{3,2,1,0:T(8,128)(2,1)} %param.11) | copy-start | bytes 12582916
  3.9 12.4 %collective-permute-start.1 = (bf16[64,1024]{1,0:T(8,128)(2,1)S(1)}, bf16[64,1024]{1,0:T(8,128)(2,1)S(1)}, u32[]{:S(2)}, u32[]{:S(2)}) collective-permute-start(bf16[64,1024]{1,0:T(8,128)(2,1)S(1)} %get-tuple-element.75.top), channel_id=1, source_target_pairs={{1,0},{2,1},{3,2},{4,3},{5,4},{6,5},{7,6},{0,7},{9,8},{10,9},{11,1... | collective-permute-start | bytes 393224 | tf_op jit(solution)/shard_map/ppermute | solution.py:454
  10.4 8.6 %collective-permute-start = (bf16[64,1024]{1,0:T(8,128)(2,1)S(1)}, bf16[64,1024]{1,0:T(8,128)(2,1)S(1)}, u32[]{:S(2)}, u32[]{:S(2)}) collective-permute-start(bf16[64,1024]{1,0:T(8,128)(2,1)S(1)} %get-tuple-element.76.bottom), channel_id=1, source_target_pairs={{0,1},{1,2},{2,3},{3,4},{4,5},{5,6},{6,7},{7,0},{8,9},{9,10},{10,1... | collective-permute-start | bytes 393224 | tf_op jit(solution)/shard_map/ppermute | solution.py:455
  18.9 7.3 %copy-start.1 = (bf16[1,8,256,1024]{3,2,1,0:T(8,128)(2,1)S(1)}, bf16[1,8,256,1024]{3,2,1,0:T(8,128)(2,1)}, u32[]{:S(2)}) copy-start(bf16[1,8,256,1024]{3,2,1,0:T(8,128)(2,1)} %param.21) | copy-start | bytes 12582916
  20.6 10.9 %collective-permute-start.2 = (bf16[64,1024]{1,0:T(8,128)(2,1)S(1)}, bf16[64,1024]{1,0:T(8,128)(2,1)S(1)}, u32[]{:S(2)}, u32[]{:S(2)}) collective-permute-start(bf16[64,1024]{1,0:T(8,128)(2,1)S(1)} %get-tuple-element.96), channel_id=1, source_target_pairs={{0,1},{1,2},{2,3},{3,4},{4,5},{5,6},{6,7},{7,0},{8,9},{9,10},{10,1... | collective-permute-start | bytes 393224 | tf_op jit(solution)/shard_map/ppermute | solution.py:455
  20.6 10.8 %collective-permute-start.3 = (bf16[64,1024]{1,0:T(8,128)(2,1)S(1)}, bf16[64,1024]{1,0:T(8,128)(2,1)S(1)}, u32[]{:S(2)}, u32[]{:S(2)}) collective-permute-start(bf16[64,1024]{1,0:T(8,128)(2,1)S(1)} %get-tuple-element.97), channel_id=1, source_target_pairs={{1,0},{2,1},{3,2},{4,3},{5,4},{6,5},{7,6},{0,7},{9,8},{10,9},{11,1... | collective-permute-start | bytes 393224 | tf_op jit(solution)/shard_map/ppermute | solution.py:454
  33.1 10.6 %collective-permute-start.4 = (bf16[64,1024]{1,0:T(8,128)(2,1)S(1)}, bf16[64,1024]{1,0:T(8,128)(2,1)S(1)}, u32[]{:S(2)}, u32[]{:S(2)}) collective-permute-start(bf16[64,1024]{1,0:T(8,128)(2,1)S(1)} %get-tuple-element.103), channel_id=1, source_target_pairs={{0,1},{1,2},{2,3},{3,4},{4,5},{5,6},{6,7},{7,0},{8,9},{9,10},{10,1... | collective-permute-start | bytes 393224 | tf_op jit(solution)/shard_map/ppermute | solution.py:455
  33.2 10.5 %collective-permute-start.5 = (bf16[64,1024]{1,0:T(8,128)(2,1)S(1)}, bf16[64,1024]{1,0:T(8,128)(2,1)S(1)}, u32[]{:S(2)}, u32[]{:S(2)}) collective-permute-start(bf16[64,1024]{1,0:T(8,128)(2,1)S(1)} %get-tuple-element.104), channel_id=1, source_target_pairs={{1,0},{2,1},{3,2},{4,3},{5,4},{6,5},{7,6},{0,7},{9,8},{10,9},{11,1... | collective-permute-start | bytes 393224 | tf_op jit(solution)/shard_map/ppermute | solution.py:454
  45.0 10.9 %collective-permute-start.6 = (bf16[64,1024]{1,0:T(8,128)(2,1)S(1)}, bf16[64,1024]{1,0:T(8,128)(2,1)S(1)}, u32[]{:S(2)}, u32[]{:S(2)}) collective-permute-start(bf16[64,1024]{1,0:T(8,128)(2,1)S(1)} %get-tuple-element.121), channel_id=1, source_target_pairs={{0,1},{1,2},{2,3},{3,4},{4,5},{5,6},{6,7},{7,0},{8,9},{9,10},{10,1... | collective-permute-start | bytes 393224 | tf_op jit(solution)/shard_map/ppermute | solution.py:455
  45.1 10.8 %collective-permute-start.7 = (bf16[64,1024]{1,0:T(8,128)(2,1)S(1)}, bf16[64,1024]{1,0:T(8,128)(2,1)S(1)}, u32[]{:S(2)}, u32[]{:S(2)}) collective-permute-start(bf16[64,1024]{1,0:T(8,128)(2,1)S(1)} %get-tuple-element.122), channel_id=1, source_target_pairs={{1,0},{2,1},{3,2},{4,3},{5,4},{6,5},{7,6},{0,7},{9,8},{10,9},{11,1... | collective-permute-start | bytes 393224 | tf_op jit(solution)/shard_map/ppermute | solution.py:454
  56.8 1.4 %collective-permute-start.8 = (bf16[272,256]{1,0:T(8,128)(2,1)S(1)}, bf16[272,256]{1,0:T(8,128)(2,1)S(1)}, u32[]{:S(2)}, u32[]{:S(2)}) collective-permute-start(bf16[272,256]{1,0:T(8,128)(2,1)S(1)} %get-tuple-element.136), channel_id=1, source_target_pairs={{0,8},{8,0},{16,24},{24,16},{32,40},{40,32},{48,56},{56,48},{64,72... | collective-permute-start | bytes 417800 | tf_op jit(solution)/shard_map/ppermute | solution.py:474
  58.3 6.7 %collective-permute-start.11 = (bf16[272,256]{1,0:T(8,128)(2,1)S(1)}, bf16[272,256]{1,0:T(8,128)(2,1)S(1)}, u32[]{:S(2)}, u32[]{:S(2)}) collective-permute-start(bf16[272,256]{1,0:T(8,128)(2,1)S(1)} %fusion), channel_id=1, source_target_pairs={{0,32},{2,34},{4,36},{6,38},{8,12},{10,14},{12,8},{14,10},{16,48},... | collective-permute-start | bytes 417800 | tf_op jit(solution)/shard_map/ppermute | solution.py:479
  61.4 6.3 %collective-permute-start.10 = (bf16[272,256]{1,0:T(8,128)(2,1)S(1)}, bf16[272,256]{1,0:T(8,128)(2,1)S(1)}, u32[]{:S(2)}, u32[]{:S(2)}) collective-permute-start(bf16[272,256]{1,0:T(8,128)(2,1)S(1)} %fusion), channel_id=1, source_target_pairs={{0,48},{2,50},{4,52},{6,54},{8,14},{10,12},{12,10},{14,8},{16,32},... | collective-permute-start | bytes 417800 | tf_op jit(solution)/shard_map/ppermute | solution.py:479
  62.6 5.1 %collective-permute-start.9 = (bf16[272,256]{1,0:T(8,128)(2,1)S(1)}, bf16[272,256]{1,0:T(8,128)(2,1)S(1)}, u32[]{:S(2)}, u32[]{:S(2)}) collective-permute-start(bf16[272,256]{1,0:T(8,128)(2,1)S(1)} %fusion), channel_id=1, source_target_pairs={{0,16},{2,18},{4,20},{6,22},{8,10},{10,8},{12,14},{14,12},{16,0},{... | collective-permute-start | bytes 417800 | tf_op jit(solution)/shard_map/ppermute | solution.py:479
  65.0 21.2 %copy-start.2 = (f32[2,256]{1,0:T(2,128)S(1)}, f32[2,256]{1,0:T(2,128)}, u32[]{:S(2)}) copy-start(f32[2,256]{1,0:T(2,128)} %scale_out.1) | copy-start | bytes 6148
  67.8 6.7 %collective-permute-start.14 = (bf16[272,256]{1,0:T(8,128)(2,1)S(1)}, bf16[272,256]{1,0:T(8,128)(2,1)S(1)}, u32[]{:S(2)}, u32[]{:S(2)}) collective-permute-start(bf16[272,256]{1,0:T(8,128)(2,1)S(1)} %convert_element_type.51), channel_id=1, source_target_pairs={{0,4},{2,6},{4,0},{6,2},{8,9},{10,11},{12,13},{14,15},{16,20},{18,... | collective-permute-start | bytes 417800 | tf_op jit(solution)/shard_map/ppermute | solution.py:479
  67.9 7.8 %collective-permute-start.13 = (bf16[272,256]{1,0:T(8,128)(2,1)S(1)}, bf16[272,256]{1,0:T(8,128)(2,1)S(1)}, u32[]{:S(2)}, u32[]{:S(2)}) collective-permute-start(bf16[272,256]{1,0:T(8,128)(2,1)S(1)} %convert_element_type.51), channel_id=1, source_target_pairs={{0,6},{2,4},{4,2},{6,0},{8,73},{10,75},{12,77},{14,79},{16,22},{18... | collective-permute-start | bytes 417800 | tf_op jit(solution)/shard_map/ppermute | solution.py:479
  68.0 7.7 %collective-permute-start.12 = (bf16[272,256]{1,0:T(8,128)(2,1)S(1)}, bf16[272,256]{1,0:T(8,128)(2,1)S(1)}, u32[]{:S(2)}, u32[]{:S(2)}) collective-permute-start(bf16[272,256]{1,0:T(8,128)(2,1)S(1)} %convert_element_type.51), channel_id=1, source_target_pairs={{0,2},{2,0},{4,6},{6,4},{8,72},{10,74},{12,76},{14,78},{16,18},{18... | collective-permute-start | bytes 417800 | tf_op jit(solution)/shard_map/ppermute | solution.py:479
  75.8 6.7 %collective-permute-start.17 = (bf16[272,256]{1,0:T(8,128)(2,1)S(1)}, bf16[272,256]{1,0:T(8,128)(2,1)S(1)}, u32[]{:S(2)}, u32[]{:S(2)}) collective-permute-start(bf16[272,256]{1,0:T(8,128)(2,1)S(1)} %fusion.1), channel_id=1, source_target_pairs={{0,1},{2,3},{4,5},{6,7},{8,40},{10,42},{12,44},{14,46},{16,17},{18... | collective-permute-start | bytes 417800 | tf_op jit(solution)/shard_map/ppermute | solution.py:479
  77.4 6.5 %collective-permute-start.16 = (bf16[272,256]{1,0:T(8,128)(2,1)S(1)}, bf16[272,256]{1,0:T(8,128)(2,1)S(1)}, u32[]{:S(2)}, u32[]{:S(2)}) collective-permute-start(bf16[272,256]{1,0:T(8,128)(2,1)S(1)} %fusion.1), channel_id=1, source_target_pairs={{0,65},{2,67},{4,69},{6,71},{8,56},{10,58},{12,60},{14,62},{16,81}... | collective-permute-start | bytes 417800 | tf_op jit(solution)/shard_map/ppermute | solution.py:479
  79.6 5.1 %collective-permute-start.15 = (bf16[272,256]{1,0:T(8,128)(2,1)S(1)}, bf16[272,256]{1,0:T(8,128)(2,1)S(1)}, u32[]{:S(2)}, u32[]{:S(2)}) collective-permute-start(bf16[272,256]{1,0:T(8,128)(2,1)S(1)} %fusion.1), channel_id=1, source_target_pairs={{0,64},{2,66},{4,68},{6,70},{8,24},{10,26},{12,28},{14,30},{16,80}... | collective-permute-start | bytes 417800 | tf_op jit(solution)/shard_map/ppermute | solution.py:479
  84.8 1.4 %collective-permute-start.18 = (bf16[272,256]{1,0:T(8,128)(2,1)S(1)}, bf16[272,256]{1,0:T(8,128)(2,1)S(1)}, u32[]{:S(2)}, u32[]{:S(2)}) collective-permute-start(bf16[272,256]{1,0:T(8,128)(2,1)S(1)} %add_convert_fusion.mine), channel_id=1, source_target_pairs={{0,8},{8,0},{16,24},{24,16},{32,40},{40,32},{48,56},{56,48},{64,72... | collective-permute-start | bytes 417800 | tf_op jit(solution)/shard_map/ppermute | solution.py:482
